TPU v7x, 32 devices: a whole 2x2x4 slice. The times are simulated.
32 devices in a mesh: groups: 2 (over x), tensor: 16 (over z, y, core).
Axes of the slice: x: 2, y: 2, z: 4, core: 2. Of those that a mesh axis runs over, the one named last changes fastest.
Arguments:
- tokens: bfloat16 [64, 8192], P(('groups', 'tensor')), parts along dimension 0, may hold values from -6 to 6
- gate_weight: bfloat16 [8192, 28672], P(None, 'tensor'), may hold values from -0.0625 to 0.0625
- up_weight: bfloat16 [8192, 28672], P(None, 'tensor'), may hold values from -0.0625 to 0.0625
- down_weight: bfloat16 [28672, 8192], P('tensor'), may hold values from -0.03125 to 0.03125
Outputs:
- mixed: bfloat16 [64, 8192], P(('groups', 'tensor')), parts along dimension 0
There are 2 independent parts, one for each index of `groups`. A program takes and returns all parts, laid end to end along the dimension named above; an argument that names none is the same for every part. Nothing has to cross between parts.
All inputs are finite; a program needn't handle non-finite values.
Results may differ from a plain program's by a relative error of at most 0.015.
Values may be sent and summed in bfloat16 or wider, within the bound.
No kernel may reach another device: no remote copies, remote signals or barrier semaphores. Data moves between devices by JAX's collectives and lax.ppermute only.
A program may use at most 128 MiB of HBM per device.

v0:
```python
import jax
import jax.numpy as jnp
import numpy as np
from jax import lax
from jax.sharding import PartitionSpec as P

BLOCK = 32


def swapped(value, axis, stride):
    mask = 2**stride
    pairs = [(source, source ^ mask) for source in range(lax.axis_size(axis))]
    return lax.ppermute(value, axis, pairs)


def walsh(order):
    index = np.arange(order)
    common = index[:, None] & index[None, :]
    parity = common * 0
    for shift in range(max(order.bit_length(), 1)):
        parity = parity ^ common >> shift & 1
    return (1 - 2 * parity).astype(np.float32)


def per_device(tokens, gate_weight, up_weight, down_weight):
    devices = lax.axis_size("tensor")
    width = gate_weight.shape[1]
    scale = 1.0 / np.sqrt(devices * BLOCK)
    inner = jnp.asarray(walsh(BLOCK), jnp.float32)
    piece = lax.all_gather(tokens, "tensor", axis=0, tiled=True)
    gate = jnp.dot(piece, gate_weight, preferred_element_type=jnp.float32)
    up = jnp.dot(piece, up_weight, preferred_element_type=jnp.float32)
    hidden = jax.nn.silu(gate) * up
    total = hidden.shape[0]
    local = jnp.einsum(
        "tbr,rs->tbs",
        hidden.reshape(total, width // BLOCK, BLOCK),
        inner,
        precision=lax.Precision.HIGHEST,
    ).reshape(total, width)
    index = lax.axis_index("tensor")
    for level in range(devices.bit_length() - 1):
        partner = swapped(local.astype(jnp.bfloat16), "tensor", level).astype(local.dtype)
        upper = index // (1 << level) % 2
        local = jnp.where(upper == 1, partner - local, local + partner)
    rotated = (local * scale).astype(jnp.bfloat16)
    terms = jnp.dot(rotated, down_weight, preferred_element_type=jnp.float32)
    mixed = lax.psum_scatter(terms, "tensor", scatter_dimension=0, tiled=True)
    return mixed.astype(jnp.bfloat16)


def solution(mesh):
    return jax.shard_map(
        per_device,
        mesh=mesh,
        in_specs=(
            P(("groups", "tensor"), None),
            P(None, "tensor"),
            P(None, "tensor"),
            P("tensor", None),
        ),
        out_specs=P(("groups", "tensor"), None),
        check_vma=False,
    )
```

profile of v0, /device:TPU:0, one launch (start us, length us, event | category | flops | bytes accessed | tf_op | source)
XLA Modules:
  0.0 150.9 jit_solution(9514124808251258983)
XLA Ops:
  0.0 24.8 %all-gather = bf16[16,2,8192]{2,1,0:T(2,128)(2,1)S(1)} all-gather(bf16[1,2,8192]{2,1,0:T(2,128)(2,1)} %bitcast.10), channel_id=1, replica_groups=mesh['groups'=2,'tensor'=16] {'tensor'}, dimensions={0}, use_global_device_ids=true | all-gather | bytes 557056 | tf_op jit(solution)/shard_map/all_gather | solution.py:30
  24.8 0.2 reshape.9
  25.0 0.0 copy-start
  25.0 11.9 %fusion.16 = f32[32,1792]{1,0:T(8,128)S(1)} fusion(bf16[32,8192]{1,0:T(8,128)(2,1)S(1)} %reshape.9, bf16[8192,1792]{1,0:T(8,128)(2,1)} %param.6), kind=kOutput, calls=%fused_computation.24 | convolution fusion | flops 939524096 | bytes 30113792 | tf_op jit(solution)/shard_map/dot_general | solution.py:31
  36.9 0.0 copy-start.1
  36.9 12.0 %convolution_multiply_fusion = f32[32,1792]{1,0:T(8,128)S(1)} fusion(bf16[32,8192]{1,0:T(8,128)(2,1)S(1)} %reshape.9, bf16[8192,1792]{1,0:T(8,128)(2,1)} %param.7, f32[32,1792]{1,0:T(8,128)S(1)} %fusion.16), kind=kOutput, calls=%fused_computation | convolution fusion | flops 939810816 | bytes 30343168 | tf_op jit(solution)/shard_map/dot_general | solution.py:32
  48.9 0.3 reshape.6
  49.2 0.0 copy-done
  49.2 0.9 fusion.17
  50.1 0.3 reshape.7
  50.4 0.4 collective-permute-start
  50.8 1.0 collective-permute-done
  51.8 0.1 collective-permute-start.1
  51.9 5.4 %collective-permute-done.1 = bf16[32,1792]{1,0:T(8,128)(2,1)S(1)} collective-permute-done((bf16[32,1792]{1,0:T(8,128)(2,1)S(1)}, bf16[32,1792]{1,0:T(8,128)(2,1)S(1)}, u32[]{:S(2)}, u32[]{:S(2)}) %collective-permute-start.1) | collective-permute-done | bytes 114720 | tf_op jit(solution)/shard_map/ppermute | solution.py:13
  57.3 0.1 fusion.14
  57.3 0.1 collective-permute-start.2
  57.5 4.7 %collective-permute-done.2 = bf16[32,1792]{1,0:T(8,128)(2,1)S(1)} collective-permute-done((bf16[32,1792]{1,0:T(8,128)(2,1)S(1)}, bf16[32,1792]{1,0:T(8,128)(2,1)S(1)}, u32[]{:S(2)}, u32[]{:S(2)}) %collective-permute-start.2) | collective-permute-done | bytes 114720 | tf_op jit(solution)/shard_map/ppermute | solution.py:13
  62.2 0.1 collective-permute-start.3
  62.4 0.0 copy-done.1
  62.4 0.6 dynamic-slice
  63.6 5.5 %collective-permute-done.3 = bf16[32,1792]{1,0:T(8,128)(2,1)S(1)} collective-permute-done((bf16[32,1792]{1,0:T(8,128)(2,1)S(1)}, bf16[32,1792]{1,0:T(8,128)(2,1)S(1)}, u32[]{:S(2)}, u32[]{:S(2)}) %collective-permute-start.3) | collective-permute-done | bytes 114720 | tf_op jit(solution)/shard_map/ppermute | solution.py:13
  69.1 11.9 %fusion.8 = f32[32,8192]{1,0:T(8,128)S(1)} fusion(bf16[1792,8192]{1,0:T(8,128)(2,1)} %param.8, bf16[32,1792]{1,0:T(8,128)(2,1)S(1)} %collective-permute-done.3, f32[32,1792]{1,0:T(8,128)S(1)} %get-tuple-element.6, bf16[32,1792]{1,0:T(8,128)(2,1)S(1)} %collective-permute-done.2, pred[]{:T(512)S(6)} %eq.18, pred[]{:T(512)S(6)} %eq.17), kind=kOutput, calls=%fused_computation.17 | convolution fusion | flops 940097536 | bytes 30867458 | tf_op jit(solution)/shard_map/dot_general | solution.py:47
  81.0 69.2 %all-reduce.2 = bf16[32,8192]{1,0:T(8,128)(2,1)S(1)} all-reduce(f32[32,8192]{1,0:T(8,128)S(1)} %fusion.8), channel_id=2, replica_groups=mesh['groups'=2,'tensor'=16] {'tensor'}, use_global_device_ids=true, to_apply=%region_0.1.clone | all-reduce | flops 262144 | bytes 1572864
  150.2 0.7 dynamic-slice_convert_fusion
  (3 shorter events, 0.1 us)
Async XLA Ops:
  25.0 24.2 %copy-start = (f32[32,32,1]{0,1,2:T(8,128)S(1)}, f32[32,32,1]{0,1,2:T(8,128)}, u32[]{:S(2)}) copy-start(f32[32,32,1]{0,1,2:T(8,128)} %constant.82) | copy-start | bytes 12292
  36.9 25.5 %copy-start.1 = (u32[32]{0:T(128)S(1)}, u32[32]{0:T(128)}, u32[]{:S(2)}) copy-start(u32[32]{0:T(128)} %constant.80) | copy-start | bytes 388
  50.4 1.4 collective-permute-start
  51.8 5.5 %collective-permute-start.1 = (bf16[32,1792]{1,0:T(8,128)(2,1)S(1)}, bf16[32,1792]{1,0:T(8,128)(2,1)S(1)}, u32[]{:S(2)}, u32[]{:S(2)}) collective-permute-start(bf16[32,1792]{1,0:T(8,128)(2,1)S(1)} %fusion.7), channel_id=1, source_target_pairs={{0,2},{1,3},{2,0},{3,1},{4,6},{5,7},{6,4},{7,5},{8,10},{9,11},{10,... | collective-permute-start | bytes 344072 | tf_op jit(solution)/shard_map/ppermute | solution.py:13
  57.3 4.9 %collective-permute-start.2 = (bf16[32,1792]{1,0:T(8,128)(2,1)S(1)}, bf16[32,1792]{1,0:T(8,128)(2,1)S(1)}, u32[]{:S(2)}, u32[]{:S(2)}) collective-permute-start(bf16[32,1792]{1,0:T(8,128)(2,1)S(1)} %get-tuple-element.5), channel_id=1, source_target_pairs={{0,4},{1,5},{2,6},{3,7},{4,0},{5,1},{6,2},{7,3},{8,12},{9,13},{10,... | collective-permute-start | bytes 344072 | tf_op jit(solution)/shard_map/ppermute | solution.py:13
  62.2 6.9 %collective-permute-start.3 = (bf16[32,1792]{1,0:T(8,128)(2,1)S(1)}, bf16[32,1792]{1,0:T(8,128)(2,1)S(1)}, u32[]{:S(2)}, u32[]{:S(2)}) collective-permute-start(bf16[32,1792]{1,0:T(8,128)(2,1)S(1)} %fusion.6), channel_id=1, source_target_pairs={{0,8},{1,9},{2,10},{3,11},{4,12},{5,13},{6,14},{7,15},{8,0},{9,1},... | collective-permute-start | bytes 344072 | tf_op jit(solution)/shard_map/ppermute | solution.py:13
where the time goes:
time: 151 us
  blocking collectives  93.9 us (62%)
  matrix products  36.7 us (24%)
  waiting for transfers between devices  16.6 us (11%)
  local copies, waits for them, and re-layouts  2 us (1%)
    unnamed x1, blocking collectives  69.2 us
    all_gather x1, blocking collectives, per_device(): piece = lax.all_gather(tokens, 'tensor', axis=0, tiled=True)  24.8 us
    ppermute x4, waiting for transfers between devices, swapped(): return lax.ppermute(value, axis, pairs)  16.6 us
    dot_general x1, matrix products, per_device(): up = jnp.dot(piece, up_weight, preferred_element_type=jnp.float32)  12 us
    dot_general x1, matrix products, per_device(): terms = jnp.dot(rotated, down_weight, preferred_element_type=jnp.float32)  11.9 us
    dot_general x1, matrix products, per_device(): gate = jnp.dot(piece, gate_weight, preferred_element_type=jnp.float32)  11.9 us
  transfers between devices with their start and end apart: 4, of which 4 were waited for; matrix products, arithmetic and copies ran while one was open for 0% of the time, Pallas kernels for 0%

commit v1 on v0

--- a/solution.py
+++ b/solution.py
@@ -24,10 +24,22 @@
 
 def per_device(tokens, gate_weight, up_weight, down_weight):
     devices = lax.axis_size("tensor")
+    levels = devices.bit_length() - 1
     width = gate_weight.shape[1]
+    own = tokens.shape[0]
     scale = 1.0 / np.sqrt(devices * BLOCK)
     inner = jnp.asarray(walsh(BLOCK), jnp.float32)
-    piece = lax.all_gather(tokens, "tensor", axis=0, tiled=True)
+    index = lax.axis_index("tensor")
+    upper = [(index >> level) & 1 for level in range(levels)]
+
+    order = list(range(levels))[::-1]
+    piece = tokens
+    for level in order:
+        other = swapped(piece, "tensor", level)
+        low = jnp.where(upper[level] == 1, other, piece)
+        high = jnp.where(upper[level] == 1, piece, other)
+        piece = jnp.concatenate([low, high], axis=0)
+
     gate = jnp.dot(piece, gate_weight, preferred_element_type=jnp.float32)
     up = jnp.dot(piece, up_weight, preferred_element_type=jnp.float32)
     hidden = jax.nn.silu(gate) * up
@@ -38,15 +50,20 @@
         inner,
         precision=lax.Precision.HIGHEST,
     ).reshape(total, width)
-    index = lax.axis_index("tensor")
-    for level in range(devices.bit_length() - 1):
+    for level in range(levels):
         partner = swapped(local.astype(jnp.bfloat16), "tensor", level).astype(local.dtype)
-        upper = index // (1 << level) % 2
-        local = jnp.where(upper == 1, partner - local, local + partner)
+        local = jnp.where(upper[level] == 1, partner - local, local + partner)
     rotated = (local * scale).astype(jnp.bfloat16)
     terms = jnp.dot(rotated, down_weight, preferred_element_type=jnp.float32)
-    mixed = lax.psum_scatter(terms, "tensor", scatter_dimension=0, tiled=True)
-    return mixed.astype(jnp.bfloat16)
+
+    for level in order[::-1]:
+        half = terms.shape[0] // 2
+        low, high = terms[:half], terms[half:]
+        keep = jnp.where(upper[level] == 1, high, low)
+        send = jnp.where(upper[level] == 1, low, high)
+        got = swapped(send.astype(jnp.bfloat16), "tensor", level)
+        terms = keep + got.astype(jnp.float32)
+    return terms.astype(jnp.bfloat16)
 
 
 def solution(mesh):

time: 151 us -> 92.4 us (0.61)
  blocking collectives: 93.9 us -> 0 us
  starting transfers between devices: 0.63 us -> 18.5 us
  waiting for transfers between devices: 16.6 us -> 33.9 us
  other arithmetic: 0.15 us -> 2.46 us
    unnamed x1 -> x0, blocking collectives: 69.2 us -> none
    all_gather x1 -> x0, blocking collectives: 24.8 us -> none  [per_device(): piece = lax.all_gather(tokens, 'tensor', axis=0, tiled=True)]
    ppermute x4 -> x12, starting transfers between devices: 0.63 us -> 18.5 us  [swapped(): return lax.ppermute(value, axis, pairs)]
    ppermute x4 -> x12, waiting for transfers between devices: 16.6 us -> 33.9 us  [swapped(): return lax.ppermute(value, axis, pairs)]
  transfers between devices with their start and end apart: 4 -> 12, of which waited for: 4 -> 12; matrix products, arithmetic and copies ran while one was open for 0% -> 0% of each run, Pallas kernels for 0% -> 0%
where the time goes in v1:
time: 92.4 us; the launch traced here: 92.3 us
  matrix products  36.7 us (40%)
  waiting for transfers between devices  33.9 us (37%)
  starting transfers between devices  18.5 us (20%)
  other arithmetic  2.46 us (3%)
    ppermute x12, waiting for transfers between devices, swapped(): return lax.ppermute(value, axis, pairs)  33.9 us
    ppermute x12, starting transfers between devices, swapped(): return lax.ppermute(value, axis, pairs)  18.5 us
    dot_general x1, matrix products, per_device(): up = jnp.dot(piece, up_weight, preferred_element_type=jnp.float32)  12 us
    dot_general x1, matrix products, per_device(): terms = jnp.dot(rotated, down_weight, preferred_element_type=jnp.float32)  12 us
    dot_general x1, matrix products, per_device(): gate = jnp.dot(piece, gate_weight, preferred_element_type=jnp.float32)  11.9 us
  transfers between devices with their start and end apart: 12, of which 12 were waited for; matrix products, arithmetic and copies ran while one was open for 0% of the time, Pallas kernels for 0%

profile of v1, /device:TPU:0, one launch (start us, length us, event | category | flops | bytes accessed | tf_op | source)
XLA Modules:
  0.0 92.3 jit_solution(15799504718655435966)
XLA Ops:
  0.0 4.0 %collective-permute-start = (bf16[2,8192]{1,0:T(2,128)(2,1)}, bf16[2,8192]{1,0:T(2,128)(2,1)S(1)}, u32[]{:S(2)}, u32[]{:S(2)}) collective-permute-start(bf16[2,8192]{1,0:T(2,128)(2,1)} %param.5), channel_id=1, source_target_pairs={{0,8},{1,9},{2,10},{3,11},{4,12},{5,13},{6,14},{7,15},{8,0},{9,1},... | collective-permute-start | bytes 98312 | tf_op jit(solution)/shard_map/ppermute | solution.py:13
  4.0 2.5 %collective-permute-done = bf16[2,8192]{1,0:T(2,128)(2,1)S(1)} collective-permute-done((bf16[2,8192]{1,0:T(2,128)(2,1)}, bf16[2,8192]{1,0:T(2,128)(2,1)S(1)}, u32[]{:S(2)}, u32[]{:S(2)}) %collective-permute-start) | collective-permute-done | bytes 32800 | tf_op jit(solution)/shard_map/ppermute | solution.py:13
  6.5 0.8 broadcast_select_fusion.7
  7.3 0.1 pad_maximum_fusion.5
  7.4 1.6 %collective-permute-start.1 = (bf16[4,8192]{1,0:T(4,128)(2,1)S(1)}, bf16[4,8192]{1,0:T(4,128)(2,1)S(1)}, u32[]{:S(2)}, u32[]{:S(2)}) collective-permute-start(bf16[4,8192]{1,0:T(4,128)(2,1)S(1)} %pad_maximum_fusion.5), channel_id=1, source_target_pairs={{0,4},{1,5},{2,6},{3,7},{4,0},{5,1},{6,2},{7,3},{8,12},{9,13},{10,... | collective-permute-start | bytes 196616 | tf_op jit(solution)/shard_map/ppermute | solution.py:13
  9.0 2.7 %collective-permute-done.1 = bf16[4,8192]{1,0:T(4,128)(2,1)S(1)} collective-permute-done((bf16[4,8192]{1,0:T(4,128)(2,1)S(1)}, bf16[4,8192]{1,0:T(4,128)(2,1)S(1)}, u32[]{:S(2)}, u32[]{:S(2)}) %collective-permute-start.1) | collective-permute-done | bytes 65568 | tf_op jit(solution)/shard_map/ppermute | solution.py:13
  11.7 0.1 broadcast_select_fusion.5
  11.8 0.1 pad_maximum_fusion.4
  11.9 1.8 %collective-permute-start.2 = (bf16[8,8192]{1,0:T(8,128)(2,1)S(1)}, bf16[8,8192]{1,0:T(8,128)(2,1)S(1)}, u32[]{:S(2)}, u32[]{:S(2)}) collective-permute-start(bf16[8,8192]{1,0:T(8,128)(2,1)S(1)} %pad_maximum_fusion.4), channel_id=1, source_target_pairs={{0,2},{1,3},{2,0},{3,1},{4,6},{5,7},{6,4},{7,5},{8,10},{9,11},{10,... | collective-permute-start | bytes 393224 | tf_op jit(solution)/shard_map/ppermute | solution.py:13
  13.7 3.2 %collective-permute-done.2 = bf16[8,8192]{1,0:T(8,128)(2,1)S(1)} collective-permute-done((bf16[8,8192]{1,0:T(8,128)(2,1)S(1)}, bf16[8,8192]{1,0:T(8,128)(2,1)S(1)}, u32[]{:S(2)}, u32[]{:S(2)}) %collective-permute-start.2) | collective-permute-done | bytes 131104 | tf_op jit(solution)/shard_map/ppermute | solution.py:13
  16.9 0.1 broadcast_select_fusion.3
  17.1 0.1 collective-permute-start.3
  17.2 1.5 %collective-permute-done.3 = bf16[16,8192]{1,0:T(8,128)(2,1)S(1)} collective-permute-done((bf16[16,8192]{1,0:T(8,128)(2,1)S(1)}, bf16[16,8192]{1,0:T(8,128)(2,1)S(1)}, u32[]{:S(2)}, u32[]{:S(2)}) %collective-permute-start.3) | collective-permute-done | bytes 262176 | tf_op jit(solution)/shard_map/ppermute | solution.py:13
  18.7 0.1 broadcast_select_fusion.1
  18.8 0.0 copy-start
  18.8 11.9 %fusion.1 = f32[32,1792]{1,0:T(8,128)S(1)} fusion(bf16[8192,1792]{1,0:T(8,128)(2,1)} %param.6, bf16[16,8192]{1,0:T(8,128)(2,1)S(1)} %get-tuple-element.8, bf16[16,8192]{1,0:T(8,128)(2,1)S(1)} %get-tuple-element.7), kind=kOutput, calls=%fused_computation.4 | convolution fusion | flops 940572672 | bytes 30113792 | tf_op jit(solution)/shard_map/dot_general | solution.py:43
  30.7 12.0 %multiply_multiply_fusion = f32[32,1792]{1,0:T(8,128)S(1)} fusion(f32[32,1792]{1,0:T(8,128)S(1)} %fusion.1, bf16[8192,1792]{1,0:T(8,128)(2,1)} %param.7, bf16[16,8192]{1,0:T(8,128)(2,1)S(1)} %get-tuple-element.8, bf16[16,8192]{1,0:T(8,128)(2,1)S(1)} %get-tuple-element.7), kind=kOutput, calls=%fused_computation.24 | convolution fusion | flops 940859392 | bytes 30343168 | tf_op jit(solution)/shard_map/dot_general | solution.py:44
  42.7 0.3 reshape.6
  43.0 0.0 copy-done
  43.0 0.9 fusion.20
  43.9 0.3 reshape.7
  44.2 0.2 collective-permute-start.4
  44.4 1.2 %collective-permute-done.4 = bf16[32,1792]{1,0:T(8,128)(2,1)S(1)} collective-permute-done((bf16[32,1792]{1,0:T(8,128)(2,1)S(1)}, bf16[32,1792]{1,0:T(8,128)(2,1)S(1)}, u32[]{:S(2)}, u32[]{:S(2)}) %collective-permute-start.4) | collective-permute-done | bytes 114720 | tf_op jit(solution)/shard_map/ppermute | solution.py:13
  45.6 1.8 %collective-permute-start.5 = (bf16[32,1792]{1,0:T(8,128)(2,1)S(1)}, bf16[32,1792]{1,0:T(8,128)(2,1)S(1)}, u32[]{:S(2)}, u32[]{:S(2)}) collective-permute-start(bf16[32,1792]{1,0:T(8,128)(2,1)S(1)} %fusion.9), channel_id=1, source_target_pairs={{0,2},{1,3},{2,0},{3,1},{4,6},{5,7},{6,4},{7,5},{8,10},{9,11},{10,... | collective-permute-start | bytes 344072 | tf_op jit(solution)/shard_map/ppermute | solution.py:13
  47.4 3.5 %collective-permute-done.5 = bf16[32,1792]{1,0:T(8,128)(2,1)S(1)} collective-permute-done((bf16[32,1792]{1,0:T(8,128)(2,1)S(1)}, bf16[32,1792]{1,0:T(8,128)(2,1)S(1)}, u32[]{:S(2)}, u32[]{:S(2)}) %collective-permute-start.5) | collective-permute-done | bytes 114720 | tf_op jit(solution)/shard_map/ppermute | solution.py:13
  50.9 0.1 fusion.18
  50.9 1.6 %collective-permute-start.6 = (bf16[32,1792]{1,0:T(8,128)(2,1)S(1)}, bf16[32,1792]{1,0:T(8,128)(2,1)S(1)}, u32[]{:S(2)}, u32[]{:S(2)}) collective-permute-start(bf16[32,1792]{1,0:T(8,128)(2,1)S(1)} %get-tuple-element.5), channel_id=1, source_target_pairs={{0,4},{1,5},{2,6},{3,7},{4,0},{5,1},{6,2},{7,3},{8,12},{9,13},{10,... | collective-permute-start | bytes 344072 | tf_op jit(solution)/shard_map/ppermute | solution.py:13
  52.6 3.2 %collective-permute-done.6 = bf16[32,1792]{1,0:T(8,128)(2,1)S(1)} collective-permute-done((bf16[32,1792]{1,0:T(8,128)(2,1)S(1)}, bf16[32,1792]{1,0:T(8,128)(2,1)S(1)}, u32[]{:S(2)}, u32[]{:S(2)}) %collective-permute-start.6) | collective-permute-done | bytes 114720 | tf_op jit(solution)/shard_map/ppermute | solution.py:13
  55.8 2.7 %collective-permute-start.7 = (bf16[32,1792]{1,0:T(8,128)(2,1)S(1)}, bf16[32,1792]{1,0:T(8,128)(2,1)S(1)}, u32[]{:S(2)}, u32[]{:S(2)}) collective-permute-start(bf16[32,1792]{1,0:T(8,128)(2,1)S(1)} %fusion.8), channel_id=1, source_target_pairs={{0,8},{1,9},{2,10},{3,11},{4,12},{5,13},{6,14},{7,15},{8,0},{9,1},... | collective-permute-start | bytes 344072 | tf_op jit(solution)/shard_map/ppermute | solution.py:13
  58.5 4.3 %collective-permute-done.7 = bf16[32,1792]{1,0:T(8,128)(2,1)S(1)} collective-permute-done((bf16[32,1792]{1,0:T(8,128)(2,1)S(1)}, bf16[32,1792]{1,0:T(8,128)(2,1)S(1)}, u32[]{:S(2)}, u32[]{:S(2)}) %collective-permute-start.7) | collective-permute-done | bytes 114720 | tf_op jit(solution)/shard_map/ppermute | solution.py:13
  62.8 12.0 %fusion.10 = f32[32,8192]{1,0:T(8,128)S(1)} fusion(bf16[1792,8192]{1,0:T(8,128)(2,1)} %param.8, bf16[32,1792]{1,0:T(8,128)(2,1)S(1)} %collective-permute-done.7, f32[32,1792]{1,0:T(8,128)S(1)} %get-tuple-element.6, bf16[32,1792]{1,0:T(8,128)(2,1)S(1)} %collective-permute-done.6, pred[]{:T(512)S(6)} %eq.9, pred[]{:T(512)S(6)} %eq.8), kind=kOutput, calls=%fused_computation.32 | convolution fusion | flops 940097536 | bytes 30867458 | tf_op jit(solution)/shard_map/dot_general | solution.py:57
  74.8 0.1 select_convert_fusion
  74.8 0.1 collective-permute-start.8
  74.9 1.5 %collective-permute-done.8 = bf16[16,8192]{1,0:T(8,128)(2,1)S(1)} collective-permute-done((bf16[16,8192]{1,0:T(8,128)(2,1)S(1)}, bf16[16,8192]{1,0:T(8,128)(2,1)S(1)}, u32[]{:S(2)}, u32[]{:S(2)}) %collective-permute-start.8) | collective-permute-done | bytes 262176 | tf_op jit(solution)/shard_map/ppermute | solution.py:13
  76.5 0.1 convert_add_fusion
  76.6 1.8 %collective-permute-start.9 = (bf16[8,8192]{1,0:T(8,128)(2,1)S(1)}, bf16[8,8192]{1,0:T(8,128)(2,1)S(1)}, u32[]{:S(2)}, u32[]{:S(2)}) collective-permute-start(bf16[8,8192]{1,0:T(8,128)(2,1)S(1)} %select_convert_fusion.1), channel_id=1, source_target_pairs={{0,2},{1,3},{2,0},{3,1},{4,6},{5,7},{6,4},{7,5},{8,10},{9,11},{10,... | collective-permute-start | bytes 393224 | tf_op jit(solution)/shard_map/ppermute | solution.py:13
  78.4 3.8 %collective-permute-done.9 = bf16[8,8192]{1,0:T(8,128)(2,1)S(1)} collective-permute-done((bf16[8,8192]{1,0:T(8,128)(2,1)S(1)}, bf16[8,8192]{1,0:T(8,128)(2,1)S(1)}, u32[]{:S(2)}, u32[]{:S(2)}) %collective-permute-start.9) | collective-permute-done | bytes 131104 | tf_op jit(solution)/shard_map/ppermute | solution.py:13
  82.2 0.1 select_convert_fusion.2
  82.3 0.7 collective-permute-start.10
  83.0 3.6 %collective-permute-done.10 = bf16[4,8192]{1,0:T(4,128)(2,1)S(1)} collective-permute-done((bf16[4,8192]{1,0:T(4,128)(2,1)S(1)}, bf16[4,8192]{1,0:T(4,128)(2,1)S(1)}, u32[]{:S(2)}, u32[]{:S(2)}) %collective-permute-start.10) | collective-permute-done | bytes 65568 | tf_op jit(solution)/shard_map/ppermute | solution.py:13
  86.7 0.1 select_convert_fusion.3
  86.7 2.1 %collective-permute-start.11 = (bf16[2,8192]{1,0:T(2,128)(2,1)S(1)}, bf16[2,8192]{1,0:T(2,128)(2,1)S(1)}, u32[]{:S(2)}, u32[]{:S(2)}) collective-permute-start(bf16[2,8192]{1,0:T(2,128)(2,1)S(1)} %select_convert_fusion.3), channel_id=1, source_target_pairs={{0,8},{1,9},{2,10},{3,11},{4,12},{5,13},{6,14},{7,15},{8,0},{9,1},... | collective-permute-start | bytes 98312 | tf_op jit(solution)/shard_map/ppermute | solution.py:13
  88.8 2.8 %collective-permute-done.11 = bf16[2,8192]{1,0:T(2,128)(2,1)S(1)} collective-permute-done((bf16[2,8192]{1,0:T(2,128)(2,1)S(1)}, bf16[2,8192]{1,0:T(2,128)(2,1)S(1)}, u32[]{:S(2)}, u32[]{:S(2)}) %collective-permute-start.11) | collective-permute-done | bytes 32800 | tf_op jit(solution)/shard_map/ppermute | solution.py:13
  91.6 0.7 add_convert_fusion
  (7 shorter events, 0.2 us)
Async XLA Ops:
  0.0 6.5 %collective-permute-start = (bf16[2,8192]{1,0:T(2,128)(2,1)}, bf16[2,8192]{1,0:T(2,128)(2,1)S(1)}, u32[]{:S(2)}, u32[]{:S(2)}) collective-permute-start(bf16[2,8192]{1,0:T(2,128)(2,1)} %param.5), channel_id=1, source_target_pairs={{0,8},{1,9},{2,10},{3,11},{4,12},{5,13},{6,14},{7,15},{8,0},{9,1},... | collective-permute-start | bytes 98312 | tf_op jit(solution)/shard_map/ppermute | solution.py:13
  7.4 4.3 %collective-permute-start.1 = (bf16[4,8192]{1,0:T(4,128)(2,1)S(1)}, bf16[4,8192]{1,0:T(4,128)(2,1)S(1)}, u32[]{:S(2)}, u32[]{:S(2)}) collective-permute-start(bf16[4,8192]{1,0:T(4,128)(2,1)S(1)} %pad_maximum_fusion.5), channel_id=1, source_target_pairs={{0,4},{1,5},{2,6},{3,7},{4,0},{5,1},{6,2},{7,3},{8,12},{9,13},{10,... | collective-permute-start | bytes 196616 | tf_op jit(solution)/shard_map/ppermute | solution.py:13
  11.9 5.0 %collective-permute-start.2 = (bf16[8,8192]{1,0:T(8,128)(2,1)S(1)}, bf16[8,8192]{1,0:T(8,128)(2,1)S(1)}, u32[]{:S(2)}, u32[]{:S(2)}) collective-permute-start(bf16[8,8192]{1,0:T(8,128)(2,1)S(1)} %pad_maximum_fusion.4), channel_id=1, source_target_pairs={{0,2},{1,3},{2,0},{3,1},{4,6},{5,7},{6,4},{7,5},{8,10},{9,11},{10,... | collective-permute-start | bytes 393224 | tf_op jit(solution)/shard_map/ppermute | solution.py:13
  17.1 1.6 %collective-permute-start.3 = (bf16[16,8192]{1,0:T(8,128)(2,1)S(1)}, bf16[16,8192]{1,0:T(8,128)(2,1)S(1)}, u32[]{:S(2)}, u32[]{:S(2)}) collective-permute-start(bf16[16,8192]{1,0:T(8,128)(2,1)S(1)} %pad_maximum_fusion.3), channel_id=1, source_target_pairs={{0,1},{1,0},{2,3},{3,2},{4,5},{5,4},{6,7},{7,6},{8,9},{9,8},{10,11... | collective-permute-start | bytes 786440 | tf_op jit(solution)/shard_map/ppermute | solution.py:13
  18.8 24.2 %copy-start = (f32[32,32,1]{0,1,2:T(8,128)S(1)}, f32[32,32,1]{0,1,2:T(8,128)}, u32[]{:S(2)}) copy-start(f32[32,32,1]{0,1,2:T(8,128)} %constant.21) | copy-start | bytes 12292
  44.2 1.4 %collective-permute-start.4 = (bf16[32,1792]{1,0:T(8,128)(2,1)S(1)}, bf16[32,1792]{1,0:T(8,128)(2,1)S(1)}, u32[]{:S(2)}, u32[]{:S(2)}) collective-permute-start(bf16[32,1792]{1,0:T(8,128)(2,1)S(1)} %convert_element_type.54), channel_id=1, source_target_pairs={{0,1},{1,0},{2,3},{3,2},{4,5},{5,4},{6,7},{7,6},{8,9},{9,8},{10,11... | collective-permute-start | bytes 344072 | tf_op jit(solution)/shard_map/ppermute | solution.py:13
  45.6 5.3 %collective-permute-start.5 = (bf16[32,1792]{1,0:T(8,128)(2,1)S(1)}, bf16[32,1792]{1,0:T(8,128)(2,1)S(1)}, u32[]{:S(2)}, u32[]{:S(2)}) collective-permute-start(bf16[32,1792]{1,0:T(8,128)(2,1)S(1)} %fusion.9), channel_id=1, source_target_pairs={{0,2},{1,3},{2,0},{3,1},{4,6},{5,7},{6,4},{7,5},{8,10},{9,11},{10,... | collective-permute-start | bytes 344072 | tf_op jit(solution)/shard_map/ppermute | solution.py:13
  50.9 4.9 %collective-permute-start.6 = (bf16[32,1792]{1,0:T(8,128)(2,1)S(1)}, bf16[32,1792]{1,0:T(8,128)(2,1)S(1)}, u32[]{:S(2)}, u32[]{:S(2)}) collective-permute-start(bf16[32,1792]{1,0:T(8,128)(2,1)S(1)} %get-tuple-element.5), channel_id=1, source_target_pairs={{0,4},{1,5},{2,6},{3,7},{4,0},{5,1},{6,2},{7,3},{8,12},{9,13},{10,... | collective-permute-start | bytes 344072 | tf_op jit(solution)/shard_map/ppermute | solution.py:13
  55.8 7.0 %collective-permute-start.7 = (bf16[32,1792]{1,0:T(8,128)(2,1)S(1)}, bf16[32,1792]{1,0:T(8,128)(2,1)S(1)}, u32[]{:S(2)}, u32[]{:S(2)}) collective-permute-start(bf16[32,1792]{1,0:T(8,128)(2,1)S(1)} %fusion.8), channel_id=1, source_target_pairs={{0,8},{1,9},{2,10},{3,11},{4,12},{5,13},{6,14},{7,15},{8,0},{9,1},... | collective-permute-start | bytes 344072 | tf_op jit(solution)/shard_map/ppermute | solution.py:13
  74.8 1.6 %collective-permute-start.8 = (bf16[16,8192]{1,0:T(8,128)(2,1)S(1)}, bf16[16,8192]{1,0:T(8,128)(2,1)S(1)}, u32[]{:S(2)}, u32[]{:S(2)}) collective-permute-start(bf16[16,8192]{1,0:T(8,128)(2,1)S(1)} %select_convert_fusion), channel_id=1, source_target_pairs={{0,1},{1,0},{2,3},{3,2},{4,5},{5,4},{6,7},{7,6},{8,9},{9,8},{10,11... | collective-permute-start | bytes 786440 | tf_op jit(solution)/shard_map/ppermute | solution.py:13
  76.6 5.6 %collective-permute-start.9 = (bf16[8,8192]{1,0:T(8,128)(2,1)S(1)}, bf16[8,8192]{1,0:T(8,128)(2,1)S(1)}, u32[]{:S(2)}, u32[]{:S(2)}) collective-permute-start(bf16[8,8192]{1,0:T(8,128)(2,1)S(1)} %select_convert_fusion.1), channel_id=1, source_target_pairs={{0,2},{1,3},{2,0},{3,1},{4,6},{5,7},{6,4},{7,5},{8,10},{9,11},{10,... | collective-permute-start | bytes 393224 | tf_op jit(solution)/shard_map/ppermute | solution.py:13
  82.3 4.3 %collective-permute-start.10 = (bf16[4,8192]{1,0:T(4,128)(2,1)S(1)}, bf16[4,8192]{1,0:T(4,128)(2,1)S(1)}, u32[]{:S(2)}, u32[]{:S(2)}) collective-permute-start(bf16[4,8192]{1,0:T(4,128)(2,1)S(1)} %select_convert_fusion.2), channel_id=1, source_target_pairs={{0,4},{1,5},{2,6},{3,7},{4,0},{5,1},{6,2},{7,3},{8,12},{9,13},{10,... | collective-permute-start | bytes 196616 | tf_op jit(solution)/shard_map/ppermute | solution.py:13
  86.7 4.9 %collective-permute-start.11 = (bf16[2,8192]{1,0:T(2,128)(2,1)S(1)}, bf16[2,8192]{1,0:T(2,128)(2,1)S(1)}, u32[]{:S(2)}, u32[]{:S(2)}) collective-permute-start(bf16[2,8192]{1,0:T(2,128)(2,1)S(1)} %select_convert_fusion.3), channel_id=1, source_target_pairs={{0,8},{1,9},{2,10},{3,11},{4,12},{5,13},{6,14},{7,15},{8,0},{9,1},... | collective-permute-start | bytes 98312 | tf_op jit(solution)/shard_map/ppermute | solution.py:13

commit v2 on v0

v2 whole, which is shorter than its diff:
```python
import functools
import itertools

import jax
import jax.numpy as jnp
import numpy as np
from jax import lax
from jax.experimental import pallas as pl
from jax.experimental.pallas import tpu as pltpu
from jax.sharding import PartitionSpec as P

BLOCK = 32
MIB = 2**20
VMEM = pl.BlockSpec(memory_space=pltpu.VMEM)
ANY = pl.BlockSpec(memory_space=pl.ANY)
GATHER_BYTES = (4 * MIB, 8 * MIB, 8 * MIB, 2 * MIB)
HADAMARD_BYTES = (0, 5 * MIB, 5 * MIB, 5 * MIB)


def walsh(order):
    index = np.arange(order)
    common = index[:, None] & index[None, :]
    parity = common * 0
    for shift in range(max(order.bit_length(), 1)):
        parity = parity ^ common >> shift & 1
    return (1 - 2 * parity).astype(np.float32)


def swapped(value, mask):
    pairs = [(source, source ^ mask) for source in range(lax.axis_size("tensor"))]
    return lax.ppermute(value, "tensor", pairs)


def in_hbm(value):
    return pltpu.with_memory_space_constraint(value, pltpu.HBM)


def in_vmem(value):
    return pltpu.with_memory_space_constraint(value, pltpu.VMEM)


def divisor(size, most, step):
    return max(d for d in range(step, min(size, most) + 1, step) if size % d == 0)


def fetch(weight, first, rows, after):
    def kernel(weight_ref, *refs):
        out_ref, sem = refs[-2:]
        copy = pltpu.make_async_copy(weight_ref.at[pl.ds(first, rows)], out_ref, sem)
        copy.start()
        copy.wait()

    width = weight.shape[1]
    size = rows * width * weight.dtype.itemsize
    return pl.pallas_call(
        kernel,
        out_shape=jax.ShapeDtypeStruct((rows, width), weight.dtype),
        in_specs=[ANY] * (1 + len(after)),
        out_specs=VMEM,
        scratch_shapes=[pltpu.SemaphoreType.DMA],
        cost_estimate=pl.CostEstimate(flops=0, transcendentals=0, bytes_accessed=2 * size),
        compiler_params=pltpu.CompilerParams(vmem_limit_bytes=MIB),
    )(in_hbm(weight), *after)


class Fetched:
    def __init__(self, weight, chunk, most):
        self.weight, self.chunk, self.most = weight, chunk, most
        self.rows, self.pieces = 0, []

    def beside(self, value, size, after):
        row = self.weight.shape[1] * self.weight.dtype.itemsize * self.chunk
        rows = min(size // row * self.chunk, self.most - self.rows)
        if rows <= 0:
            return value
        piece = fetch(self.weight, self.rows, rows, after)
        value, piece = lax.optimization_barrier((value, piece))
        self.rows += rows
        self.pieces.append(piece)
        return value


def gate_up(x, gate, up, fetched, chunk):
    tokens, depth = x.shape
    width = gate.shape[1]
    tile = divisor(width, 256, BLOCK)
    pieces = fetched.pieces
    count = len(pieces)
    chunks = [(0, first) for first in range(fetched.rows, depth, chunk)]
    chunks += [(1, first) for first in range(0, depth, chunk)]
    slots = min(8, len(chunks))
    spread = np.kron(np.eye(tile // BLOCK, dtype=np.float32), walsh(BLOCK))

    def kernel(x_ref, spread_ref, gate_ref, up_ref, *refs):
        piece_refs = refs[:count]
        out_ref, gate_acc, up_acc, buffer, sems = refs[count:]

        def copy(i):
            which, first = chunks[i]
            return pltpu.make_async_copy(
                (gate_ref, up_ref)[which].at[pl.ds(first, chunk)],
                buffer.at[i % slots],
                sems.at[i % slots],
            )

        for i in range(slots):
            copy(i).start()
        gate_acc[...] = jnp.zeros_like(gate_acc)
        up_acc[...] = jnp.zeros_like(up_acc)

        def add(acc, first, rows, ref):
            for n in range(0, width, tile):
                acc[:, n : n + tile] += jnp.dot(
                    x_ref[:, first : first + rows],
                    ref[:, n : n + tile],
                    preferred_element_type=jnp.float32,
                )

        first = 0
        for ref in piece_refs:
            add(gate_acc, first, ref.shape[0], ref)
            first += ref.shape[0]
        for i, (which, first) in enumerate(chunks):
            copy(i).wait()
            add((gate_acc, up_acc)[which], first, chunk, buffer.at[i % slots])
            if i + slots < len(chunks):
                copy(i + slots).start()
        for n in range(0, width, tile):
            hidden = jax.nn.silu(gate_acc[:, n : n + tile]) * up_acc[:, n : n + tile]
            coarse = hidden.astype(jnp.bfloat16)
            fine = (hidden - coarse.astype(jnp.float32)).astype(jnp.bfloat16)
            turned = jnp.dot(coarse, spread_ref[...], preferred_element_type=jnp.float32)
            turned += jnp.dot(fine, spread_ref[...], preferred_element_type=jnp.float32)
            out_ref[:, n : n + tile] = turned.astype(out_ref.dtype)

    size = gate.dtype.itemsize * width
    return pl.pallas_call(
        kernel,
        out_shape=jax.ShapeDtypeStruct((tokens, width), jnp.bfloat16),
        in_specs=[VMEM, VMEM, ANY, ANY] + [VMEM] * count,
        out_specs=VMEM,
        scratch_shapes=[
            pltpu.VMEM((tokens, width), jnp.float32),
            pltpu.VMEM((tokens, width), jnp.float32),
            pltpu.VMEM((slots, chunk, width), gate.dtype),
            pltpu.SemaphoreType.DMA((slots,)),
        ],
        cost_estimate=pl.CostEstimate(
            flops=4 * tokens * depth * width,
            transcendentals=tokens * width,
            bytes_accessed=len(chunks) * chunk * size,
        ),
        compiler_params=pltpu.CompilerParams(
            vmem_limit_bytes=slots * chunk * size + 3 * tokens * width * 4 + 4 * MIB
        ),
    )(
        x,
        jnp.asarray(spread, jnp.bfloat16),
        in_hbm(gate),
        in_hbm(up),
        *[in_vmem(piece) for piece in pieces],
    )


def down(rotated, weight, fetched, chunk):
    tokens, depth = rotated.shape
    width = weight.shape[1]
    tile = divisor(width, 256, 128)
    half = tokens // 2
    pieces = fetched.pieces
    count = len(pieces)
    chunks = list(range(fetched.rows, depth, chunk))

    def kernel(rotated_ref, weight_ref, *refs):
        piece_refs = refs[:count]
        keep_ref, send_ref, acc, buffer, sems = refs[count:]
        copies = [
            pltpu.make_async_copy(weight_ref.at[pl.ds(first, chunk)], buffer.at[i], sems.at[i])
            for i, first in enumerate(chunks)
        ]
        for copy in copies:
            copy.start()
        mine = lax.axis_index("tensor") % 2
        upper = mine == 1

        first = 0
        todo = []
        for ref in piece_refs:
            todo.append((first, ref.shape[0], ref, None))
            first += ref.shape[0]
        for i, first in enumerate(chunks):
            todo.append((first, chunk, buffer.at[i], copies[i]))
        for step, (first, rows, ref, copy) in enumerate(todo):
            if copy is not None:
                copy.wait()
            for n in range(0, width, tile):
                at = slice(n, n + tile)
                part = jnp.dot(
                    rotated_ref[:, first : first + rows],
                    ref[:, at],
                    preferred_element_type=jnp.float32,
                )
                if step:
                    part += acc[:, at]
                if step < len(todo) - 1:
                    acc[:, at] = part
                else:
                    low, high = part[:half], part[half:]
                    keep_ref[:, at] = jnp.where(upper, high, low)
                    send_ref[:, at] = jnp.where(upper, low, high).astype(send_ref.dtype)

    size = weight.dtype.itemsize * width
    return pl.pallas_call(
        kernel,
        out_shape=(
            jax.ShapeDtypeStruct((half, width), jnp.float32),
            jax.ShapeDtypeStruct((half, width), jnp.bfloat16),
        ),
        in_specs=[VMEM, ANY] + [VMEM] * count,
        out_specs=(VMEM, VMEM),
        scratch_shapes=[
            pltpu.VMEM((tokens, width), jnp.float32),
            pltpu.VMEM((len(chunks), chunk, width), weight.dtype),
            pltpu.SemaphoreType.DMA((len(chunks),)),
        ],
        cost_estimate=pl.CostEstimate(
            flops=2 * tokens * depth * width,
            transcendentals=0,
            bytes_accessed=len(chunks) * chunk * size,
        ),
        compiler_params=pltpu.CompilerParams(
            vmem_limit_bytes=len(chunks) * chunk * size + 2 * tokens * width * 4 + 4 * MIB
        ),
    )(rotated, in_hbm(weight), *[in_vmem(piece) for piece in pieces])


def masks_of(levels):
    return [
        (flips, sum(flip << level for flip, level in zip(flips, levels)))
        for flips in itertools.product((0, 1), repeat=len(levels))
    ]


def pick(choices, bits):
    if not bits:
        return choices[()]
    one, zero = (
        pick({k[1:]: v for k, v in choices.items() if k[0] == b}, bits[1:]) for b in (1, 0)
    )
    return jnp.where(bits[0], one, zero)


def xor(a, b):
    return tuple(i ^ j for i, j in zip(a, b))


def rounds_of(levels):
    return [(level,) for level in range(levels)[::-1]]


def per_device(tokens, gate_weight, up_weight, down_weight):
    devices = lax.axis_size("tensor")
    levels = devices.bit_length() - 1
    depth, width = gate_weight.shape
    scale = np.float32(1.0 / np.sqrt(devices * BLOCK))
    index = lax.axis_index("tensor")
    rounds = rounds_of(levels)
    upper = [(index >> level) & 1 == 1 for level in range(levels)]
    odd = {}
    for combined in rounds:
        for flips, mask in masks_of(combined[::-1]):
            odd[combined, flips] = functools.reduce(
                jnp.logical_xor,
                [upper[level] for flip, level in zip(flips, combined[::-1]) if not flip],
                jnp.zeros_like(upper[0]),
            )
    tokens, upper, odd = lax.optimization_barrier((tokens, upper, odd))

    gate_chunk = divisor(depth, 512, 16)
    gate_rows = Fetched(gate_weight, gate_chunk, depth - 2 * gate_chunk)
    piece = tokens
    for number, combined in enumerate(rounds):
        combined = combined[::-1]
        got = {(0,) * len(combined): piece}
        for flips, mask in masks_of(combined)[1:]:
            got[flips] = swapped(piece, mask)
        size = GATHER_BYTES[number] if number < len(GATHER_BYTES) else 0
        got[(0,) * len(combined)] = gate_rows.beside(piece, size, [piece] if number else [])
        bits = [upper[level] for level in combined]
        rows = []
        for slot in itertools.product((0, 1), repeat=len(combined)):
            rows.append(pick({xor(slot, flips): v for flips, v in got.items()}, bits))
        piece = jnp.concatenate(rows, axis=0)

    local = gate_up(piece, gate_weight, up_weight, gate_rows, gate_chunk)

    down_chunk = divisor(width, 256, 16)
    down_rows = Fetched(down_weight, down_chunk, width - down_chunk)
    for number, combined in enumerate(rounds[::-1]):
        levels_of = combined[::-1]
        last = number == len(rounds) - 1
        got = {}
        for flips, mask in masks_of(levels_of)[1:]:
            got[flips] = swapped(local, mask)
        size = HADAMARD_BYTES[number] if number < len(HADAMARD_BYTES) else 0
        got[(0,) * len(combined)] = down_rows.beside(local, size, [local])
        turned = 0.0
        for flips, value in got.items():
            value = value.astype(jnp.float32)
            if not all(flips):
                value = jnp.where(odd[combined, flips], -value, value)
            turned += value
        if last:
            turned *= scale
        local = turned.astype(jnp.bfloat16)

    keep, send = down(local, down_weight, down_rows, down_chunk)
    terms = keep + swapped(send, 1).astype(jnp.float32)
    for combined in rounds[::-1][1:]:
        combined = combined[::-1]
        parts = terms.reshape((2,) * len(combined) + (-1, terms.shape[1]))
        bits = [upper[level] for level in combined]
        total = None
        for flips, mask in masks_of(combined):
            slots = {
                xor(slot, flips): parts[slot]
                for slot in itertools.product((0, 1), repeat=len(combined))
            }
            part = pick(slots, bits)
            if mask:
                part = swapped(part.astype(jnp.bfloat16), mask).astype(jnp.float32)
            total = part if total is None else total + part
        terms = total
    return terms.astype(jnp.bfloat16)


def solution(mesh):
    return jax.shard_map(
        per_device,
        mesh=mesh,
        in_specs=(
            P(("groups", "tensor"), None),
            P(None, "tensor"),
            P(None, "tensor"),
            P("tensor", None),
        ),
        out_specs=P(("groups", "tensor"), None),
        check_vma=False,
    )
```

time: 151 us -> 77.7 us (0.51)
  blocking collectives: 93.9 us -> 0 us
  Pallas kernels: 0 us -> 38.8 us
  matrix products: 36.7 us -> 0 us
  starting transfers between devices: 0.63 us -> 17.7 us
  waiting for transfers between devices: 16.6 us -> 19.1 us
  local copies, waits for them, and re-layouts: 2 us -> 0.01 us
    unnamed x1 -> x0, blocking collectives: 69.2 us -> none
    pallas_call x0 -> x9, Pallas kernels: none -> 38.8 us  [the longest x7 16.3 us: fetch(): pl.pallas_call(kernel, out_shape=jax.ShapeDtypeStruct((rows, width), weig...]
    dot_general x4 -> x0, matrix products: 36.7 us -> none  [the longest x1 12 us: per_device(): up = jnp.dot(piece, up_weight, preferred_element_type=jnp.float32)]
    all_gather x1 -> x0, blocking collectives: 24.8 us -> none  [per_device(): piece = lax.all_gather(tokens, 'tensor', axis=0, tiled=True)]
    ppermute x4 -> x12, starting transfers between devices: 0.63 us -> 17.7 us  [swapped(): return lax.ppermute(value, 'tensor', pairs)]
    ppermute x4 -> x12, waiting for transfers between devices: 16.6 us -> 19.1 us  [swapped(): return lax.ppermute(value, 'tensor', pairs)]
  transfers between devices with their start and end apart: 4 -> 12, of which waited for: 4 -> 10; matrix products, arithmetic and copies ran while one was open for 0% -> 0% of each run, Pallas kernels for 0% -> 21%
where the time goes in v2:
time: 77.7 us; the launch traced here: 77.3 us
  Pallas kernels  38.8 us (50%)
  waiting for transfers between devices  19.1 us (25%)
  starting transfers between devices  17.7 us (23%)
  other arithmetic  1.54 us (2%)
    ppermute x12, waiting for transfers between devices, swapped(): return lax.ppermute(value, 'tensor', pairs)  19.1 us
    ppermute x12, starting transfers between devices, swapped(): return lax.ppermute(value, 'tensor', pairs)  17.7 us
    pallas_call x7, Pallas kernels, fetch(): pl.pallas_call(kernel, out_shape=jax.ShapeDtypeStruct((rows, width), weig...  16.3 us
    pallas_call x1, Pallas kernels, gate_up(): pl.pallas_call(kernel, out_shape=jax.ShapeDtypeStruct((tokens, width), jn...  15.5 us
    pallas_call x1, Pallas kernels, down(): pl.pallas_call(kernel, out_shape=(jax.ShapeDtypeStruct((half, width), jnp...  6.89 us
  transfers between devices with their start and end apart: 12, of which 10 were waited for; matrix products, arithmetic and copies ran while one was open for 0% of the time, Pallas kernels for 21%

profile of v2, /device:TPU:0, one launch (start us, length us, event | category | flops | bytes accessed | tf_op | source)
XLA Modules:
  0.0 77.3 jit_solution(9249020238114445747)
XLA Ops:
  0.0 0.0 copy-start.1
  0.0 4.0 %collective-permute-start = (bf16[2,8192]{1,0:T(2,128)(2,1)}, bf16[2,8192]{1,0:T(2,128)(2,1)S(1)}, u32[]{:S(2)}, u32[]{:S(2)}) collective-permute-start(bf16[2,8192]{1,0:T(2,128)(2,1)} %param.5), channel_id=1, source_target_pairs={{0,8},{1,9},{2,10},{3,11},{4,12},{5,13},{6,14},{7,15},{8,0},{9,1},... | collective-permute-start | bytes 98312 | tf_op jit(solution)/shard_map/ppermute | solution.py:31
  4.0 2.0 %shard_map.55.refs_0_ = bf16[1024,1792]{1,0:T(8,128)(2,1)S(1)} custom-call(bf16[8192,1792]{1,0:T(8,128)(2,1)} %gate_ref.1), custom_call_target="tpu_custom_call" | custom-call | bytes 7340032 | tf_op jit(solution)/shard_map/pallas_call | solution.py:55
  6.1 0.5 collective-permute-done
  6.6 0.0 copy-done.1
  6.6 0.1 broadcast_select_fusion.7
  6.6 0.1 pad_maximum_fusion.3.refs_0_
  6.7 1.6 %collective-permute-start.1 = (bf16[4,8192]{1,0:T(4,128)(2,1)S(1)}, bf16[4,8192]{1,0:T(4,128)(2,1)S(1)}, u32[]{:S(2)}, u32[]{:S(2)}) collective-permute-start(bf16[4,8192]{1,0:T(4,128)(2,1)S(1)} %pad_maximum_fusion.3.refs_0_), channel_id=1, source_target_pairs={{0,4},{1,5},{2,6},{3,7},{4,0},{5,1},{6,2},{7,3},{8,12},{9,13},{10,... | collective-permute-start | bytes 196616 | tf_op jit(solution)/shard_map/ppermute | solution.py:31
  8.3 3.1 %shard_map.56.refs_1_ = bf16[2048,1792]{1,0:T(8,128)(2,1)S(1)} custom-call(bf16[8192,1792]{1,0:T(8,128)(2,1)} %gate_ref.1, bf16[4,8192]{1,0:T(4,128)(2,1)S(1)} %pad_maximum_fusion.3.refs_0_), custom_call_target="tpu_custom_call" | custom-call | bytes 14680064 | tf_op jit(solution)/shard_map/pallas_call | solution.py:55
  11.4 0.0 collective-permute-done.1
  11.4 0.1 broadcast_select_fusion.5
  11.4 0.1 pad_maximum_fusion.2.refs_0_
  11.5 1.6 %collective-permute-start.2 = (bf16[8,8192]{1,0:T(8,128)(2,1)S(1)}, bf16[8,8192]{1,0:T(8,128)(2,1)S(1)}, u32[]{:S(2)}, u32[]{:S(2)}) collective-permute-start(bf16[8,8192]{1,0:T(8,128)(2,1)S(1)} %pad_maximum_fusion.2.refs_0_), channel_id=1, source_target_pairs={{0,2},{1,3},{2,0},{3,1},{4,6},{5,7},{6,4},{7,5},{8,10},{9,11},{10,... | collective-permute-start | bytes 393224 | tf_op jit(solution)/shard_map/ppermute | solution.py:31
  13.1 3.1 %shard_map.57.refs_2_ = bf16[2048,1792]{1,0:T(8,128)(2,1)S(1)} custom-call(bf16[8192,1792]{1,0:T(8,128)(2,1)} %gate_ref.1, bf16[8,8192]{1,0:T(8,128)(2,1)S(1)} %pad_maximum_fusion.2.refs_0_), custom_call_target="tpu_custom_call" | custom-call | bytes 14680064 | tf_op jit(solution)/shard_map/pallas_call | solution.py:55
  16.2 0.3 collective-permute-done.2
  16.6 0.0 copy-start
  16.6 0.1 collective-permute-start.3
  16.7 1.5 %shard_map.58.refs_3_ = bf16[512,1792]{1,0:T(8,128)(2,1)S(1)} custom-call(bf16[8192,1792]{1,0:T(8,128)(2,1)} %gate_ref.1, bf16[16,8192]{1,0:T(8,128)(2,1)S(1)} %pad_maximum_fusion.1.refs_0_), custom_call_target="tpu_custom_call" | custom-call | bytes 3670016 | tf_op jit(solution)/shard_map/pallas_call | solution.py:55
  18.2 0.0 collective-permute-done.3
  18.2 0.1 broadcast_select_fusion.1
  18.3 0.0 copy-done
  18.3 15.5 %shard_map.59 = bf16[32,1792]{1,0:T(8,128)(2,1)S(1)} custom-call(bf16[32,8192]{1,0:T(8,128)(2,1)S(1)} %pad_maximum_fusion.x_ref, bf16[256,256]{1,0:T(8,128)(2,1)S(1)} %copy-done, bf16[8192,1792]{1,0:T(8,128)(2,1)} %gate_ref.1, bf16[8192,1792]{1,0:T(8,128)(2,1)} %up_ref.1, bf16[1024,1792]{1,0:T(8,128)(2,1)S(1)} %shard_map.55.refs_0_, ...), custom_call_target="tpu_custom_call" | custom-call | flops 1879048192 | bytes 38535168 | tf_op jit(solution)/shard_map/pallas_call | solution.py:137
  33.9 0.6 collective-permute-start.4
  34.4 1.0 %collective-permute-done.4 = bf16[32,1792]{1,0:T(8,128)(2,1)S(1)} collective-permute-done((bf16[32,1792]{1,0:T(8,128)(2,1)S(1)}, bf16[32,1792]{1,0:T(8,128)(2,1)S(1)}, u32[]{:S(2)}, u32[]{:S(2)}) %collective-permute-start.4) | collective-permute-done | bytes 114720 | tf_op jit(solution)/shard_map/ppermute | solution.py:31
  35.5 1.6 %collective-permute-start.5 = (bf16[32,1792]{1,0:T(8,128)(2,1)S(1)}, bf16[32,1792]{1,0:T(8,128)(2,1)S(1)}, u32[]{:S(2)}, u32[]{:S(2)}) collective-permute-start(bf16[32,1792]{1,0:T(8,128)(2,1)S(1)} %fusion.1.refs_0_), channel_id=1, source_target_pairs={{0,2},{1,3},{2,0},{3,1},{4,6},{5,7},{6,4},{7,5},{8,10},{9,11},{10,... | collective-permute-start | bytes 344072 | tf_op jit(solution)/shard_map/ppermute | solution.py:31
  37.1 2.2 %shard_map.60.refs_0_ = bf16[256,8192]{1,0:T(8,128)(2,1)S(1)} custom-call(bf16[1792,8192]{1,0:T(8,128)(2,1)} %weight_ref.15, bf16[32,1792]{1,0:T(8,128)(2,1)S(1)} %fusion.1.refs_0_), custom_call_target="tpu_custom_call" | custom-call | bytes 8388608 | tf_op jit(solution)/shard_map/pallas_call | solution.py:55
  39.3 1.7 %collective-permute-done.5 = bf16[32,1792]{1,0:T(8,128)(2,1)S(1)} collective-permute-done((bf16[32,1792]{1,0:T(8,128)(2,1)S(1)}, bf16[32,1792]{1,0:T(8,128)(2,1)S(1)}, u32[]{:S(2)}, u32[]{:S(2)}) %collective-permute-start.5) | collective-permute-done | bytes 114720 | tf_op jit(solution)/shard_map/ppermute | solution.py:31
  41.0 1.2 %collective-permute-start.6 = (bf16[32,1792]{1,0:T(8,128)(2,1)S(1)}, bf16[32,1792]{1,0:T(8,128)(2,1)S(1)}, u32[]{:S(2)}, u32[]{:S(2)}) collective-permute-start(bf16[32,1792]{1,0:T(8,128)(2,1)S(1)} %fusion.3.refs_0_), channel_id=1, source_target_pairs={{0,4},{1,5},{2,6},{3,7},{4,0},{5,1},{6,2},{7,3},{8,12},{9,13},{10,... | collective-permute-start | bytes 344072 | tf_op jit(solution)/shard_map/ppermute | solution.py:31
  42.2 2.2 %shard_map.61.refs_1_ = bf16[256,8192]{1,0:T(8,128)(2,1)S(1)} custom-call(bf16[1792,8192]{1,0:T(8,128)(2,1)} %weight_ref.15, bf16[32,1792]{1,0:T(8,128)(2,1)S(1)} %fusion.3.refs_0_), custom_call_target="tpu_custom_call" | custom-call | bytes 8388608 | tf_op jit(solution)/shard_map/pallas_call | solution.py:55
  44.4 1.4 %collective-permute-done.6 = bf16[32,1792]{1,0:T(8,128)(2,1)S(1)} collective-permute-done((bf16[32,1792]{1,0:T(8,128)(2,1)S(1)}, bf16[32,1792]{1,0:T(8,128)(2,1)S(1)}, u32[]{:S(2)}, u32[]{:S(2)}) %collective-permute-start.6) | collective-permute-done | bytes 114720 | tf_op jit(solution)/shard_map/ppermute | solution.py:31
  45.9 2.9 %collective-permute-start.7 = (bf16[32,1792]{1,0:T(8,128)(2,1)S(1)}, bf16[32,1792]{1,0:T(8,128)(2,1)S(1)}, u32[]{:S(2)}, u32[]{:S(2)}) collective-permute-start(bf16[32,1792]{1,0:T(8,128)(2,1)S(1)} %fusion.5.refs_0_), channel_id=1, source_target_pairs={{0,8},{1,9},{2,10},{3,11},{4,12},{5,13},{6,14},{7,15},{8,0},{9,1},... | collective-permute-start | bytes 344072 | tf_op jit(solution)/shard_map/ppermute | solution.py:31
  48.8 2.2 %shard_map.62.refs_2_ = bf16[256,8192]{1,0:T(8,128)(2,1)S(1)} custom-call(bf16[1792,8192]{1,0:T(8,128)(2,1)} %weight_ref.15, bf16[32,1792]{1,0:T(8,128)(2,1)S(1)} %fusion.5.refs_0_), custom_call_target="tpu_custom_call" | custom-call | bytes 8388608 | tf_op jit(solution)/shard_map/pallas_call | solution.py:55
  51.0 2.0 %collective-permute-done.7 = bf16[32,1792]{1,0:T(8,128)(2,1)S(1)} collective-permute-done((bf16[32,1792]{1,0:T(8,128)(2,1)S(1)}, bf16[32,1792]{1,0:T(8,128)(2,1)S(1)}, u32[]{:S(2)}, u32[]{:S(2)}) %collective-permute-start.7) | collective-permute-done | bytes 114720 | tf_op jit(solution)/shard_map/ppermute | solution.py:31
  52.9 0.1 fusion.8.rotated_ref
  53.0 6.9 %shard_map.63 = (f32[16,8192]{1,0:T(8,128)S(1)}, bf16[16,8192]{1,0:T(8,128)(2,1)S(1)}) custom-call(bf16[32,1792]{1,0:T(8,128)(2,1)S(1)} %fusion.8.rotated_ref, bf16[1792,8192]{1,0:T(8,128)(2,1)} %weight_ref.15, bf16[256,8192]{1,0:T(8,128)(2,1)S(1)} %shard_map.60.refs_0_, bf16[256,8192]{1,0:T(8,128)(2,1)S(1)} %shard_map.61.refs_1_, ...), custom_call_target="tpu_custom_call" | custom-call | flops 939524096 | bytes 16777216 | tf_op jit(solution)/shard_map/pallas_call | solution.py:213
  59.9 0.1 collective-permute-start.8
  60.0 1.5 %collective-permute-done.8 = bf16[16,8192]{1,0:T(8,128)(2,1)S(1)} collective-permute-done((bf16[16,8192]{1,0:T(8,128)(2,1)S(1)}, bf16[16,8192]{1,0:T(8,128)(2,1)S(1)}, u32[]{:S(2)}, u32[]{:S(2)}) %collective-permute-start.8) | collective-permute-done | bytes 262176 | tf_op jit(solution)/shard_map/ppermute | solution.py:31
  61.5 0.1 convert_add_fusion
  61.6 1.6 %collective-permute-start.9 = (bf16[8,8192]{1,0:T(8,128)(2,1)S(1)}, bf16[8,8192]{1,0:T(8,128)(2,1)S(1)}, u32[]{:S(2)}, u32[]{:S(2)}) collective-permute-start(bf16[8,8192]{1,0:T(8,128)(2,1)S(1)} %select_convert_fusion), channel_id=1, source_target_pairs={{0,2},{1,3},{2,0},{3,1},{4,6},{5,7},{6,4},{7,5},{8,10},{9,11},{10,... | collective-permute-start | bytes 393224 | tf_op jit(solution)/shard_map/ppermute | solution.py:31
  63.2 4.0 %collective-permute-done.9 = bf16[8,8192]{1,0:T(8,128)(2,1)S(1)} collective-permute-done((bf16[8,8192]{1,0:T(8,128)(2,1)S(1)}, bf16[8,8192]{1,0:T(8,128)(2,1)S(1)}, u32[]{:S(2)}, u32[]{:S(2)}) %collective-permute-start.9) | collective-permute-done | bytes 131104 | tf_op jit(solution)/shard_map/ppermute | solution.py:31
  67.2 0.1 select_convert_fusion.1
  67.3 0.6 collective-permute-start.10
  67.9 3.7 %collective-permute-done.10 = bf16[4,8192]{1,0:T(4,128)(2,1)S(1)} collective-permute-done((bf16[4,8192]{1,0:T(4,128)(2,1)S(1)}, bf16[4,8192]{1,0:T(4,128)(2,1)S(1)}, u32[]{:S(2)}, u32[]{:S(2)}) %collective-permute-start.10) | collective-permute-done | bytes 65568 | tf_op jit(solution)/shard_map/ppermute | solution.py:31
  71.7 0.1 select_convert_fusion.2
  71.7 2.0 %collective-permute-start.11 = (bf16[2,8192]{1,0:T(2,128)(2,1)S(1)}, bf16[2,8192]{1,0:T(2,128)(2,1)S(1)}, u32[]{:S(2)}, u32[]{:S(2)}) collective-permute-start(bf16[2,8192]{1,0:T(2,128)(2,1)S(1)} %select_convert_fusion.2), channel_id=1, source_target_pairs={{0,8},{1,9},{2,10},{3,11},{4,12},{5,13},{6,14},{7,15},{8,0},{9,1},... | collective-permute-start | bytes 98312 | tf_op jit(solution)/shard_map/ppermute | solution.py:31
  73.7 2.9 %collective-permute-done.11 = bf16[2,8192]{1,0:T(2,128)(2,1)S(1)} collective-permute-done((bf16[2,8192]{1,0:T(2,128)(2,1)S(1)}, bf16[2,8192]{1,0:T(2,128)(2,1)S(1)}, u32[]{:S(2)}, u32[]{:S(2)}) %collective-permute-start.11) | collective-permute-done | bytes 32800 | tf_op jit(solution)/shard_map/ppermute | solution.py:31
  76.6 0.7 add_convert_fusion
  (9 shorter events, 0.3 us)
Async XLA Ops:
  0.0 6.6 %copy-start.1 = (bf16[2,8192]{1,0:T(2,128)(2,1)S(1)}, bf16[2,8192]{1,0:T(2,128)(2,1)}, u32[]{:S(2)}) copy-start(bf16[2,8192]{1,0:T(2,128)(2,1)} %param.5) | copy-start | bytes 98308
  0.0 6.6 %collective-permute-start = (bf16[2,8192]{1,0:T(2,128)(2,1)}, bf16[2,8192]{1,0:T(2,128)(2,1)S(1)}, u32[]{:S(2)}, u32[]{:S(2)}) collective-permute-start(bf16[2,8192]{1,0:T(2,128)(2,1)} %param.5), channel_id=1, source_target_pairs={{0,8},{1,9},{2,10},{3,11},{4,12},{5,13},{6,14},{7,15},{8,0},{9,1},... | collective-permute-start | bytes 98312 | tf_op jit(solution)/shard_map/ppermute | solution.py:31
  6.7 4.7 %collective-permute-start.1 = (bf16[4,8192]{1,0:T(4,128)(2,1)S(1)}, bf16[4,8192]{1,0:T(4,128)(2,1)S(1)}, u32[]{:S(2)}, u32[]{:S(2)}) collective-permute-start(bf16[4,8192]{1,0:T(4,128)(2,1)S(1)} %pad_maximum_fusion.3.refs_0_), channel_id=1, source_target_pairs={{0,4},{1,5},{2,6},{3,7},{4,0},{5,1},{6,2},{7,3},{8,12},{9,13},{10,... | collective-permute-start | bytes 196616 | tf_op jit(solution)/shard_map/ppermute | solution.py:31
  11.5 5.0 %collective-permute-start.2 = (bf16[8,8192]{1,0:T(8,128)(2,1)S(1)}, bf16[8,8192]{1,0:T(8,128)(2,1)S(1)}, u32[]{:S(2)}, u32[]{:S(2)}) collective-permute-start(bf16[8,8192]{1,0:T(8,128)(2,1)S(1)} %pad_maximum_fusion.2.refs_0_), channel_id=1, source_target_pairs={{0,2},{1,3},{2,0},{3,1},{4,6},{5,7},{6,4},{7,5},{8,10},{9,11},{10,... | collective-permute-start | bytes 393224 | tf_op jit(solution)/shard_map/ppermute | solution.py:31
  16.6 1.7 %copy-start = (bf16[256,256]{1,0:T(8,128)(2,1)S(1)}, bf16[256,256]{1,0:T(8,128)(2,1)}, u32[]{:S(2)}) copy-start(bf16[256,256]{1,0:T(8,128)(2,1)} %constant.6.clone.spread_ref) | copy-start | bytes 393220
  16.6 1.6 %collective-permute-start.3 = (bf16[16,8192]{1,0:T(8,128)(2,1)S(1)}, bf16[16,8192]{1,0:T(8,128)(2,1)S(1)}, u32[]{:S(2)}, u32[]{:S(2)}) collective-permute-start(bf16[16,8192]{1,0:T(8,128)(2,1)S(1)} %pad_maximum_fusion.1.refs_0_), channel_id=1, source_target_pairs={{0,1},{1,0},{2,3},{3,2},{4,5},{5,4},{6,7},{7,6},{8,9},{9,8},{10,11... | collective-permute-start | bytes 786440 | tf_op jit(solution)/shard_map/ppermute | solution.py:31
  33.9 1.5 %collective-permute-start.4 = (bf16[32,1792]{1,0:T(8,128)(2,1)S(1)}, bf16[32,1792]{1,0:T(8,128)(2,1)S(1)}, u32[]{:S(2)}, u32[]{:S(2)}) collective-permute-start(bf16[32,1792]{1,0:T(8,128)(2,1)S(1)} %shard_map.59), channel_id=1, source_target_pairs={{0,1},{1,0},{2,3},{3,2},{4,5},{5,4},{6,7},{7,6},{8,9},{9,8},{10,11... | collective-permute-start | bytes 344072 | tf_op jit(solution)/shard_map/ppermute | solution.py:31
  35.5 5.5 %collective-permute-start.5 = (bf16[32,1792]{1,0:T(8,128)(2,1)S(1)}, bf16[32,1792]{1,0:T(8,128)(2,1)S(1)}, u32[]{:S(2)}, u32[]{:S(2)}) collective-permute-start(bf16[32,1792]{1,0:T(8,128)(2,1)S(1)} %fusion.1.refs_0_), channel_id=1, source_target_pairs={{0,2},{1,3},{2,0},{3,1},{4,6},{5,7},{6,4},{7,5},{8,10},{9,11},{10,... | collective-permute-start | bytes 344072 | tf_op jit(solution)/shard_map/ppermute | solution.py:31
  41.0 4.9 %collective-permute-start.6 = (bf16[32,1792]{1,0:T(8,128)(2,1)S(1)}, bf16[32,1792]{1,0:T(8,128)(2,1)S(1)}, u32[]{:S(2)}, u32[]{:S(2)}) collective-permute-start(bf16[32,1792]{1,0:T(8,128)(2,1)S(1)} %fusion.3.refs_0_), channel_id=1, source_target_pairs={{0,4},{1,5},{2,6},{3,7},{4,0},{5,1},{6,2},{7,3},{8,12},{9,13},{10,... | collective-permute-start | bytes 344072 | tf_op jit(solution)/shard_map/ppermute | solution.py:31
  45.9 7.1 %collective-permute-start.7 = (bf16[32,1792]{1,0:T(8,128)(2,1)S(1)}, bf16[32,1792]{1,0:T(8,128)(2,1)S(1)}, u32[]{:S(2)}, u32[]{:S(2)}) collective-permute-start(bf16[32,1792]{1,0:T(8,128)(2,1)S(1)} %fusion.5.refs_0_), channel_id=1, source_target_pairs={{0,8},{1,9},{2,10},{3,11},{4,12},{5,13},{6,14},{7,15},{8,0},{9,1},... | collective-permute-start | bytes 344072 | tf_op jit(solution)/shard_map/ppermute | solution.py:31
  59.9 1.6 %collective-permute-start.8 = (bf16[16,8192]{1,0:T(8,128)(2,1)S(1)}, bf16[16,8192]{1,0:T(8,128)(2,1)S(1)}, u32[]{:S(2)}, u32[]{:S(2)}) collective-permute-start(bf16[16,8192]{1,0:T(8,128)(2,1)S(1)} %get-tuple-element.54), channel_id=1, source_target_pairs={{0,1},{1,0},{2,3},{3,2},{4,5},{5,4},{6,7},{7,6},{8,9},{9,8},{10,11... | collective-permute-start | bytes 786440 | tf_op jit(solution)/shard_map/ppermute | solution.py:31
  61.6 5.6 %collective-permute-start.9 = (bf16[8,8192]{1,0:T(8,128)(2,1)S(1)}, bf16[8,8192]{1,0:T(8,128)(2,1)S(1)}, u32[]{:S(2)}, u32[]{:S(2)}) collective-permute-start(bf16[8,8192]{1,0:T(8,128)(2,1)S(1)} %select_convert_fusion), channel_id=1, source_target_pairs={{0,2},{1,3},{2,0},{3,1},{4,6},{5,7},{6,4},{7,5},{8,10},{9,11},{10,... | collective-permute-start | bytes 393224 | tf_op jit(solution)/shard_map/ppermute | solution.py:31
  67.3 4.3 %collective-permute-start.10 = (bf16[4,8192]{1,0:T(4,128)(2,1)S(1)}, bf16[4,8192]{1,0:T(4,128)(2,1)S(1)}, u32[]{:S(2)}, u32[]{:S(2)}) collective-permute-start(bf16[4,8192]{1,0:T(4,128)(2,1)S(1)} %select_convert_fusion.1), channel_id=1, source_target_pairs={{0,4},{1,5},{2,6},{3,7},{4,0},{5,1},{6,2},{7,3},{8,12},{9,13},{10,... | collective-permute-start | bytes 196616 | tf_op jit(solution)/shard_map/ppermute | solution.py:31
  71.7 4.9 %collective-permute-start.11 = (bf16[2,8192]{1,0:T(2,128)(2,1)S(1)}, bf16[2,8192]{1,0:T(2,128)(2,1)S(1)}, u32[]{:S(2)}, u32[]{:S(2)}) collective-permute-start(bf16[2,8192]{1,0:T(2,128)(2,1)S(1)} %select_convert_fusion.2), channel_id=1, source_target_pairs={{0,8},{1,9},{2,10},{3,11},{4,12},{5,13},{6,14},{7,15},{8,0},{9,1},... | collective-permute-start | bytes 98312 | tf_op jit(solution)/shard_map/ppermute | solution.py:31

commit v3 on v2

--- a/solution.py
+++ b/solution.py
@@ -13,8 +13,8 @@
 MIB = 2**20
 VMEM = pl.BlockSpec(memory_space=pltpu.VMEM)
 ANY = pl.BlockSpec(memory_space=pl.ANY)
-GATHER_BYTES = (4 * MIB, 8 * MIB, 8 * MIB, 2 * MIB)
-HADAMARD_BYTES = (0, 5 * MIB, 5 * MIB, 5 * MIB)
+GATHER_BYTES = (4 * MIB, 12 * MIB, 0)
+HADAMARD_BYTES = (0, 8 * MIB, 8 * MIB)
 
 
 def walsh(order):
@@ -109,12 +109,13 @@
         up_acc[...] = jnp.zeros_like(up_acc)
 
         def add(acc, first, rows, ref):
-            for n in range(0, width, tile):
-                acc[:, n : n + tile] += jnp.dot(
-                    x_ref[:, first : first + rows],
-                    ref[:, n : n + tile],
-                    preferred_element_type=jnp.float32,
-                )
+            for k in range(0, rows, chunk):
+                for n in range(0, width, tile):
+                    acc[:, n : n + tile] += jnp.dot(
+                        x_ref[:, first + k : first + k + chunk],
+                        ref[k : k + chunk, n : n + tile],
+                        preferred_element_type=jnp.float32,
+                    )
 
         first = 0
         for ref in piece_refs:
@@ -254,8 +255,12 @@
     return tuple(i ^ j for i, j in zip(a, b))
 
 
-def rounds_of(levels):
-    return [(level,) for level in range(levels)[::-1]]
+def gather_rounds(levels):
+    return [(level,) for level in range(levels)[:2:-1]] + [(1, 2), (0,)]
+
+
+def hadamard_rounds(levels):
+    return [(0,)] + [(level,) for level in range(levels)[3:]] + [(2, 1)]
 
 
 def per_device(tokens, gate_weight, up_weight, down_weight):
@@ -264,14 +269,15 @@
     depth, width = gate_weight.shape
     scale = np.float32(1.0 / np.sqrt(devices * BLOCK))
     index = lax.axis_index("tensor")
-    rounds = rounds_of(levels)
+    rounds = gather_rounds(levels)
+    turns = hadamard_rounds(levels)
     upper = [(index >> level) & 1 == 1 for level in range(levels)]
     odd = {}
-    for combined in rounds:
-        for flips, mask in masks_of(combined[::-1]):
+    for combined in turns:
+        for flips, mask in masks_of(combined):
             odd[combined, flips] = functools.reduce(
                 jnp.logical_xor,
-                [upper[level] for flip, level in zip(flips, combined[::-1]) if not flip],
+                [upper[level] for flip, level in zip(flips, combined) if not flip],
                 jnp.zeros_like(upper[0]),
             )
     tokens, upper, odd = lax.optimization_barrier((tokens, upper, odd))
@@ -296,11 +302,10 @@
 
     down_chunk = divisor(width, 256, 16)
     down_rows = Fetched(down_weight, down_chunk, width - down_chunk)
-    for number, combined in enumerate(rounds[::-1]):
-        levels_of = combined[::-1]
-        last = number == len(rounds) - 1
+    for number, combined in enumerate(turns):
+        last = number == len(turns) - 1
         got = {}
-        for flips, mask in masks_of(levels_of)[1:]:
+        for flips, mask in masks_of(combined)[1:]:
             got[flips] = swapped(local, mask)
         size = HADAMARD_BYTES[number] if number < len(HADAMARD_BYTES) else 0
         got[(0,) * len(combined)] = down_rows.beside(local, size, [local])

time: 77.7 us -> 72.5 us (0.933)
  Pallas kernels: 38.8 us -> 34 us
  waiting for transfers between devices: 19.1 us -> 14.6 us
  starting transfers between devices: 17.7 us -> 21.4 us
    ppermute x12 -> x15, waiting for transfers between devices: 19.1 us -> 14.6 us  [swapped(): return lax.ppermute(value, 'tensor', pairs)]
    ppermute x12 -> x15, starting transfers between devices: 17.7 us -> 21.4 us  [swapped(): return lax.ppermute(value, 'tensor', pairs)]
    pallas_call x7 -> x4, Pallas kernels: 16.3 us -> 13 us  [fetch(): pl.pallas_call(kernel, out_shape=jax.ShapeDtypeStruct((rows, width), weig...]
    pallas_call x1, Pallas kernels: 6.89 us -> 5.53 us  [down(): pl.pallas_call(kernel, out_shape=(jax.ShapeDtypeStruct((half, width), jnp...]
  transfers between devices with their start and end apart: 12 -> 15, of which waited for: 10 -> 12; matrix products, arithmetic and copies ran while one was open for 0% -> 0% of each run, Pallas kernels for 21% -> 18%
where the time goes in v3:
time: 72.5 us; the launch traced here: 72.3 us
  Pallas kernels  34 us (47%)
  starting transfers between devices  21.4 us (30%)
  waiting for transfers between devices  14.6 us (20%)
  other arithmetic  1.89 us (3%)
    ppermute x15, starting transfers between devices, swapped(): return lax.ppermute(value, 'tensor', pairs)  21.4 us
    pallas_call x1, Pallas kernels, gate_up(): pl.pallas_call(kernel, out_shape=jax.ShapeDtypeStruct((tokens, width), jn...  15.5 us
    ppermute x15, waiting for transfers between devices, swapped(): return lax.ppermute(value, 'tensor', pairs)  14.6 us
    pallas_call x4, Pallas kernels, fetch(): pl.pallas_call(kernel, out_shape=jax.ShapeDtypeStruct((rows, width), weig...  13 us
    pallas_call x1, Pallas kernels, down(): pl.pallas_call(kernel, out_shape=(jax.ShapeDtypeStruct((half, width), jnp...  5.53 us
  transfers between devices with their start and end apart: 15, of which 12 were waited for; matrix products, arithmetic and copies ran while one was open for 0% of the time, Pallas kernels for 18%

profile of v3, /device:TPU:0, one launch (start us, length us, event | category | flops | bytes accessed | tf_op | source)
XLA Modules:
  0.0 72.3 jit_solution(16452254477469209268)
XLA Ops:
  0.0 4.0 %collective-permute-start = (bf16[2,8192]{1,0:T(2,128)(2,1)}, bf16[2,8192]{1,0:T(2,128)(2,1)S(1)}, u32[]{:S(2)}, u32[]{:S(2)}) collective-permute-start(bf16[2,8192]{1,0:T(2,128)(2,1)} %param.5), channel_id=1, source_target_pairs={{0,8},{1,9},{2,10},{3,11},{4,12},{5,13},{6,14},{7,15},{8,0},{9,1},... | collective-permute-start | bytes 98312 | tf_op jit(solution)/shard_map/ppermute | solution.py:31
  4.0 2.0 %shard_map.55.refs_0_ = bf16[1024,1792]{1,0:T(8,128)(2,1)S(1)} custom-call(bf16[8192,1792]{1,0:T(8,128)(2,1)} %gate_ref.1), custom_call_target="tpu_custom_call" | custom-call | bytes 7340032 | tf_op jit(solution)/shard_map/pallas_call | solution.py:55
  6.1 0.5 collective-permute-done
  6.6 0.1 broadcast_select_fusion.11
  6.6 0.1 pad_maximum_fusion.2.refs_0_
  6.7 0.0 copy-start
  6.7 1.7 %collective-permute-start.3 = (bf16[4,8192]{1,0:T(4,128)(2,1)S(1)}, bf16[4,8192]{1,0:T(4,128)(2,1)S(1)}, u32[]{:S(2)}, u32[]{:S(2)}) collective-permute-start(bf16[4,8192]{1,0:T(4,128)(2,1)S(1)} %pad_maximum_fusion.2.refs_0_), channel_id=1, source_target_pairs={{0,2},{1,3},{2,0},{3,1},{4,6},{5,7},{6,4},{7,5},{8,10},{9,11},{10,... | collective-permute-start | bytes 196616 | tf_op jit(solution)/shard_map/ppermute | solution.py:31
  8.5 1.3 %collective-permute-start.2 = (bf16[4,8192]{1,0:T(4,128)(2,1)S(1)}, bf16[4,8192]{1,0:T(4,128)(2,1)S(1)}, u32[]{:S(2)}, u32[]{:S(2)}) collective-permute-start(bf16[4,8192]{1,0:T(4,128)(2,1)S(1)} %pad_maximum_fusion.2.refs_0_), channel_id=1, source_target_pairs={{0,4},{1,5},{2,6},{3,7},{4,0},{5,1},{6,2},{7,3},{8,12},{9,13},{10,... | collective-permute-start | bytes 196616 | tf_op jit(solution)/shard_map/ppermute | solution.py:31
  9.8 0.5 collective-permute-start.1
  10.3 4.1 %shard_map.56.refs_1_ = bf16[3072,1792]{1,0:T(8,128)(2,1)S(1)} custom-call(bf16[8192,1792]{1,0:T(8,128)(2,1)} %gate_ref.1, bf16[4,8192]{1,0:T(4,128)(2,1)S(1)} %pad_maximum_fusion.2.refs_0_), custom_call_target="tpu_custom_call" | custom-call | bytes 22020096 | tf_op jit(solution)/shard_map/pallas_call | solution.py:55
  14.4 0.0 collective-permute-done.2
  14.4 0.5 collective-permute-done.1
  15.0 0.1 broadcast_select_fusion.9
  15.1 0.2 pad_maximum_fusion.1
  15.3 0.1 collective-permute-start.4
  15.3 1.5 %collective-permute-done.4 = bf16[16,8192]{1,0:T(8,128)(2,1)S(1)} collective-permute-done((bf16[16,8192]{1,0:T(8,128)(2,1)S(1)}, bf16[16,8192]{1,0:T(8,128)(2,1)S(1)}, u32[]{:S(2)}, u32[]{:S(2)}) %collective-permute-start.4) | collective-permute-done | bytes 262176 | tf_op jit(solution)/shard_map/ppermute | solution.py:31
  16.9 0.2 broadcast_select_fusion.1
  17.1 15.5 %shard_map.57 = bf16[32,1792]{1,0:T(8,128)(2,1)S(1)} custom-call(bf16[32,8192]{1,0:T(8,128)(2,1)S(1)} %pad_maximum_fusion.x_ref, bf16[256,256]{1,0:T(8,128)(2,1)S(1)} %copy-done, bf16[8192,1792]{1,0:T(8,128)(2,1)} %gate_ref.1, bf16[8192,1792]{1,0:T(8,128)(2,1)} %up_ref.1, bf16[1024,1792]{1,0:T(8,128)(2,1)S(1)} %shard_map.55.refs_0_, ...), custom_call_target="tpu_custom_call" | custom-call | flops 1879048192 | bytes 44040192 | tf_op jit(solution)/shard_map/pallas_call | solution.py:138
  32.7 0.2 collective-permute-start.5
  32.9 1.2 %collective-permute-done.5 = bf16[32,1792]{1,0:T(8,128)(2,1)S(1)} collective-permute-done((bf16[32,1792]{1,0:T(8,128)(2,1)S(1)}, bf16[32,1792]{1,0:T(8,128)(2,1)S(1)}, u32[]{:S(2)}, u32[]{:S(2)}) %collective-permute-start.5) | collective-permute-done | bytes 114720 | tf_op jit(solution)/shard_map/ppermute | solution.py:31
  34.1 2.9 %collective-permute-start.6 = (bf16[32,1792]{1,0:T(8,128)(2,1)S(1)}, bf16[32,1792]{1,0:T(8,128)(2,1)S(1)}, u32[]{:S(2)}, u32[]{:S(2)}) collective-permute-start(bf16[32,1792]{1,0:T(8,128)(2,1)S(1)} %fusion.1.refs_0_), channel_id=1, source_target_pairs={{0,8},{1,9},{2,10},{3,11},{4,12},{5,13},{6,14},{7,15},{8,0},{9,1},... | collective-permute-start | bytes 344072 | tf_op jit(solution)/shard_map/ppermute | solution.py:31
  37.0 3.4 %shard_map.58.refs_0_ = bf16[512,8192]{1,0:T(8,128)(2,1)S(1)} custom-call(bf16[1792,8192]{1,0:T(8,128)(2,1)} %weight_ref.9, bf16[32,1792]{1,0:T(8,128)(2,1)S(1)} %fusion.1.refs_0_), custom_call_target="tpu_custom_call" | custom-call | bytes 16777216 | tf_op jit(solution)/shard_map/pallas_call | solution.py:55
  40.4 2.5 %collective-permute-done.6 = bf16[32,1792]{1,0:T(8,128)(2,1)S(1)} collective-permute-done((bf16[32,1792]{1,0:T(8,128)(2,1)S(1)}, bf16[32,1792]{1,0:T(8,128)(2,1)S(1)}, u32[]{:S(2)}, u32[]{:S(2)}) %collective-permute-start.6) | collective-permute-done | bytes 114720 | tf_op jit(solution)/shard_map/ppermute | solution.py:31
  43.0 1.0 %collective-permute-start.9 = (bf16[32,1792]{1,0:T(8,128)(2,1)S(1)}, bf16[32,1792]{1,0:T(8,128)(2,1)S(1)}, u32[]{:S(2)}, u32[]{:S(2)}) collective-permute-start(bf16[32,1792]{1,0:T(8,128)(2,1)S(1)} %fusion.3.refs_0_), channel_id=1, source_target_pairs={{0,6},{1,7},{2,4},{3,5},{4,2},{5,3},{6,0},{7,1},{8,14},{9,15},{10,... | collective-permute-start | bytes 344072 | tf_op jit(solution)/shard_map/ppermute | solution.py:31
  44.0 1.6 %collective-permute-start.8 = (bf16[32,1792]{1,0:T(8,128)(2,1)S(1)}, bf16[32,1792]{1,0:T(8,128)(2,1)S(1)}, u32[]{:S(2)}, u32[]{:S(2)}) collective-permute-start(bf16[32,1792]{1,0:T(8,128)(2,1)S(1)} %fusion.3.refs_0_), channel_id=1, source_target_pairs={{0,4},{1,5},{2,6},{3,7},{4,0},{5,1},{6,2},{7,3},{8,12},{9,13},{10,... | collective-permute-start | bytes 344072 | tf_op jit(solution)/shard_map/ppermute | solution.py:31
  45.5 1.0 %collective-permute-start.7 = (bf16[32,1792]{1,0:T(8,128)(2,1)S(1)}, bf16[32,1792]{1,0:T(8,128)(2,1)S(1)}, u32[]{:S(2)}, u32[]{:S(2)}) collective-permute-start(bf16[32,1792]{1,0:T(8,128)(2,1)S(1)} %fusion.3.refs_0_), channel_id=1, source_target_pairs={{0,2},{1,3},{2,0},{3,1},{4,6},{5,7},{6,4},{7,5},{8,10},{9,11},{10,... | collective-permute-start | bytes 344072 | tf_op jit(solution)/shard_map/ppermute | solution.py:31
  46.6 3.4 %shard_map.59.refs_1_ = bf16[512,8192]{1,0:T(8,128)(2,1)S(1)} custom-call(bf16[1792,8192]{1,0:T(8,128)(2,1)} %weight_ref.9, bf16[32,1792]{1,0:T(8,128)(2,1)S(1)} %fusion.3.refs_0_), custom_call_target="tpu_custom_call" | custom-call | bytes 16777216 | tf_op jit(solution)/shard_map/pallas_call | solution.py:55
  50.0 0.0 collective-permute-done.9
  50.0 0.4 collective-permute-done.8
  50.3 0.8 %collective-permute-done.7 = bf16[32,1792]{1,0:T(8,128)(2,1)S(1)} collective-permute-done((bf16[32,1792]{1,0:T(8,128)(2,1)S(1)}, bf16[32,1792]{1,0:T(8,128)(2,1)S(1)}, u32[]{:S(2)}, u32[]{:S(2)}) %collective-permute-start.7) | collective-permute-done | bytes 114720 | tf_op jit(solution)/shard_map/ppermute | solution.py:31
  51.1 0.1 fusion.8.rotated_ref
  51.2 5.5 %shard_map.60 = (f32[16,8192]{1,0:T(8,128)S(1)}, bf16[16,8192]{1,0:T(8,128)(2,1)S(1)}) custom-call(bf16[32,1792]{1,0:T(8,128)(2,1)S(1)} %fusion.8.rotated_ref, bf16[1792,8192]{1,0:T(8,128)(2,1)} %weight_ref.9, bf16[512,8192]{1,0:T(8,128)(2,1)S(1)} %shard_map.58.refs_0_, bf16[512,8192]{1,0:T(8,128)(2,1)S(1)} %shard_map.59.refs_1_), custom_call_target="tpu_custom_call" | custom-call | flops 939524096 | bytes 12582912 | tf_op jit(solution)/shard_map/pallas_call | solution.py:214
  56.8 0.1 collective-permute-start.10
  56.9 1.5 %collective-permute-done.10 = bf16[16,8192]{1,0:T(8,128)(2,1)S(1)} collective-permute-done((bf16[16,8192]{1,0:T(8,128)(2,1)S(1)}, bf16[16,8192]{1,0:T(8,128)(2,1)S(1)}, u32[]{:S(2)}, u32[]{:S(2)}) %collective-permute-start.10) | collective-permute-done | bytes 262176 | tf_op jit(solution)/shard_map/ppermute | solution.py:31
  58.4 0.1 convert_add_fusion
  58.4 0.1 reshape.27
  58.6 0.1 fusion.11
  58.7 0.9 %collective-permute-start.11 = (bf16[4,8192]{1,0:T(4,128)(2,1)S(1)}, bf16[4,8192]{1,0:T(4,128)(2,1)S(1)}, u32[]{:S(2)}, u32[]{:S(2)}) collective-permute-start(bf16[4,8192]{1,0:T(4,128)(2,1)S(1)} %get-tuple-element.45), channel_id=1, source_target_pairs={{0,2},{1,3},{2,0},{3,1},{4,6},{5,7},{6,4},{7,5},{8,10},{9,11},{10,... | collective-permute-start | bytes 196616 | tf_op jit(solution)/shard_map/ppermute | solution.py:31
  59.6 1.0 %collective-permute-start.12 = (bf16[4,8192]{1,0:T(4,128)(2,1)S(1)}, bf16[4,8192]{1,0:T(4,128)(2,1)S(1)}, u32[]{:S(2)}, u32[]{:S(2)}) collective-permute-start(bf16[4,8192]{1,0:T(4,128)(2,1)S(1)} %get-tuple-element.46), channel_id=1, source_target_pairs={{0,4},{1,5},{2,6},{3,7},{4,0},{5,1},{6,2},{7,3},{8,12},{9,13},{10,... | collective-permute-start | bytes 196616 | tf_op jit(solution)/shard_map/ppermute | solution.py:31
  60.6 1.7 %collective-permute-start.13 = (bf16[4,8192]{1,0:T(4,128)(2,1)S(1)}, bf16[4,8192]{1,0:T(4,128)(2,1)S(1)}, u32[]{:S(2)}, u32[]{:S(2)}) collective-permute-start(bf16[4,8192]{1,0:T(4,128)(2,1)S(1)} %get-tuple-element.47), channel_id=1, source_target_pairs={{0,6},{1,7},{2,4},{3,5},{4,2},{5,3},{6,0},{7,1},{8,14},{9,15},{10,... | collective-permute-start | bytes 196616 | tf_op jit(solution)/shard_map/ppermute | solution.py:31
  62.3 0.8 %collective-permute-done.11 = bf16[4,8192]{1,0:T(4,128)(2,1)S(1)} collective-permute-done((bf16[4,8192]{1,0:T(4,128)(2,1)S(1)}, bf16[4,8192]{1,0:T(4,128)(2,1)S(1)}, u32[]{:S(2)}, u32[]{:S(2)}) %collective-permute-start.11) | collective-permute-done | bytes 65568 | tf_op jit(solution)/shard_map/ppermute | solution.py:31
  63.0 1.1 %collective-permute-done.12 = bf16[4,8192]{1,0:T(4,128)(2,1)S(1)} collective-permute-done((bf16[4,8192]{1,0:T(4,128)(2,1)S(1)}, bf16[4,8192]{1,0:T(4,128)(2,1)S(1)}, u32[]{:S(2)}, u32[]{:S(2)}) %collective-permute-start.12) | collective-permute-done | bytes 65568 | tf_op jit(solution)/shard_map/ppermute | solution.py:31
  64.2 1.6 %collective-permute-done.13 = bf16[4,8192]{1,0:T(4,128)(2,1)S(1)} collective-permute-done((bf16[4,8192]{1,0:T(4,128)(2,1)S(1)}, bf16[4,8192]{1,0:T(4,128)(2,1)S(1)}, u32[]{:S(2)}, u32[]{:S(2)}) %collective-permute-start.13) | collective-permute-done | bytes 65568 | tf_op jit(solution)/shard_map/ppermute | solution.py:31
  65.8 0.1 fusion.10
  65.9 0.1 select_convert_fusion.3
  66.0 3.4 %collective-permute-start.14 = (bf16[2,8192]{1,0:T(2,128)(2,1)S(1)}, bf16[2,8192]{1,0:T(2,128)(2,1)S(1)}, u32[]{:S(2)}, u32[]{:S(2)}) collective-permute-start(bf16[2,8192]{1,0:T(2,128)(2,1)S(1)} %select_convert_fusion.3), channel_id=1, source_target_pairs={{0,8},{1,9},{2,10},{3,11},{4,12},{5,13},{6,14},{7,15},{8,0},{9,1},... | collective-permute-start | bytes 98312 | tf_op jit(solution)/shard_map/ppermute | solution.py:31
  69.4 2.2 %collective-permute-done.14 = bf16[2,8192]{1,0:T(2,128)(2,1)S(1)} collective-permute-done((bf16[2,8192]{1,0:T(2,128)(2,1)S(1)}, bf16[2,8192]{1,0:T(2,128)(2,1)S(1)}, u32[]{:S(2)}, u32[]{:S(2)}) %collective-permute-start.14) | collective-permute-done | bytes 32800 | tf_op jit(solution)/shard_map/ppermute | solution.py:31
  71.6 0.7 add_convert_fusion
  (7 shorter events, 0.1 us)
Async XLA Ops:
  0.0 6.6 %copy-start.1 = (bf16[2,8192]{1,0:T(2,128)(2,1)S(1)}, bf16[2,8192]{1,0:T(2,128)(2,1)}, u32[]{:S(2)}) copy-start(bf16[2,8192]{1,0:T(2,128)(2,1)} %param.5) | copy-start | bytes 98308
  0.0 6.6 %collective-permute-start = (bf16[2,8192]{1,0:T(2,128)(2,1)}, bf16[2,8192]{1,0:T(2,128)(2,1)S(1)}, u32[]{:S(2)}, u32[]{:S(2)}) collective-permute-start(bf16[2,8192]{1,0:T(2,128)(2,1)} %param.5), channel_id=1, source_target_pairs={{0,8},{1,9},{2,10},{3,11},{4,12},{5,13},{6,14},{7,15},{8,0},{9,1},... | collective-permute-start | bytes 98312 | tf_op jit(solution)/shard_map/ppermute | solution.py:31
  6.7 10.4 %copy-start = (bf16[256,256]{1,0:T(8,128)(2,1)S(1)}, bf16[256,256]{1,0:T(8,128)(2,1)}, u32[]{:S(2)}) copy-start(bf16[256,256]{1,0:T(8,128)(2,1)} %constant.6.clone.spread_ref) | copy-start | bytes 393220
  6.7 7.7 %collective-permute-start.3 = (bf16[4,8192]{1,0:T(4,128)(2,1)S(1)}, bf16[4,8192]{1,0:T(4,128)(2,1)S(1)}, u32[]{:S(2)}, u32[]{:S(2)}) collective-permute-start(bf16[4,8192]{1,0:T(4,128)(2,1)S(1)} %pad_maximum_fusion.2.refs_0_), channel_id=1, source_target_pairs={{0,2},{1,3},{2,0},{3,1},{4,6},{5,7},{6,4},{7,5},{8,10},{9,11},{10,... | collective-permute-start | bytes 196616 | tf_op jit(solution)/shard_map/ppermute | solution.py:31
  8.5 6.0 %collective-permute-start.2 = (bf16[4,8192]{1,0:T(4,128)(2,1)S(1)}, bf16[4,8192]{1,0:T(4,128)(2,1)S(1)}, u32[]{:S(2)}, u32[]{:S(2)}) collective-permute-start(bf16[4,8192]{1,0:T(4,128)(2,1)S(1)} %pad_maximum_fusion.2.refs_0_), channel_id=1, source_target_pairs={{0,4},{1,5},{2,6},{3,7},{4,0},{5,1},{6,2},{7,3},{8,12},{9,13},{10,... | collective-permute-start | bytes 196616 | tf_op jit(solution)/shard_map/ppermute | solution.py:31
  9.8 5.2 %collective-permute-start.1 = (bf16[4,8192]{1,0:T(4,128)(2,1)S(1)}, bf16[4,8192]{1,0:T(4,128)(2,1)S(1)}, u32[]{:S(2)}, u32[]{:S(2)}) collective-permute-start(bf16[4,8192]{1,0:T(4,128)(2,1)S(1)} %pad_maximum_fusion.2.refs_0_), channel_id=1, source_target_pairs={{0,6},{1,7},{2,4},{3,5},{4,2},{5,3},{6,0},{7,1},{8,14},{9,15},{10,... | collective-permute-start | bytes 196616 | tf_op jit(solution)/shard_map/ppermute | solution.py:31
  15.3 1.6 %collective-permute-start.4 = (bf16[16,8192]{1,0:T(8,128)(2,1)S(1)}, bf16[16,8192]{1,0:T(8,128)(2,1)S(1)}, u32[]{:S(2)}, u32[]{:S(2)}) collective-permute-start(bf16[16,8192]{1,0:T(8,128)(2,1)S(1)} %pad_maximum_fusion.1), channel_id=1, source_target_pairs={{0,1},{1,0},{2,3},{3,2},{4,5},{5,4},{6,7},{7,6},{8,9},{9,8},{10,11... | collective-permute-start | bytes 786440 | tf_op jit(solution)/shard_map/ppermute | solution.py:31
  32.7 1.4 %collective-permute-start.5 = (bf16[32,1792]{1,0:T(8,128)(2,1)S(1)}, bf16[32,1792]{1,0:T(8,128)(2,1)S(1)}, u32[]{:S(2)}, u32[]{:S(2)}) collective-permute-start(bf16[32,1792]{1,0:T(8,128)(2,1)S(1)} %shard_map.57), channel_id=1, source_target_pairs={{0,1},{1,0},{2,3},{3,2},{4,5},{5,4},{6,7},{7,6},{8,9},{9,8},{10,11... | collective-permute-start | bytes 344072 | tf_op jit(solution)/shard_map/ppermute | solution.py:31
  34.1 8.8 %collective-permute-start.6 = (bf16[32,1792]{1,0:T(8,128)(2,1)S(1)}, bf16[32,1792]{1,0:T(8,128)(2,1)S(1)}, u32[]{:S(2)}, u32[]{:S(2)}) collective-permute-start(bf16[32,1792]{1,0:T(8,128)(2,1)S(1)} %fusion.1.refs_0_), channel_id=1, source_target_pairs={{0,8},{1,9},{2,10},{3,11},{4,12},{5,13},{6,14},{7,15},{8,0},{9,1},... | collective-permute-start | bytes 344072 | tf_op jit(solution)/shard_map/ppermute | solution.py:31
  43.0 7.0 %collective-permute-start.9 = (bf16[32,1792]{1,0:T(8,128)(2,1)S(1)}, bf16[32,1792]{1,0:T(8,128)(2,1)S(1)}, u32[]{:S(2)}, u32[]{:S(2)}) collective-permute-start(bf16[32,1792]{1,0:T(8,128)(2,1)S(1)} %fusion.3.refs_0_), channel_id=1, source_target_pairs={{0,6},{1,7},{2,4},{3,5},{4,2},{5,3},{6,0},{7,1},{8,14},{9,15},{10,... | collective-permute-start | bytes 344072 | tf_op jit(solution)/shard_map/ppermute | solution.py:31
  44.0 6.4 %collective-permute-start.8 = (bf16[32,1792]{1,0:T(8,128)(2,1)S(1)}, bf16[32,1792]{1,0:T(8,128)(2,1)S(1)}, u32[]{:S(2)}, u32[]{:S(2)}) collective-permute-start(bf16[32,1792]{1,0:T(8,128)(2,1)S(1)} %fusion.3.refs_0_), channel_id=1, source_target_pairs={{0,4},{1,5},{2,6},{3,7},{4,0},{5,1},{6,2},{7,3},{8,12},{9,13},{10,... | collective-permute-start | bytes 344072 | tf_op jit(solution)/shard_map/ppermute | solution.py:31
  45.5 5.6 %collective-permute-start.7 = (bf16[32,1792]{1,0:T(8,128)(2,1)S(1)}, bf16[32,1792]{1,0:T(8,128)(2,1)S(1)}, u32[]{:S(2)}, u32[]{:S(2)}) collective-permute-start(bf16[32,1792]{1,0:T(8,128)(2,1)S(1)} %fusion.3.refs_0_), channel_id=1, source_target_pairs={{0,2},{1,3},{2,0},{3,1},{4,6},{5,7},{6,4},{7,5},{8,10},{9,11},{10,... | collective-permute-start | bytes 344072 | tf_op jit(solution)/shard_map/ppermute | solution.py:31
  56.8 1.6 %collective-permute-start.10 = (bf16[16,8192]{1,0:T(8,128)(2,1)S(1)}, bf16[16,8192]{1,0:T(8,128)(2,1)S(1)}, u32[]{:S(2)}, u32[]{:S(2)}) collective-permute-start(bf16[16,8192]{1,0:T(8,128)(2,1)S(1)} %get-tuple-element.44), channel_id=1, source_target_pairs={{0,1},{1,0},{2,3},{3,2},{4,5},{5,4},{6,7},{7,6},{8,9},{9,8},{10,11... | collective-permute-start | bytes 786440 | tf_op jit(solution)/shard_map/ppermute | solution.py:31
  58.7 4.3 %collective-permute-start.11 = (bf16[4,8192]{1,0:T(4,128)(2,1)S(1)}, bf16[4,8192]{1,0:T(4,128)(2,1)S(1)}, u32[]{:S(2)}, u32[]{:S(2)}) collective-permute-start(bf16[4,8192]{1,0:T(4,128)(2,1)S(1)} %get-tuple-element.45), channel_id=1, source_target_pairs={{0,2},{1,3},{2,0},{3,1},{4,6},{5,7},{6,4},{7,5},{8,10},{9,11},{10,... | collective-permute-start | bytes 196616 | tf_op jit(solution)/shard_map/ppermute | solution.py:31
  59.6 4.6 %collective-permute-start.12 = (bf16[4,8192]{1,0:T(4,128)(2,1)S(1)}, bf16[4,8192]{1,0:T(4,128)(2,1)S(1)}, u32[]{:S(2)}, u32[]{:S(2)}) collective-permute-start(bf16[4,8192]{1,0:T(4,128)(2,1)S(1)} %get-tuple-element.46), channel_id=1, source_target_pairs={{0,4},{1,5},{2,6},{3,7},{4,0},{5,1},{6,2},{7,3},{8,12},{9,13},{10,... | collective-permute-start | bytes 196616 | tf_op jit(solution)/shard_map/ppermute | solution.py:31
  60.6 5.2 %collective-permute-start.13 = (bf16[4,8192]{1,0:T(4,128)(2,1)S(1)}, bf16[4,8192]{1,0:T(4,128)(2,1)S(1)}, u32[]{:S(2)}, u32[]{:S(2)}) collective-permute-start(bf16[4,8192]{1,0:T(4,128)(2,1)S(1)} %get-tuple-element.47), channel_id=1, source_target_pairs={{0,6},{1,7},{2,4},{3,5},{4,2},{5,3},{6,0},{7,1},{8,14},{9,15},{10,... | collective-permute-start | bytes 196616 | tf_op jit(solution)/shard_map/ppermute | solution.py:31
  66.0 5.7 %collective-permute-start.14 = (bf16[2,8192]{1,0:T(2,128)(2,1)S(1)}, bf16[2,8192]{1,0:T(2,128)(2,1)S(1)}, u32[]{:S(2)}, u32[]{:S(2)}) collective-permute-start(bf16[2,8192]{1,0:T(2,128)(2,1)S(1)} %select_convert_fusion.3), channel_id=1, source_target_pairs={{0,8},{1,9},{2,10},{3,11},{4,12},{5,13},{6,14},{7,15},{8,0},{9,1},... | collective-permute-start | bytes 98312 | tf_op jit(solution)/shard_map/ppermute | solution.py:31

commit v4 on v3

--- a/solution.py
+++ b/solution.py
@@ -13,8 +13,9 @@
 MIB = 2**20
 VMEM = pl.BlockSpec(memory_space=pltpu.VMEM)
 ANY = pl.BlockSpec(memory_space=pl.ANY)
-GATHER_BYTES = (4 * MIB, 12 * MIB, 0)
-HADAMARD_BYTES = (0, 8 * MIB, 8 * MIB)
+GATHER_BYTES = (4 * MIB, 12 * MIB, 3 * MIB)
+HADAMARD_BYTES = (0, 12 * MIB, 12 * MIB)
+SLOTS = 5
 
 
 def walsh(order):
@@ -84,11 +85,15 @@
     tokens, depth = x.shape
     width = gate.shape[1]
     tile = divisor(width, 256, BLOCK)
+    wide = width // 2 if width % 256 == 0 else tile
     pieces = fetched.pieces
     count = len(pieces)
-    chunks = [(0, first) for first in range(fetched.rows, depth, chunk)]
-    chunks += [(1, first) for first in range(0, depth, chunk)]
-    slots = min(8, len(chunks))
+    chunks = [
+        (which, first, min(chunk, depth - first))
+        for which, begin in ((0, fetched.rows), (1, 0))
+        for first in range(begin, depth, chunk)
+    ]
+    slots = min(SLOTS, len(chunks))
     spread = np.kron(np.eye(tile // BLOCK, dtype=np.float32), walsh(BLOCK))
 
     def kernel(x_ref, spread_ref, gate_ref, up_ref, *refs):
@@ -96,10 +101,10 @@
         out_ref, gate_acc, up_acc, buffer, sems = refs[count:]
 
         def copy(i):
-            which, first = chunks[i]
+            which, first, rows = chunks[i]
             return pltpu.make_async_copy(
-                (gate_ref, up_ref)[which].at[pl.ds(first, chunk)],
-                buffer.at[i % slots],
+                (gate_ref, up_ref)[which].at[pl.ds(first, rows)],
+                buffer.at[i % slots, pl.ds(0, rows)],
                 sems.at[i % slots],
             )
 
@@ -109,21 +114,20 @@
         up_acc[...] = jnp.zeros_like(up_acc)
 
         def add(acc, first, rows, ref):
-            for k in range(0, rows, chunk):
-                for n in range(0, width, tile):
-                    acc[:, n : n + tile] += jnp.dot(
-                        x_ref[:, first + k : first + k + chunk],
-                        ref[k : k + chunk, n : n + tile],
-                        preferred_element_type=jnp.float32,
-                    )
+            for n in range(0, width, wide):
+                acc[:, n : n + wide] += jnp.dot(
+                    x_ref[:, first : first + rows],
+                    ref[:rows, n : n + wide],
+                    preferred_element_type=jnp.float32,
+                )
 
         first = 0
         for ref in piece_refs:
             add(gate_acc, first, ref.shape[0], ref)
             first += ref.shape[0]
-        for i, (which, first) in enumerate(chunks):
+        for i, (which, first, rows) in enumerate(chunks):
             copy(i).wait()
-            add((gate_acc, up_acc)[which], first, chunk, buffer.at[i % slots])
+            add((gate_acc, up_acc)[which], first, rows, buffer.at[i % slots])
             if i + slots < len(chunks):
                 copy(i + slots).start()
         for n in range(0, width, tile):
@@ -149,7 +153,7 @@
         cost_estimate=pl.CostEstimate(
             flops=4 * tokens * depth * width,
             transcendentals=tokens * width,
-            bytes_accessed=len(chunks) * chunk * size,
+            bytes_accessed=sum(rows for _, _, rows in chunks) * size,
         ),
         compiler_params=pltpu.CompilerParams(
             vmem_limit_bytes=slots * chunk * size + 3 * tokens * width * 4 + 4 * MIB
@@ -298,7 +302,7 @@
             rows.append(pick({xor(slot, flips): v for flips, v in got.items()}, bits))
         piece = jnp.concatenate(rows, axis=0)
 
-    local = gate_up(piece, gate_weight, up_weight, gate_rows, gate_chunk)
+    local = gate_up(piece, gate_weight, up_weight, gate_rows, 3 * gate_chunk)
 
     down_chunk = divisor(width, 256, 16)
     down_rows = Fetched(down_weight, down_chunk, width - down_chunk)

time: 72.5 us -> 71.3 us (0.983)
  waiting for transfers between devices: 14.6 us -> 10.7 us
  Pallas kernels: 34 us -> 36.5 us
    ppermute x15, waiting for transfers between devices: 14.6 us -> 10.7 us  [swapped(): return lax.ppermute(value, 'tensor', pairs)]
    pallas_call x4 -> x5, Pallas kernels: 13 us -> 16.9 us  [fetch(): pl.pallas_call(kernel, out_shape=jax.ShapeDtypeStruct((rows, width), weig...]
    pallas_call x1, Pallas kernels: 15.5 us -> 14.5 us  [gate_up(): pl.pallas_call(kernel, out_shape=jax.ShapeDtypeStruct((tokens, width), jn...]
  transfers between devices with their start and end apart: 15 -> 15, of which waited for: 12 -> 10; matrix products, arithmetic and copies ran while one was open for 0% -> 0% of each run, Pallas kernels for 18% -> 24%
where the time goes in v4:
time: 71.3 us; the launch traced here: 71 us
  Pallas kernels  36.5 us (51%)
  starting transfers between devices  21.7 us (30%)
  waiting for transfers between devices  10.7 us (15%)
  other arithmetic  1.74 us (2%)
    ppermute x15, starting transfers between devices, swapped(): return lax.ppermute(value, 'tensor', pairs)  21.7 us
    pallas_call x5, Pallas kernels, fetch(): pl.pallas_call(kernel, out_shape=jax.ShapeDtypeStruct((rows, width), weig...  16.9 us
    pallas_call x1, Pallas kernels, gate_up(): pl.pallas_call(kernel, out_shape=jax.ShapeDtypeStruct((tokens, width), jn...  14.5 us
    ppermute x15, waiting for transfers between devices, swapped(): return lax.ppermute(value, 'tensor', pairs)  10.7 us
    pallas_call x1, Pallas kernels, down(): pl.pallas_call(kernel, out_shape=(jax.ShapeDtypeStruct((half, width), jnp...  5.14 us
  transfers between devices with their start and end apart: 15, of which 10 were waited for; matrix products, arithmetic and copies ran while one was open for 0% of the time, Pallas kernels for 24%

profile of v4, /device:TPU:0, one launch (start us, length us, event | category | flops | bytes accessed | tf_op | source)
XLA Modules:
  0.0 71.0 jit_solution(3292913070496236077)
XLA Ops:
  0.0 4.0 %collective-permute-start = (bf16[2,8192]{1,0:T(2,128)(2,1)}, bf16[2,8192]{1,0:T(2,128)(2,1)S(1)}, u32[]{:S(2)}, u32[]{:S(2)}) collective-permute-start(bf16[2,8192]{1,0:T(2,128)(2,1)} %param.5), channel_id=1, source_target_pairs={{0,8},{1,9},{2,10},{3,11},{4,12},{5,13},{6,14},{7,15},{8,0},{9,1},... | collective-permute-start | bytes 98312 | tf_op jit(solution)/shard_map/ppermute | solution.py:32
  4.0 2.0 %shard_map.55.refs_0_ = bf16[1024,1792]{1,0:T(8,128)(2,1)S(1)} custom-call(bf16[8192,1792]{1,0:T(8,128)(2,1)} %gate_ref.1), custom_call_target="tpu_custom_call" | custom-call | bytes 7340032 | tf_op jit(solution)/shard_map/pallas_call | solution.py:56
  6.1 0.5 collective-permute-done
  6.6 0.1 broadcast_select_fusion.11
  6.6 0.1 pad_maximum_fusion.2.refs_0_
  6.7 1.7 %collective-permute-start.3 = (bf16[4,8192]{1,0:T(4,128)(2,1)S(1)}, bf16[4,8192]{1,0:T(4,128)(2,1)S(1)}, u32[]{:S(2)}, u32[]{:S(2)}) collective-permute-start(bf16[4,8192]{1,0:T(4,128)(2,1)S(1)} %pad_maximum_fusion.2.refs_0_), channel_id=1, source_target_pairs={{0,2},{1,3},{2,0},{3,1},{4,6},{5,7},{6,4},{7,5},{8,10},{9,11},{10,... | collective-permute-start | bytes 196616 | tf_op jit(solution)/shard_map/ppermute | solution.py:32
  8.5 1.3 %collective-permute-start.2 = (bf16[4,8192]{1,0:T(4,128)(2,1)S(1)}, bf16[4,8192]{1,0:T(4,128)(2,1)S(1)}, u32[]{:S(2)}, u32[]{:S(2)}) collective-permute-start(bf16[4,8192]{1,0:T(4,128)(2,1)S(1)} %pad_maximum_fusion.2.refs_0_), channel_id=1, source_target_pairs={{0,4},{1,5},{2,6},{3,7},{4,0},{5,1},{6,2},{7,3},{8,12},{9,13},{10,... | collective-permute-start | bytes 196616 | tf_op jit(solution)/shard_map/ppermute | solution.py:32
  9.8 0.5 collective-permute-start.1
  10.3 4.1 %shard_map.56.refs_1_ = bf16[3072,1792]{1,0:T(8,128)(2,1)S(1)} custom-call(bf16[8192,1792]{1,0:T(8,128)(2,1)} %gate_ref.1, bf16[4,8192]{1,0:T(4,128)(2,1)S(1)} %pad_maximum_fusion.2.refs_0_), custom_call_target="tpu_custom_call" | custom-call | bytes 22020096 | tf_op jit(solution)/shard_map/pallas_call | solution.py:56
  14.4 0.0 collective-permute-done.3
  14.4 0.0 collective-permute-done.2
  14.4 0.5 collective-permute-done.1
  14.9 0.1 broadcast_select_fusion.9
  15.1 0.2 pad_maximum_fusion.1.refs_0_
  15.3 0.0 copy-start
  15.3 0.1 collective-permute-start.4
  15.3 1.5 %shard_map.57.refs_2_ = bf16[512,1792]{1,0:T(8,128)(2,1)S(1)} custom-call(bf16[8192,1792]{1,0:T(8,128)(2,1)} %gate_ref.1, bf16[16,8192]{1,0:T(8,128)(2,1)S(1)} %pad_maximum_fusion.1.refs_0_), custom_call_target="tpu_custom_call" | custom-call | bytes 3670016 | tf_op jit(solution)/shard_map/pallas_call | solution.py:56
  16.9 0.1 broadcast_select_fusion.1
  17.0 14.5 %shard_map.58 = bf16[32,1792]{1,0:T(8,128)(2,1)S(1)} custom-call(bf16[32,8192]{1,0:T(8,128)(2,1)S(1)} %pad_maximum_fusion.x_ref, bf16[256,256]{1,0:T(8,128)(2,1)S(1)} %copy-done, bf16[8192,1792]{1,0:T(8,128)(2,1)} %gate_ref.1, bf16[8192,1792]{1,0:T(8,128)(2,1)} %up_ref.1, bf16[1024,1792]{1,0:T(8,128)(2,1)S(1)} %shard_map.55.refs_0_, ...), custom_call_target="tpu_custom_call" | custom-call | flops 1879048192 | bytes 42205184 | tf_op jit(solution)/shard_map/pallas_call | solution.py:142
  31.5 0.6 collective-permute-start.5
  32.0 1.0 %collective-permute-done.5 = bf16[32,1792]{1,0:T(8,128)(2,1)S(1)} collective-permute-done((bf16[32,1792]{1,0:T(8,128)(2,1)S(1)}, bf16[32,1792]{1,0:T(8,128)(2,1)S(1)}, u32[]{:S(2)}, u32[]{:S(2)}) %collective-permute-start.5) | collective-permute-done | bytes 114720 | tf_op jit(solution)/shard_map/ppermute | solution.py:32
  33.0 2.9 %collective-permute-start.6 = (bf16[32,1792]{1,0:T(8,128)(2,1)S(1)}, bf16[32,1792]{1,0:T(8,128)(2,1)S(1)}, u32[]{:S(2)}, u32[]{:S(2)}) collective-permute-start(bf16[32,1792]{1,0:T(8,128)(2,1)S(1)} %fusion.1.refs_0_), channel_id=1, source_target_pairs={{0,8},{1,9},{2,10},{3,11},{4,12},{5,13},{6,14},{7,15},{8,0},{9,1},... | collective-permute-start | bytes 344072 | tf_op jit(solution)/shard_map/ppermute | solution.py:32
  35.9 4.6 %shard_map.59.refs_0_ = bf16[768,8192]{1,0:T(8,128)(2,1)S(1)} custom-call(bf16[1792,8192]{1,0:T(8,128)(2,1)} %weight_ref.11, bf16[32,1792]{1,0:T(8,128)(2,1)S(1)} %fusion.1.refs_0_), custom_call_target="tpu_custom_call" | custom-call | bytes 25165824 | tf_op jit(solution)/shard_map/pallas_call | solution.py:56
  40.5 1.5 %collective-permute-done.6 = bf16[32,1792]{1,0:T(8,128)(2,1)S(1)} collective-permute-done((bf16[32,1792]{1,0:T(8,128)(2,1)S(1)}, bf16[32,1792]{1,0:T(8,128)(2,1)S(1)}, u32[]{:S(2)}, u32[]{:S(2)}) %collective-permute-start.6) | collective-permute-done | bytes 114720 | tf_op jit(solution)/shard_map/ppermute | solution.py:32
  42.1 1.0 %collective-permute-start.9 = (bf16[32,1792]{1,0:T(8,128)(2,1)S(1)}, bf16[32,1792]{1,0:T(8,128)(2,1)S(1)}, u32[]{:S(2)}, u32[]{:S(2)}) collective-permute-start(bf16[32,1792]{1,0:T(8,128)(2,1)S(1)} %fusion.3.refs_0_), channel_id=1, source_target_pairs={{0,6},{1,7},{2,4},{3,5},{4,2},{5,3},{6,0},{7,1},{8,14},{9,15},{10,... | collective-permute-start | bytes 344072 | tf_op jit(solution)/shard_map/ppermute | solution.py:32
  43.1 1.6 %collective-permute-start.8 = (bf16[32,1792]{1,0:T(8,128)(2,1)S(1)}, bf16[32,1792]{1,0:T(8,128)(2,1)S(1)}, u32[]{:S(2)}, u32[]{:S(2)}) collective-permute-start(bf16[32,1792]{1,0:T(8,128)(2,1)S(1)} %fusion.3.refs_0_), channel_id=1, source_target_pairs={{0,4},{1,5},{2,6},{3,7},{4,0},{5,1},{6,2},{7,3},{8,12},{9,13},{10,... | collective-permute-start | bytes 344072 | tf_op jit(solution)/shard_map/ppermute | solution.py:32
  44.6 1.0 %collective-permute-start.7 = (bf16[32,1792]{1,0:T(8,128)(2,1)S(1)}, bf16[32,1792]{1,0:T(8,128)(2,1)S(1)}, u32[]{:S(2)}, u32[]{:S(2)}) collective-permute-start(bf16[32,1792]{1,0:T(8,128)(2,1)S(1)} %fusion.3.refs_0_), channel_id=1, source_target_pairs={{0,2},{1,3},{2,0},{3,1},{4,6},{5,7},{6,4},{7,5},{8,10},{9,11},{10,... | collective-permute-start | bytes 344072 | tf_op jit(solution)/shard_map/ppermute | solution.py:32
  45.7 4.6 %shard_map.60.refs_1_ = bf16[768,8192]{1,0:T(8,128)(2,1)S(1)} custom-call(bf16[1792,8192]{1,0:T(8,128)(2,1)} %weight_ref.11, bf16[32,1792]{1,0:T(8,128)(2,1)S(1)} %fusion.3.refs_0_), custom_call_target="tpu_custom_call" | custom-call | bytes 25165824 | tf_op jit(solution)/shard_map/pallas_call | solution.py:56
  50.3 0.0 collective-permute-done.8
  50.3 0.1 collective-permute-done.7
  50.4 0.1 fusion.8.rotated_ref
  50.5 5.1 %shard_map.61 = (f32[16,8192]{1,0:T(8,128)S(1)}, bf16[16,8192]{1,0:T(8,128)(2,1)S(1)}) custom-call(bf16[32,1792]{1,0:T(8,128)(2,1)S(1)} %fusion.8.rotated_ref, bf16[1792,8192]{1,0:T(8,128)(2,1)} %weight_ref.11, bf16[768,8192]{1,0:T(8,128)(2,1)S(1)} %shard_map.59.refs_0_, bf16[768,8192]{1,0:T(8,128)(2,1)S(1)} %shard_map.60.refs_1_), custom_call_target="tpu_custom_call" | custom-call | flops 939524096 | bytes 4194304 | tf_op jit(solution)/shard_map/pallas_call | solution.py:218
  55.6 0.1 collective-permute-start.10
  55.7 1.5 %collective-permute-done.10 = bf16[16,8192]{1,0:T(8,128)(2,1)S(1)} collective-permute-done((bf16[16,8192]{1,0:T(8,128)(2,1)S(1)}, bf16[16,8192]{1,0:T(8,128)(2,1)S(1)}, u32[]{:S(2)}, u32[]{:S(2)}) %collective-permute-start.10) | collective-permute-done | bytes 262176 | tf_op jit(solution)/shard_map/ppermute | solution.py:32
  57.2 0.1 convert_add_fusion
  57.3 0.1 reshape.27
  57.4 0.1 fusion.11
  57.6 1.0 %collective-permute-start.11 = (bf16[4,8192]{1,0:T(4,128)(2,1)S(1)}, bf16[4,8192]{1,0:T(4,128)(2,1)S(1)}, u32[]{:S(2)}, u32[]{:S(2)}) collective-permute-start(bf16[4,8192]{1,0:T(4,128)(2,1)S(1)} %get-tuple-element.49), channel_id=1, source_target_pairs={{0,2},{1,3},{2,0},{3,1},{4,6},{5,7},{6,4},{7,5},{8,10},{9,11},{10,... | collective-permute-start | bytes 196616 | tf_op jit(solution)/shard_map/ppermute | solution.py:32
  58.6 0.8 %collective-permute-start.12 = (bf16[4,8192]{1,0:T(4,128)(2,1)S(1)}, bf16[4,8192]{1,0:T(4,128)(2,1)S(1)}, u32[]{:S(2)}, u32[]{:S(2)}) collective-permute-start(bf16[4,8192]{1,0:T(4,128)(2,1)S(1)} %get-tuple-element.50), channel_id=1, source_target_pairs={{0,4},{1,5},{2,6},{3,7},{4,0},{5,1},{6,2},{7,3},{8,12},{9,13},{10,... | collective-permute-start | bytes 196616 | tf_op jit(solution)/shard_map/ppermute | solution.py:32
  59.3 1.8 %collective-permute-start.13 = (bf16[4,8192]{1,0:T(4,128)(2,1)S(1)}, bf16[4,8192]{1,0:T(4,128)(2,1)S(1)}, u32[]{:S(2)}, u32[]{:S(2)}) collective-permute-start(bf16[4,8192]{1,0:T(4,128)(2,1)S(1)} %get-tuple-element.51), channel_id=1, source_target_pairs={{0,6},{1,7},{2,4},{3,5},{4,2},{5,3},{6,0},{7,1},{8,14},{9,15},{10,... | collective-permute-start | bytes 196616 | tf_op jit(solution)/shard_map/ppermute | solution.py:32
  61.1 0.8 %collective-permute-done.11 = bf16[4,8192]{1,0:T(4,128)(2,1)S(1)} collective-permute-done((bf16[4,8192]{1,0:T(4,128)(2,1)S(1)}, bf16[4,8192]{1,0:T(4,128)(2,1)S(1)}, u32[]{:S(2)}, u32[]{:S(2)}) %collective-permute-start.11) | collective-permute-done | bytes 65568 | tf_op jit(solution)/shard_map/ppermute | solution.py:32
  61.9 1.2 %collective-permute-done.12 = bf16[4,8192]{1,0:T(4,128)(2,1)S(1)} collective-permute-done((bf16[4,8192]{1,0:T(4,128)(2,1)S(1)}, bf16[4,8192]{1,0:T(4,128)(2,1)S(1)}, u32[]{:S(2)}, u32[]{:S(2)}) %collective-permute-start.12) | collective-permute-done | bytes 65568 | tf_op jit(solution)/shard_map/ppermute | solution.py:32
  63.1 1.4 %collective-permute-done.13 = bf16[4,8192]{1,0:T(4,128)(2,1)S(1)} collective-permute-done((bf16[4,8192]{1,0:T(4,128)(2,1)S(1)}, bf16[4,8192]{1,0:T(4,128)(2,1)S(1)}, u32[]{:S(2)}, u32[]{:S(2)}) %collective-permute-start.13) | collective-permute-done | bytes 65568 | tf_op jit(solution)/shard_map/ppermute | solution.py:32
  64.5 0.1 fusion.10
  64.6 0.1 select_convert_fusion.3
  64.7 3.4 %collective-permute-start.14 = (bf16[2,8192]{1,0:T(2,128)(2,1)S(1)}, bf16[2,8192]{1,0:T(2,128)(2,1)S(1)}, u32[]{:S(2)}, u32[]{:S(2)}) collective-permute-start(bf16[2,8192]{1,0:T(2,128)(2,1)S(1)} %select_convert_fusion.3), channel_id=1, source_target_pairs={{0,8},{1,9},{2,10},{3,11},{4,12},{5,13},{6,14},{7,15},{8,0},{9,1},... | collective-permute-start | bytes 98312 | tf_op jit(solution)/shard_map/ppermute | solution.py:32
  68.1 2.2 %collective-permute-done.14 = bf16[2,8192]{1,0:T(2,128)(2,1)S(1)} collective-permute-done((bf16[2,8192]{1,0:T(2,128)(2,1)S(1)}, bf16[2,8192]{1,0:T(2,128)(2,1)S(1)}, u32[]{:S(2)}, u32[]{:S(2)}) %collective-permute-start.14) | collective-permute-done | bytes 32800 | tf_op jit(solution)/shard_map/ppermute | solution.py:32
  70.4 0.7 add_convert_fusion
  (8 shorter events, 0.1 us)
Async XLA Ops:
  0.0 6.6 %copy-start.1 = (bf16[2,8192]{1,0:T(2,128)(2,1)S(1)}, bf16[2,8192]{1,0:T(2,128)(2,1)}, u32[]{:S(2)}) copy-start(bf16[2,8192]{1,0:T(2,128)(2,1)} %param.5) | copy-start | bytes 98308
  0.0 6.6 %collective-permute-start = (bf16[2,8192]{1,0:T(2,128)(2,1)}, bf16[2,8192]{1,0:T(2,128)(2,1)S(1)}, u32[]{:S(2)}, u32[]{:S(2)}) collective-permute-start(bf16[2,8192]{1,0:T(2,128)(2,1)} %param.5), channel_id=1, source_target_pairs={{0,8},{1,9},{2,10},{3,11},{4,12},{5,13},{6,14},{7,15},{8,0},{9,1},... | collective-permute-start | bytes 98312 | tf_op jit(solution)/shard_map/ppermute | solution.py:32
  6.7 7.7 %collective-permute-start.3 = (bf16[4,8192]{1,0:T(4,128)(2,1)S(1)}, bf16[4,8192]{1,0:T(4,128)(2,1)S(1)}, u32[]{:S(2)}, u32[]{:S(2)}) collective-permute-start(bf16[4,8192]{1,0:T(4,128)(2,1)S(1)} %pad_maximum_fusion.2.refs_0_), channel_id=1, source_target_pairs={{0,2},{1,3},{2,0},{3,1},{4,6},{5,7},{6,4},{7,5},{8,10},{9,11},{10,... | collective-permute-start | bytes 196616 | tf_op jit(solution)/shard_map/ppermute | solution.py:32
  8.5 6.0 %collective-permute-start.2 = (bf16[4,8192]{1,0:T(4,128)(2,1)S(1)}, bf16[4,8192]{1,0:T(4,128)(2,1)S(1)}, u32[]{:S(2)}, u32[]{:S(2)}) collective-permute-start(bf16[4,8192]{1,0:T(4,128)(2,1)S(1)} %pad_maximum_fusion.2.refs_0_), channel_id=1, source_target_pairs={{0,4},{1,5},{2,6},{3,7},{4,0},{5,1},{6,2},{7,3},{8,12},{9,13},{10,... | collective-permute-start | bytes 196616 | tf_op jit(solution)/shard_map/ppermute | solution.py:32
  9.8 5.2 %collective-permute-start.1 = (bf16[4,8192]{1,0:T(4,128)(2,1)S(1)}, bf16[4,8192]{1,0:T(4,128)(2,1)S(1)}, u32[]{:S(2)}, u32[]{:S(2)}) collective-permute-start(bf16[4,8192]{1,0:T(4,128)(2,1)S(1)} %pad_maximum_fusion.2.refs_0_), channel_id=1, source_target_pairs={{0,6},{1,7},{2,4},{3,5},{4,2},{5,3},{6,0},{7,1},{8,14},{9,15},{10,... | collective-permute-start | bytes 196616 | tf_op jit(solution)/shard_map/ppermute | solution.py:32
  15.3 1.7 %copy-start = (bf16[256,256]{1,0:T(8,128)(2,1)S(1)}, bf16[256,256]{1,0:T(8,128)(2,1)}, u32[]{:S(2)}) copy-start(bf16[256,256]{1,0:T(8,128)(2,1)} %constant.6.clone.spread_ref) | copy-start | bytes 393220
  15.3 1.6 %collective-permute-start.4 = (bf16[16,8192]{1,0:T(8,128)(2,1)S(1)}, bf16[16,8192]{1,0:T(8,128)(2,1)S(1)}, u32[]{:S(2)}, u32[]{:S(2)}) collective-permute-start(bf16[16,8192]{1,0:T(8,128)(2,1)S(1)} %pad_maximum_fusion.1.refs_0_), channel_id=1, source_target_pairs={{0,1},{1,0},{2,3},{3,2},{4,5},{5,4},{6,7},{7,6},{8,9},{9,8},{10,11... | collective-permute-start | bytes 786440 | tf_op jit(solution)/shard_map/ppermute | solution.py:32
  31.5 1.5 %collective-permute-start.5 = (bf16[32,1792]{1,0:T(8,128)(2,1)S(1)}, bf16[32,1792]{1,0:T(8,128)(2,1)S(1)}, u32[]{:S(2)}, u32[]{:S(2)}) collective-permute-start(bf16[32,1792]{1,0:T(8,128)(2,1)S(1)} %shard_map.58), channel_id=1, source_target_pairs={{0,1},{1,0},{2,3},{3,2},{4,5},{5,4},{6,7},{7,6},{8,9},{9,8},{10,11... | collective-permute-start | bytes 344072 | tf_op jit(solution)/shard_map/ppermute | solution.py:32
  33.0 9.0 %collective-permute-start.6 = (bf16[32,1792]{1,0:T(8,128)(2,1)S(1)}, bf16[32,1792]{1,0:T(8,128)(2,1)S(1)}, u32[]{:S(2)}, u32[]{:S(2)}) collective-permute-start(bf16[32,1792]{1,0:T(8,128)(2,1)S(1)} %fusion.1.refs_0_), channel_id=1, source_target_pairs={{0,8},{1,9},{2,10},{3,11},{4,12},{5,13},{6,14},{7,15},{8,0},{9,1},... | collective-permute-start | bytes 344072 | tf_op jit(solution)/shard_map/ppermute | solution.py:32
  42.1 8.1 %collective-permute-start.9 = (bf16[32,1792]{1,0:T(8,128)(2,1)S(1)}, bf16[32,1792]{1,0:T(8,128)(2,1)S(1)}, u32[]{:S(2)}, u32[]{:S(2)}) collective-permute-start(bf16[32,1792]{1,0:T(8,128)(2,1)S(1)} %fusion.3.refs_0_), channel_id=1, source_target_pairs={{0,6},{1,7},{2,4},{3,5},{4,2},{5,3},{6,0},{7,1},{8,14},{9,15},{10,... | collective-permute-start | bytes 344072 | tf_op jit(solution)/shard_map/ppermute | solution.py:32
  43.1 7.2 %collective-permute-start.8 = (bf16[32,1792]{1,0:T(8,128)(2,1)S(1)}, bf16[32,1792]{1,0:T(8,128)(2,1)S(1)}, u32[]{:S(2)}, u32[]{:S(2)}) collective-permute-start(bf16[32,1792]{1,0:T(8,128)(2,1)S(1)} %fusion.3.refs_0_), channel_id=1, source_target_pairs={{0,4},{1,5},{2,6},{3,7},{4,0},{5,1},{6,2},{7,3},{8,12},{9,13},{10,... | collective-permute-start | bytes 344072 | tf_op jit(solution)/shard_map/ppermute | solution.py:32
  44.6 5.7 %collective-permute-start.7 = (bf16[32,1792]{1,0:T(8,128)(2,1)S(1)}, bf16[32,1792]{1,0:T(8,128)(2,1)S(1)}, u32[]{:S(2)}, u32[]{:S(2)}) collective-permute-start(bf16[32,1792]{1,0:T(8,128)(2,1)S(1)} %fusion.3.refs_0_), channel_id=1, source_target_pairs={{0,2},{1,3},{2,0},{3,1},{4,6},{5,7},{6,4},{7,5},{8,10},{9,11},{10,... | collective-permute-start | bytes 344072 | tf_op jit(solution)/shard_map/ppermute | solution.py:32
  55.6 1.6 %collective-permute-start.10 = (bf16[16,8192]{1,0:T(8,128)(2,1)S(1)}, bf16[16,8192]{1,0:T(8,128)(2,1)S(1)}, u32[]{:S(2)}, u32[]{:S(2)}) collective-permute-start(bf16[16,8192]{1,0:T(8,128)(2,1)S(1)} %get-tuple-element.48), channel_id=1, source_target_pairs={{0,1},{1,0},{2,3},{3,2},{4,5},{5,4},{6,7},{7,6},{8,9},{9,8},{10,11... | collective-permute-start | bytes 786440 | tf_op jit(solution)/shard_map/ppermute | solution.py:32
  57.6 4.3 %collective-permute-start.11 = (bf16[4,8192]{1,0:T(4,128)(2,1)S(1)}, bf16[4,8192]{1,0:T(4,128)(2,1)S(1)}, u32[]{:S(2)}, u32[]{:S(2)}) collective-permute-start(bf16[4,8192]{1,0:T(4,128)(2,1)S(1)} %get-tuple-element.49), channel_id=1, source_target_pairs={{0,2},{1,3},{2,0},{3,1},{4,6},{5,7},{6,4},{7,5},{8,10},{9,11},{10,... | collective-permute-start | bytes 196616 | tf_op jit(solution)/shard_map/ppermute | solution.py:32
  58.6 4.6 %collective-permute-start.12 = (bf16[4,8192]{1,0:T(4,128)(2,1)S(1)}, bf16[4,8192]{1,0:T(4,128)(2,1)S(1)}, u32[]{:S(2)}, u32[]{:S(2)}) collective-permute-start(bf16[4,8192]{1,0:T(4,128)(2,1)S(1)} %get-tuple-element.50), channel_id=1, source_target_pairs={{0,4},{1,5},{2,6},{3,7},{4,0},{5,1},{6,2},{7,3},{8,12},{9,13},{10,... | collective-permute-start | bytes 196616 | tf_op jit(solution)/shard_map/ppermute | solution.py:32
  59.3 5.2 %collective-permute-start.13 = (bf16[4,8192]{1,0:T(4,128)(2,1)S(1)}, bf16[4,8192]{1,0:T(4,128)(2,1)S(1)}, u32[]{:S(2)}, u32[]{:S(2)}) collective-permute-start(bf16[4,8192]{1,0:T(4,128)(2,1)S(1)} %get-tuple-element.51), channel_id=1, source_target_pairs={{0,6},{1,7},{2,4},{3,5},{4,2},{5,3},{6,0},{7,1},{8,14},{9,15},{10,... | collective-permute-start | bytes 196616 | tf_op jit(solution)/shard_map/ppermute | solution.py:32
  64.7 5.7 %collective-permute-start.14 = (bf16[2,8192]{1,0:T(2,128)(2,1)S(1)}, bf16[2,8192]{1,0:T(2,128)(2,1)S(1)}, u32[]{:S(2)}, u32[]{:S(2)}) collective-permute-start(bf16[2,8192]{1,0:T(2,128)(2,1)S(1)} %select_convert_fusion.3), channel_id=1, source_target_pairs={{0,8},{1,9},{2,10},{3,11},{4,12},{5,13},{6,14},{7,15},{8,0},{9,1},... | collective-permute-start | bytes 98312 | tf_op jit(solution)/shard_map/ppermute | solution.py:32

commit v5 on v4

--- a/solution.py
+++ b/solution.py
@@ -13,9 +13,9 @@
 MIB = 2**20
 VMEM = pl.BlockSpec(memory_space=pltpu.VMEM)
 ANY = pl.BlockSpec(memory_space=pl.ANY)
-GATHER_BYTES = (4 * MIB, 12 * MIB, 3 * MIB)
+GATHER_BYTES = (0 * MIB, 6 * MIB, 0 * MIB)
 HADAMARD_BYTES = (0, 12 * MIB, 12 * MIB)
-SLOTS = 5
+SLOTS = 4
 
 
 def walsh(order):
@@ -90,7 +90,7 @@
     count = len(pieces)
     chunks = [
         (which, first, min(chunk, depth - first))
-        for which, begin in ((0, fetched.rows), (1, 0))
+        for which, begin in ((0, fetched.rows),)
         for first in range(begin, depth, chunk)
     ]
     slots = min(SLOTS, len(chunks))
@@ -125,6 +125,7 @@
         for ref in piece_refs:
             add(gate_acc, first, ref.shape[0], ref)
             first += ref.shape[0]
+        add(up_acc, 0, depth, up_ref)
         for i, (which, first, rows) in enumerate(chunks):
             copy(i).wait()
             add((gate_acc, up_acc)[which], first, rows, buffer.at[i % slots])
@@ -142,7 +143,7 @@
     return pl.pallas_call(
         kernel,
         out_shape=jax.ShapeDtypeStruct((tokens, width), jnp.bfloat16),
-        in_specs=[VMEM, VMEM, ANY, ANY] + [VMEM] * count,
+        in_specs=[VMEM, VMEM, ANY, VMEM] + [VMEM] * count,
         out_specs=VMEM,
         scratch_shapes=[
             pltpu.VMEM((tokens, width), jnp.float32),
@@ -162,7 +163,7 @@
         x,
         jnp.asarray(spread, jnp.bfloat16),
         in_hbm(gate),
-        in_hbm(up),
+        in_vmem(up),
         *[in_vmem(piece) for piece in pieces],
     )
 
@@ -302,7 +303,7 @@
             rows.append(pick({xor(slot, flips): v for flips, v in got.items()}, bits))
         piece = jnp.concatenate(rows, axis=0)
 
-    local = gate_up(piece, gate_weight, up_weight, gate_rows, 3 * gate_chunk)
+    local = gate_up(piece, gate_weight, up_weight, gate_rows, 2 * gate_chunk)
 
     down_chunk = divisor(width, 256, 16)
     down_rows = Fetched(down_weight, down_chunk, width - down_chunk)

time: 71.3 us -> 68.3 us (0.958)
  Pallas kernels: 36.5 us -> 27.8 us
  waiting for transfers between devices: 10.7 us -> 16.4 us
  other arithmetic: 1.74 us -> 3.41 us
  starting transfers between devices: 21.7 us -> 20.1 us
    ppermute x15, waiting for transfers between devices: 10.7 us -> 16.4 us  [swapped(): return lax.ppermute(value, 'tensor', pairs)]
    pallas_call x5 -> x3, Pallas kernels: 16.9 us -> 11.7 us  [fetch(): pl.pallas_call(kernel, out_shape=jax.ShapeDtypeStruct((rows, width), weig...]
    pallas_call x1, Pallas kernels: 14.5 us -> 10.9 us  [gate_up(): pl.pallas_call(kernel, out_shape=jax.ShapeDtypeStruct((tokens, width), jn...]
    select_n x3, other arithmetic: 0.26 us -> 1.93 us  [pick(): return jnp.where(bits[0], one, zero)]
    ppermute x15, starting transfers between devices: 21.7 us -> 20.1 us  [swapped(): return lax.ppermute(value, 'tensor', pairs)]
  transfers between devices with their start and end apart: 15 -> 15, of which waited for: 10 -> 11; matrix products, arithmetic and copies ran while one was open for 0% -> 0% of each run, Pallas kernels for 24% -> 17%
where the time goes in v5:
time: 68.3 us; the launch traced here: 68 us
  Pallas kernels  27.8 us (41%)
  starting transfers between devices  20.1 us (29%)
  waiting for transfers between devices  16.4 us (24%)
  other arithmetic  3.41 us (5%)
    ppermute x15, starting transfers between devices, swapped(): return lax.ppermute(value, 'tensor', pairs)  20.1 us
    ppermute x15, waiting for transfers between devices, swapped(): return lax.ppermute(value, 'tensor', pairs)  16.4 us
    pallas_call x3, Pallas kernels, fetch(): pl.pallas_call(kernel, out_shape=jax.ShapeDtypeStruct((rows, width), weig...  11.7 us
    pallas_call x1, Pallas kernels, gate_up(): pl.pallas_call(kernel, out_shape=jax.ShapeDtypeStruct((tokens, width), jn...  10.9 us
    pallas_call x1, Pallas kernels, down(): pl.pallas_call(kernel, out_shape=(jax.ShapeDtypeStruct((half, width), jnp...  5.14 us
    select_n x3, other arithmetic, pick(): return jnp.where(bits[0], one, zero)  1.93 us
  transfers between devices with their start and end apart: 15, of which 11 were waited for; matrix products, arithmetic and copies ran while one was open for 0% of the time, Pallas kernels for 17%

profile of v5, /device:TPU:0, one launch (start us, length us, event | category | flops | bytes accessed | tf_op | source)
XLA Modules:
  0.0 68.0 jit_solution(11314865002181763597)
XLA Ops:
  0.0 4.0 %collective-permute-start = (bf16[2,8192]{1,0:T(2,128)(2,1)}, bf16[2,8192]{1,0:T(2,128)(2,1)S(1)}, u32[]{:S(2)}, u32[]{:S(2)}) collective-permute-start(bf16[2,8192]{1,0:T(2,128)(2,1)} %param.5), channel_id=1, source_target_pairs={{0,8},{1,9},{2,10},{3,11},{4,12},{5,13},{6,14},{7,15},{8,0},{9,1},... | collective-permute-start | bytes 98312 | tf_op jit(solution)/shard_map/ppermute | solution.py:32
  4.0 2.5 %collective-permute-done = bf16[2,8192]{1,0:T(2,128)(2,1)S(1)} collective-permute-done((bf16[2,8192]{1,0:T(2,128)(2,1)}, bf16[2,8192]{1,0:T(2,128)(2,1)S(1)}, u32[]{:S(2)}, u32[]{:S(2)}) %collective-permute-start) | collective-permute-done | bytes 32800 | tf_op jit(solution)/shard_map/ppermute | solution.py:32
  6.5 1.6 %broadcast_select_fusion.11 = (bf16[2,8192]{1,0:T(2,128)(2,1)S(1)}, bf16[2,8192]{1,0:T(2,128)(2,1)S(1)}) fusion(bf16[2,8192]{1,0:T(2,128)(2,1)S(1)} %collective-permute-done, bf16[2,8192]{1,0:T(2,128)(2,1)} %param.5, pred[]{:T(512)S(6)} %eq.15), kind=kLoop, calls=%fused_computation.44 | loop fusion | flops 32768 | bytes 131073 | tf_op jit(solution)/shard_map/jit(_where)/select_n | solution.py:256
  8.1 0.1 pad_maximum_fusion.2.refs_0_
  8.1 1.8 %collective-permute-start.3 = (bf16[4,8192]{1,0:T(4,128)(2,1)S(1)}, bf16[4,8192]{1,0:T(4,128)(2,1)S(1)}, u32[]{:S(2)}, u32[]{:S(2)}) collective-permute-start(bf16[4,8192]{1,0:T(4,128)(2,1)S(1)} %pad_maximum_fusion.2.refs_0_), channel_id=1, source_target_pairs={{0,2},{1,3},{2,0},{3,1},{4,6},{5,7},{6,4},{7,5},{8,10},{9,11},{10,... | collective-permute-start | bytes 196616 | tf_op jit(solution)/shard_map/ppermute | solution.py:32
  9.9 1.3 %collective-permute-start.2 = (bf16[4,8192]{1,0:T(4,128)(2,1)S(1)}, bf16[4,8192]{1,0:T(4,128)(2,1)S(1)}, u32[]{:S(2)}, u32[]{:S(2)}) collective-permute-start(bf16[4,8192]{1,0:T(4,128)(2,1)S(1)} %pad_maximum_fusion.2.refs_0_), channel_id=1, source_target_pairs={{0,4},{1,5},{2,6},{3,7},{4,0},{5,1},{6,2},{7,3},{8,12},{9,13},{10,... | collective-permute-start | bytes 196616 | tf_op jit(solution)/shard_map/ppermute | solution.py:32
  11.3 0.4 collective-permute-start.1
  11.7 2.6 %shard_map.55.refs_0_ = bf16[1536,1792]{1,0:T(8,128)(2,1)S(1)} custom-call(bf16[8192,1792]{1,0:T(8,128)(2,1)} %gate_ref.1, bf16[4,8192]{1,0:T(4,128)(2,1)S(1)} %pad_maximum_fusion.2.refs_0_), custom_call_target="tpu_custom_call" | custom-call | bytes 11010048 | tf_op jit(solution)/shard_map/pallas_call | solution.py:56
  14.3 0.0 collective-permute-done.3
  14.3 0.0 collective-permute-done.2
  14.3 2.2 %collective-permute-done.1 = bf16[4,8192]{1,0:T(4,128)(2,1)S(1)} collective-permute-done((bf16[4,8192]{1,0:T(4,128)(2,1)S(1)}, bf16[4,8192]{1,0:T(4,128)(2,1)S(1)}, u32[]{:S(2)}, u32[]{:S(2)}) %collective-permute-start.1) | collective-permute-done | bytes 65568 | tf_op jit(solution)/shard_map/ppermute | solution.py:32
  16.5 0.1 broadcast_select_fusion.9
  16.6 0.2 pad_maximum_fusion.1
  16.8 0.1 collective-permute-start.4
  16.8 1.5 %collective-permute-done.4 = bf16[16,8192]{1,0:T(8,128)(2,1)S(1)} collective-permute-done((bf16[16,8192]{1,0:T(8,128)(2,1)S(1)}, bf16[16,8192]{1,0:T(8,128)(2,1)S(1)}, u32[]{:S(2)}, u32[]{:S(2)}) %collective-permute-start.4) | collective-permute-done | bytes 262176 | tf_op jit(solution)/shard_map/ppermute | solution.py:32
  18.4 0.2 broadcast_select_fusion.1
  18.6 0.0 copy-done
  18.6 10.9 %shard_map.56 = bf16[32,1792]{1,0:T(8,128)(2,1)S(1)} custom-call(bf16[32,8192]{1,0:T(8,128)(2,1)S(1)} %pad_maximum_fusion.x_ref, bf16[256,256]{1,0:T(8,128)(2,1)S(1)} %copy-done.1, bf16[8192,1792]{1,0:T(8,128)(2,1)} %gate_ref.1, bf16[8192,1792]{1,0:T(8,128)(2,1)S(1)} %copy-done, bf16[1536,1792]{1,0:T(8,128)(2,1)S(1)} %shard_map.55.refs_0_), custom_call_target="tpu_custom_call" | custom-call | flops 1879048192 | bytes 23855104 | tf_op jit(solution)/shard_map/pallas_call | solution.py:143
  29.6 0.2 collective-permute-start.5
  29.8 1.2 %collective-permute-done.5 = bf16[32,1792]{1,0:T(8,128)(2,1)S(1)} collective-permute-done((bf16[32,1792]{1,0:T(8,128)(2,1)S(1)}, bf16[32,1792]{1,0:T(8,128)(2,1)S(1)}, u32[]{:S(2)}, u32[]{:S(2)}) %collective-permute-start.5) | collective-permute-done | bytes 114720 | tf_op jit(solution)/shard_map/ppermute | solution.py:32
  31.0 2.9 %collective-permute-start.6 = (bf16[32,1792]{1,0:T(8,128)(2,1)S(1)}, bf16[32,1792]{1,0:T(8,128)(2,1)S(1)}, u32[]{:S(2)}, u32[]{:S(2)}) collective-permute-start(bf16[32,1792]{1,0:T(8,128)(2,1)S(1)} %fusion.1.refs_0_), channel_id=1, source_target_pairs={{0,8},{1,9},{2,10},{3,11},{4,12},{5,13},{6,14},{7,15},{8,0},{9,1},... | collective-permute-start | bytes 344072 | tf_op jit(solution)/shard_map/ppermute | solution.py:32
  33.9 4.6 %shard_map.57.refs_0_ = bf16[768,8192]{1,0:T(8,128)(2,1)S(1)} custom-call(bf16[1792,8192]{1,0:T(8,128)(2,1)} %weight_ref.7, bf16[32,1792]{1,0:T(8,128)(2,1)S(1)} %fusion.1.refs_0_), custom_call_target="tpu_custom_call" | custom-call | bytes 25165824 | tf_op jit(solution)/shard_map/pallas_call | solution.py:56
  38.5 1.3 %collective-permute-done.6 = bf16[32,1792]{1,0:T(8,128)(2,1)S(1)} collective-permute-done((bf16[32,1792]{1,0:T(8,128)(2,1)S(1)}, bf16[32,1792]{1,0:T(8,128)(2,1)S(1)}, u32[]{:S(2)}, u32[]{:S(2)}) %collective-permute-start.6) | collective-permute-done | bytes 114720 | tf_op jit(solution)/shard_map/ppermute | solution.py:32
  39.8 0.1 collective-permute-start.9
  39.9 2.0 %collective-permute-start.8 = (bf16[32,1792]{1,0:T(8,128)(2,1)S(1)}, bf16[32,1792]{1,0:T(8,128)(2,1)S(1)}, u32[]{:S(2)}, u32[]{:S(2)}) collective-permute-start(bf16[32,1792]{1,0:T(8,128)(2,1)S(1)} %fusion.3.refs_0_), channel_id=1, source_target_pairs={{0,4},{1,5},{2,6},{3,7},{4,0},{5,1},{6,2},{7,3},{8,12},{9,13},{10,... | collective-permute-start | bytes 344072 | tf_op jit(solution)/shard_map/ppermute | solution.py:32
  41.9 1.4 %collective-permute-start.7 = (bf16[32,1792]{1,0:T(8,128)(2,1)S(1)}, bf16[32,1792]{1,0:T(8,128)(2,1)S(1)}, u32[]{:S(2)}, u32[]{:S(2)}) collective-permute-start(bf16[32,1792]{1,0:T(8,128)(2,1)S(1)} %fusion.3.refs_0_), channel_id=1, source_target_pairs={{0,2},{1,3},{2,0},{3,1},{4,6},{5,7},{6,4},{7,5},{8,10},{9,11},{10,... | collective-permute-start | bytes 344072 | tf_op jit(solution)/shard_map/ppermute | solution.py:32
  43.3 4.6 %shard_map.58.refs_1_ = bf16[768,8192]{1,0:T(8,128)(2,1)S(1)} custom-call(bf16[1792,8192]{1,0:T(8,128)(2,1)} %weight_ref.7, bf16[32,1792]{1,0:T(8,128)(2,1)S(1)} %fusion.3.refs_0_), custom_call_target="tpu_custom_call" | custom-call | bytes 25165824 | tf_op jit(solution)/shard_map/pallas_call | solution.py:56
  47.9 0.0 collective-permute-done.9
  47.9 0.0 collective-permute-done.8
  47.9 0.4 collective-permute-done.7
  48.3 0.1 fusion.8.rotated_ref
  48.4 5.1 %shard_map.59 = (f32[16,8192]{1,0:T(8,128)S(1)}, bf16[16,8192]{1,0:T(8,128)(2,1)S(1)}) custom-call(bf16[32,1792]{1,0:T(8,128)(2,1)S(1)} %fusion.8.rotated_ref, bf16[1792,8192]{1,0:T(8,128)(2,1)} %weight_ref.7, bf16[768,8192]{1,0:T(8,128)(2,1)S(1)} %shard_map.57.refs_0_, bf16[768,8192]{1,0:T(8,128)(2,1)S(1)} %shard_map.58.refs_1_), custom_call_target="tpu_custom_call" | custom-call | flops 939524096 | bytes 4194304 | tf_op jit(solution)/shard_map/pallas_call | solution.py:219
  53.6 0.1 collective-permute-start.10
  53.7 1.5 %collective-permute-done.10 = bf16[16,8192]{1,0:T(8,128)(2,1)S(1)} collective-permute-done((bf16[16,8192]{1,0:T(8,128)(2,1)S(1)}, bf16[16,8192]{1,0:T(8,128)(2,1)S(1)}, u32[]{:S(2)}, u32[]{:S(2)}) %collective-permute-start.10) | collective-permute-done | bytes 262176 | tf_op jit(solution)/shard_map/ppermute | solution.py:32
  55.2 0.1 convert_add_fusion
  55.2 0.1 reshape.27
  55.4 0.1 fusion.11
  55.5 0.6 collective-permute-start.11
  56.1 0.3 collective-permute-start.12
  56.4 2.6 %collective-permute-start.13 = (bf16[4,8192]{1,0:T(4,128)(2,1)S(1)}, bf16[4,8192]{1,0:T(4,128)(2,1)S(1)}, u32[]{:S(2)}, u32[]{:S(2)}) collective-permute-start(bf16[4,8192]{1,0:T(4,128)(2,1)S(1)} %get-tuple-element.43), channel_id=1, source_target_pairs={{0,6},{1,7},{2,4},{3,5},{4,2},{5,3},{6,0},{7,1},{8,14},{9,15},{10,... | collective-permute-start | bytes 196616 | tf_op jit(solution)/shard_map/ppermute | solution.py:32
  59.1 0.8 %collective-permute-done.11 = bf16[4,8192]{1,0:T(4,128)(2,1)S(1)} collective-permute-done((bf16[4,8192]{1,0:T(4,128)(2,1)S(1)}, bf16[4,8192]{1,0:T(4,128)(2,1)S(1)}, u32[]{:S(2)}, u32[]{:S(2)}) %collective-permute-start.11) | collective-permute-done | bytes 65568 | tf_op jit(solution)/shard_map/ppermute | solution.py:32
  59.8 1.1 %collective-permute-done.12 = bf16[4,8192]{1,0:T(4,128)(2,1)S(1)} collective-permute-done((bf16[4,8192]{1,0:T(4,128)(2,1)S(1)}, bf16[4,8192]{1,0:T(4,128)(2,1)S(1)}, u32[]{:S(2)}, u32[]{:S(2)}) %collective-permute-start.12) | collective-permute-done | bytes 65568 | tf_op jit(solution)/shard_map/ppermute | solution.py:32
  60.9 1.4 %collective-permute-done.13 = bf16[4,8192]{1,0:T(4,128)(2,1)S(1)} collective-permute-done((bf16[4,8192]{1,0:T(4,128)(2,1)S(1)}, bf16[4,8192]{1,0:T(4,128)(2,1)S(1)}, u32[]{:S(2)}, u32[]{:S(2)}) %collective-permute-start.13) | collective-permute-done | bytes 65568 | tf_op jit(solution)/shard_map/ppermute | solution.py:32
  62.3 0.1 fusion.10
  62.4 0.1 select_convert_fusion.3
  62.5 2.1 %collective-permute-start.14 = (bf16[2,8192]{1,0:T(2,128)(2,1)S(1)}, bf16[2,8192]{1,0:T(2,128)(2,1)S(1)}, u32[]{:S(2)}, u32[]{:S(2)}) collective-permute-start(bf16[2,8192]{1,0:T(2,128)(2,1)S(1)} %select_convert_fusion.3), channel_id=1, source_target_pairs={{0,8},{1,9},{2,10},{3,11},{4,12},{5,13},{6,14},{7,15},{8,0},{9,1},... | collective-permute-start | bytes 98312 | tf_op jit(solution)/shard_map/ppermute | solution.py:32
  64.6 2.7 %collective-permute-done.14 = bf16[2,8192]{1,0:T(2,128)(2,1)S(1)} collective-permute-done((bf16[2,8192]{1,0:T(2,128)(2,1)S(1)}, bf16[2,8192]{1,0:T(2,128)(2,1)S(1)}, u32[]{:S(2)}, u32[]{:S(2)}) %collective-permute-start.14) | collective-permute-done | bytes 32800 | tf_op jit(solution)/shard_map/ppermute | solution.py:32
  67.4 0.7 add_convert_fusion
  (6 shorter events, 0.1 us)
Async XLA Ops:
  0.0 18.6 %copy-start.1 = (bf16[256,256]{1,0:T(8,128)(2,1)S(1)}, bf16[256,256]{1,0:T(8,128)(2,1)}, u32[]{:S(2)}) copy-start(bf16[256,256]{1,0:T(8,128)(2,1)} %constant.6.clone.spread_ref) | copy-start | bytes 393220
  0.0 18.6 %copy-start = (bf16[8192,1792]{1,0:T(8,128)(2,1)S(1)}, bf16[8192,1792]{1,0:T(8,128)(2,1)}, u32[]{:S(2)}) copy-start(bf16[8192,1792]{1,0:T(8,128)(2,1)} %up_ref.1) | copy-start | bytes 88080384
  0.0 6.5 %collective-permute-start = (bf16[2,8192]{1,0:T(2,128)(2,1)}, bf16[2,8192]{1,0:T(2,128)(2,1)S(1)}, u32[]{:S(2)}, u32[]{:S(2)}) collective-permute-start(bf16[2,8192]{1,0:T(2,128)(2,1)} %param.5), channel_id=1, source_target_pairs={{0,8},{1,9},{2,10},{3,11},{4,12},{5,13},{6,14},{7,15},{8,0},{9,1},... | collective-permute-start | bytes 98312 | tf_op jit(solution)/shard_map/ppermute | solution.py:32
  8.1 6.1 %collective-permute-start.3 = (bf16[4,8192]{1,0:T(4,128)(2,1)S(1)}, bf16[4,8192]{1,0:T(4,128)(2,1)S(1)}, u32[]{:S(2)}, u32[]{:S(2)}) collective-permute-start(bf16[4,8192]{1,0:T(4,128)(2,1)S(1)} %pad_maximum_fusion.2.refs_0_), channel_id=1, source_target_pairs={{0,2},{1,3},{2,0},{3,1},{4,6},{5,7},{6,4},{7,5},{8,10},{9,11},{10,... | collective-permute-start | bytes 196616 | tf_op jit(solution)/shard_map/ppermute | solution.py:32
  9.9 4.4 %collective-permute-start.2 = (bf16[4,8192]{1,0:T(4,128)(2,1)S(1)}, bf16[4,8192]{1,0:T(4,128)(2,1)S(1)}, u32[]{:S(2)}, u32[]{:S(2)}) collective-permute-start(bf16[4,8192]{1,0:T(4,128)(2,1)S(1)} %pad_maximum_fusion.2.refs_0_), channel_id=1, source_target_pairs={{0,4},{1,5},{2,6},{3,7},{4,0},{5,1},{6,2},{7,3},{8,12},{9,13},{10,... | collective-permute-start | bytes 196616 | tf_op jit(solution)/shard_map/ppermute | solution.py:32
  11.3 5.2 %collective-permute-start.1 = (bf16[4,8192]{1,0:T(4,128)(2,1)S(1)}, bf16[4,8192]{1,0:T(4,128)(2,1)S(1)}, u32[]{:S(2)}, u32[]{:S(2)}) collective-permute-start(bf16[4,8192]{1,0:T(4,128)(2,1)S(1)} %pad_maximum_fusion.2.refs_0_), channel_id=1, source_target_pairs={{0,6},{1,7},{2,4},{3,5},{4,2},{5,3},{6,0},{7,1},{8,14},{9,15},{10,... | collective-permute-start | bytes 196616 | tf_op jit(solution)/shard_map/ppermute | solution.py:32
  16.8 1.6 %collective-permute-start.4 = (bf16[16,8192]{1,0:T(8,128)(2,1)S(1)}, bf16[16,8192]{1,0:T(8,128)(2,1)S(1)}, u32[]{:S(2)}, u32[]{:S(2)}) collective-permute-start(bf16[16,8192]{1,0:T(8,128)(2,1)S(1)} %pad_maximum_fusion.1), channel_id=1, source_target_pairs={{0,1},{1,0},{2,3},{3,2},{4,5},{5,4},{6,7},{7,6},{8,9},{9,8},{10,11... | collective-permute-start | bytes 786440 | tf_op jit(solution)/shard_map/ppermute | solution.py:32
  29.6 1.4 %collective-permute-start.5 = (bf16[32,1792]{1,0:T(8,128)(2,1)S(1)}, bf16[32,1792]{1,0:T(8,128)(2,1)S(1)}, u32[]{:S(2)}, u32[]{:S(2)}) collective-permute-start(bf16[32,1792]{1,0:T(8,128)(2,1)S(1)} %shard_map.56), channel_id=1, source_target_pairs={{0,1},{1,0},{2,3},{3,2},{4,5},{5,4},{6,7},{7,6},{8,9},{9,8},{10,11... | collective-permute-start | bytes 344072 | tf_op jit(solution)/shard_map/ppermute | solution.py:32
  31.0 8.7 %collective-permute-start.6 = (bf16[32,1792]{1,0:T(8,128)(2,1)S(1)}, bf16[32,1792]{1,0:T(8,128)(2,1)S(1)}, u32[]{:S(2)}, u32[]{:S(2)}) collective-permute-start(bf16[32,1792]{1,0:T(8,128)(2,1)S(1)} %fusion.1.refs_0_), channel_id=1, source_target_pairs={{0,8},{1,9},{2,10},{3,11},{4,12},{5,13},{6,14},{7,15},{8,0},{9,1},... | collective-permute-start | bytes 344072 | tf_op jit(solution)/shard_map/ppermute | solution.py:32
  39.8 8.1 %collective-permute-start.9 = (bf16[32,1792]{1,0:T(8,128)(2,1)S(1)}, bf16[32,1792]{1,0:T(8,128)(2,1)S(1)}, u32[]{:S(2)}, u32[]{:S(2)}) collective-permute-start(bf16[32,1792]{1,0:T(8,128)(2,1)S(1)} %fusion.3.refs_0_), channel_id=1, source_target_pairs={{0,6},{1,7},{2,4},{3,5},{4,2},{5,3},{6,0},{7,1},{8,14},{9,15},{10,... | collective-permute-start | bytes 344072 | tf_op jit(solution)/shard_map/ppermute | solution.py:32
  39.9 8.1 %collective-permute-start.8 = (bf16[32,1792]{1,0:T(8,128)(2,1)S(1)}, bf16[32,1792]{1,0:T(8,128)(2,1)S(1)}, u32[]{:S(2)}, u32[]{:S(2)}) collective-permute-start(bf16[32,1792]{1,0:T(8,128)(2,1)S(1)} %fusion.3.refs_0_), channel_id=1, source_target_pairs={{0,4},{1,5},{2,6},{3,7},{4,0},{5,1},{6,2},{7,3},{8,12},{9,13},{10,... | collective-permute-start | bytes 344072 | tf_op jit(solution)/shard_map/ppermute | solution.py:32
  41.9 6.4 %collective-permute-start.7 = (bf16[32,1792]{1,0:T(8,128)(2,1)S(1)}, bf16[32,1792]{1,0:T(8,128)(2,1)S(1)}, u32[]{:S(2)}, u32[]{:S(2)}) collective-permute-start(bf16[32,1792]{1,0:T(8,128)(2,1)S(1)} %fusion.3.refs_0_), channel_id=1, source_target_pairs={{0,2},{1,3},{2,0},{3,1},{4,6},{5,7},{6,4},{7,5},{8,10},{9,11},{10,... | collective-permute-start | bytes 344072 | tf_op jit(solution)/shard_map/ppermute | solution.py:32
  53.6 1.6 %collective-permute-start.10 = (bf16[16,8192]{1,0:T(8,128)(2,1)S(1)}, bf16[16,8192]{1,0:T(8,128)(2,1)S(1)}, u32[]{:S(2)}, u32[]{:S(2)}) collective-permute-start(bf16[16,8192]{1,0:T(8,128)(2,1)S(1)} %get-tuple-element.40), channel_id=1, source_target_pairs={{0,1},{1,0},{2,3},{3,2},{4,5},{5,4},{6,7},{7,6},{8,9},{9,8},{10,11... | collective-permute-start | bytes 786440 | tf_op jit(solution)/shard_map/ppermute | solution.py:32
  55.5 4.3 %collective-permute-start.11 = (bf16[4,8192]{1,0:T(4,128)(2,1)S(1)}, bf16[4,8192]{1,0:T(4,128)(2,1)S(1)}, u32[]{:S(2)}, u32[]{:S(2)}) collective-permute-start(bf16[4,8192]{1,0:T(4,128)(2,1)S(1)} %get-tuple-element.41), channel_id=1, source_target_pairs={{0,2},{1,3},{2,0},{3,1},{4,6},{5,7},{6,4},{7,5},{8,10},{9,11},{10,... | collective-permute-start | bytes 196616 | tf_op jit(solution)/shard_map/ppermute | solution.py:32
  56.1 4.8 %collective-permute-start.12 = (bf16[4,8192]{1,0:T(4,128)(2,1)S(1)}, bf16[4,8192]{1,0:T(4,128)(2,1)S(1)}, u32[]{:S(2)}, u32[]{:S(2)}) collective-permute-start(bf16[4,8192]{1,0:T(4,128)(2,1)S(1)} %get-tuple-element.42), channel_id=1, source_target_pairs={{0,4},{1,5},{2,6},{3,7},{4,0},{5,1},{6,2},{7,3},{8,12},{9,13},{10,... | collective-permute-start | bytes 196616 | tf_op jit(solution)/shard_map/ppermute | solution.py:32
  56.4 5.9 %collective-permute-start.13 = (bf16[4,8192]{1,0:T(4,128)(2,1)S(1)}, bf16[4,8192]{1,0:T(4,128)(2,1)S(1)}, u32[]{:S(2)}, u32[]{:S(2)}) collective-permute-start(bf16[4,8192]{1,0:T(4,128)(2,1)S(1)} %get-tuple-element.43), channel_id=1, source_target_pairs={{0,6},{1,7},{2,4},{3,5},{4,2},{5,3},{6,0},{7,1},{8,14},{9,15},{10,... | collective-permute-start | bytes 196616 | tf_op jit(solution)/shard_map/ppermute | solution.py:32
  62.5 4.9 %collective-permute-start.14 = (bf16[2,8192]{1,0:T(2,128)(2,1)S(1)}, bf16[2,8192]{1,0:T(2,128)(2,1)S(1)}, u32[]{:S(2)}, u32[]{:S(2)}) collective-permute-start(bf16[2,8192]{1,0:T(2,128)(2,1)S(1)} %select_convert_fusion.3), channel_id=1, source_target_pairs={{0,8},{1,9},{2,10},{3,11},{4,12},{5,13},{6,14},{7,15},{8,0},{9,1},... | collective-permute-start | bytes 98312 | tf_op jit(solution)/shard_map/ppermute | solution.py:32

commit v6 on v5

--- a/solution.py
+++ b/solution.py
@@ -62,6 +62,22 @@
         cost_estimate=pl.CostEstimate(flops=0, transcendentals=0, bytes_accessed=2 * size),
         compiler_params=pltpu.CompilerParams(vmem_limit_bytes=MIB),
     )(in_hbm(weight), *after)
+
+
+def in_place(value):
+    def kernel(value_ref, out_ref):
+        out_ref[...] = value_ref[...]
+
+    return pl.pallas_call(
+        kernel,
+        out_shape=jax.ShapeDtypeStruct(value.shape, value.dtype),
+        in_specs=[VMEM],
+        out_specs=VMEM,
+        cost_estimate=pl.CostEstimate(
+            flops=0, transcendentals=0, bytes_accessed=2 * value.size * value.dtype.itemsize
+        ),
+        compiler_params=pltpu.CompilerParams(vmem_limit_bytes=MIB),
+    )(value)
 
 
 class Fetched:
@@ -296,6 +312,8 @@
         for flips, mask in masks_of(combined)[1:]:
             got[flips] = swapped(piece, mask)
         size = GATHER_BYTES[number] if number < len(GATHER_BYTES) else 0
+        if not number:
+            piece = in_place(piece)
         got[(0,) * len(combined)] = gate_rows.beside(piece, size, [piece] if number else [])
         bits = [upper[level] for level in combined]
         rows = []

time: 68.3 us -> 66.7 us (0.977)
  other arithmetic: 3.41 us -> 1.89 us
  local copies, waits for them, and re-layouts: 0.16 us -> 1.67 us
  waiting for transfers between devices: 16.4 us -> 14.9 us
    select_n x3, other arithmetic: 1.93 us -> 0.41 us  [pick(): return jnp.where(bits[0], one, zero)]
    unnamed x4 -> x6, local copies, waits for them, and re-layouts: 0.01 us -> 1.52 us
    ppermute x15, waiting for transfers between devices: 16.4 us -> 14.9 us  [swapped(): return lax.ppermute(value, 'tensor', pairs)]
  transfers between devices with their start and end apart: 15 -> 15, of which waited for: 11 -> 11; matrix products, arithmetic and copies ran while one was open for 0% -> 0% of each run, Pallas kernels for 17% -> 18%
where the time goes in v6:
time: 66.7 us; the launch traced here: 66.5 us
  Pallas kernels  27.8 us (42%)
  starting transfers between devices  20.1 us (30%)
  waiting for transfers between devices  14.9 us (22%)
  other arithmetic  1.89 us (3%)
  local copies, waits for them, and re-layouts  1.67 us (3%)
    ppermute x15, starting transfers between devices, swapped(): return lax.ppermute(value, 'tensor', pairs)  20.1 us
    ppermute x15, waiting for transfers between devices, swapped(): return lax.ppermute(value, 'tensor', pairs)  14.9 us
    pallas_call x3, Pallas kernels, fetch(): pl.pallas_call(kernel, out_shape=jax.ShapeDtypeStruct((rows, width), weig...  11.7 us
    pallas_call x1, Pallas kernels, gate_up(): pl.pallas_call(kernel, out_shape=jax.ShapeDtypeStruct((tokens, width), jn...  10.9 us
    pallas_call x1, Pallas kernels, down(): pl.pallas_call(kernel, out_shape=(jax.ShapeDtypeStruct((half, width), jnp...  5.14 us
    unnamed x6, local copies, waits for them, and re-layouts  1.52 us
  transfers between devices with their start and end apart: 15, of which 11 were waited for; matrix products, arithmetic and copies ran while one was open for 0% of the time, Pallas kernels for 18%

profile of v6, /device:TPU:0, one launch (start us, length us, event | category | flops | bytes accessed | tf_op | source)
XLA Modules:
  0.0 66.5 jit_solution(11989737254843083293)
XLA Ops:
  0.0 4.0 %collective-permute-start = (bf16[2,8192]{1,0:T(2,128)(2,1)}, bf16[2,8192]{1,0:T(2,128)(2,1)S(1)}, u32[]{:S(2)}, u32[]{:S(2)}) collective-permute-start(bf16[2,8192]{1,0:T(2,128)(2,1)} %value_ref), channel_id=1, source_target_pairs={{0,8},{1,9},{2,10},{3,11},{4,12},{5,13},{6,14},{7,15},{8,0},{9,1},... | collective-permute-start | bytes 98312 | tf_op jit(solution)/shard_map/ppermute | solution.py:32
  4.0 1.5 %copy-done.2 = bf16[2,8192]{1,0:T(2,128)(2,1)S(1)} copy-done((bf16[2,8192]{1,0:T(2,128)(2,1)S(1)}, bf16[2,8192]{1,0:T(2,128)(2,1)}, u32[]{:S(2)}) %copy-start.2) | copy-done | bytes 32792
  5.6 0.9 %collective-permute-done = bf16[2,8192]{1,0:T(2,128)(2,1)S(1)} collective-permute-done((bf16[2,8192]{1,0:T(2,128)(2,1)}, bf16[2,8192]{1,0:T(2,128)(2,1)S(1)}, u32[]{:S(2)}, u32[]{:S(2)}) %collective-permute-start) | collective-permute-done | bytes 32800 | tf_op jit(solution)/shard_map/ppermute | solution.py:32
  6.5 0.1 broadcast_select_fusion.11
  6.6 0.1 pad_maximum_fusion.2.refs_0_
  6.6 1.8 %collective-permute-start.3 = (bf16[4,8192]{1,0:T(4,128)(2,1)S(1)}, bf16[4,8192]{1,0:T(4,128)(2,1)S(1)}, u32[]{:S(2)}, u32[]{:S(2)}) collective-permute-start(bf16[4,8192]{1,0:T(4,128)(2,1)S(1)} %pad_maximum_fusion.2.refs_0_), channel_id=1, source_target_pairs={{0,2},{1,3},{2,0},{3,1},{4,6},{5,7},{6,4},{7,5},{8,10},{9,11},{10,... | collective-permute-start | bytes 196616 | tf_op jit(solution)/shard_map/ppermute | solution.py:32
  8.4 1.3 %collective-permute-start.2 = (bf16[4,8192]{1,0:T(4,128)(2,1)S(1)}, bf16[4,8192]{1,0:T(4,128)(2,1)S(1)}, u32[]{:S(2)}, u32[]{:S(2)}) collective-permute-start(bf16[4,8192]{1,0:T(4,128)(2,1)S(1)} %pad_maximum_fusion.2.refs_0_), channel_id=1, source_target_pairs={{0,4},{1,5},{2,6},{3,7},{4,0},{5,1},{6,2},{7,3},{8,12},{9,13},{10,... | collective-permute-start | bytes 196616 | tf_op jit(solution)/shard_map/ppermute | solution.py:32
  9.8 0.4 collective-permute-start.1
  10.2 2.6 %shard_map.56.refs_0_ = bf16[1536,1792]{1,0:T(8,128)(2,1)S(1)} custom-call(bf16[8192,1792]{1,0:T(8,128)(2,1)} %gate_ref.1, bf16[4,8192]{1,0:T(4,128)(2,1)S(1)} %pad_maximum_fusion.2.refs_0_), custom_call_target="tpu_custom_call" | custom-call | bytes 11010048 | tf_op jit(solution)/shard_map/pallas_call | solution.py:56
  12.8 0.0 collective-permute-done.3
  12.8 0.0 collective-permute-done.2
  12.8 2.2 %collective-permute-done.1 = bf16[4,8192]{1,0:T(4,128)(2,1)S(1)} collective-permute-done((bf16[4,8192]{1,0:T(4,128)(2,1)S(1)}, bf16[4,8192]{1,0:T(4,128)(2,1)S(1)}, u32[]{:S(2)}, u32[]{:S(2)}) %collective-permute-start.1) | collective-permute-done | bytes 65568 | tf_op jit(solution)/shard_map/ppermute | solution.py:32
  14.9 0.1 broadcast_select_fusion.9
  15.1 0.2 pad_maximum_fusion.1
  15.3 0.1 collective-permute-start.4
  15.3 1.5 %collective-permute-done.4 = bf16[16,8192]{1,0:T(8,128)(2,1)S(1)} collective-permute-done((bf16[16,8192]{1,0:T(8,128)(2,1)S(1)}, bf16[16,8192]{1,0:T(8,128)(2,1)S(1)}, u32[]{:S(2)}, u32[]{:S(2)}) %collective-permute-start.4) | collective-permute-done | bytes 262176 | tf_op jit(solution)/shard_map/ppermute | solution.py:32
  16.9 0.2 broadcast_select_fusion.1
  17.1 0.0 copy-done
  17.1 10.9 %shard_map.57 = bf16[32,1792]{1,0:T(8,128)(2,1)S(1)} custom-call(bf16[32,8192]{1,0:T(8,128)(2,1)S(1)} %pad_maximum_fusion.x_ref, bf16[256,256]{1,0:T(8,128)(2,1)S(1)} %copy-done.1, bf16[8192,1792]{1,0:T(8,128)(2,1)} %gate_ref.1, bf16[8192,1792]{1,0:T(8,128)(2,1)S(1)} %copy-done, bf16[1536,1792]{1,0:T(8,128)(2,1)S(1)} %shard_map.56.refs_0_), custom_call_target="tpu_custom_call" | custom-call | flops 1879048192 | bytes 23855104 | tf_op jit(solution)/shard_map/pallas_call | solution.py:159
  28.0 0.2 collective-permute-start.5
  28.2 1.2 %collective-permute-done.5 = bf16[32,1792]{1,0:T(8,128)(2,1)S(1)} collective-permute-done((bf16[32,1792]{1,0:T(8,128)(2,1)S(1)}, bf16[32,1792]{1,0:T(8,128)(2,1)S(1)}, u32[]{:S(2)}, u32[]{:S(2)}) %collective-permute-start.5) | collective-permute-done | bytes 114720 | tf_op jit(solution)/shard_map/ppermute | solution.py:32
  29.5 2.9 %collective-permute-start.6 = (bf16[32,1792]{1,0:T(8,128)(2,1)S(1)}, bf16[32,1792]{1,0:T(8,128)(2,1)S(1)}, u32[]{:S(2)}, u32[]{:S(2)}) collective-permute-start(bf16[32,1792]{1,0:T(8,128)(2,1)S(1)} %fusion.1.refs_0_), channel_id=1, source_target_pairs={{0,8},{1,9},{2,10},{3,11},{4,12},{5,13},{6,14},{7,15},{8,0},{9,1},... | collective-permute-start | bytes 344072 | tf_op jit(solution)/shard_map/ppermute | solution.py:32
  32.4 4.6 %shard_map.58.refs_0_ = bf16[768,8192]{1,0:T(8,128)(2,1)S(1)} custom-call(bf16[1792,8192]{1,0:T(8,128)(2,1)} %weight_ref.7, bf16[32,1792]{1,0:T(8,128)(2,1)S(1)} %fusion.1.refs_0_), custom_call_target="tpu_custom_call" | custom-call | bytes 25165824 | tf_op jit(solution)/shard_map/pallas_call | solution.py:56
  37.0 1.3 %collective-permute-done.6 = bf16[32,1792]{1,0:T(8,128)(2,1)S(1)} collective-permute-done((bf16[32,1792]{1,0:T(8,128)(2,1)S(1)}, bf16[32,1792]{1,0:T(8,128)(2,1)S(1)}, u32[]{:S(2)}, u32[]{:S(2)}) %collective-permute-start.6) | collective-permute-done | bytes 114720 | tf_op jit(solution)/shard_map/ppermute | solution.py:32
  38.3 0.1 collective-permute-start.9
  38.4 2.0 %collective-permute-start.8 = (bf16[32,1792]{1,0:T(8,128)(2,1)S(1)}, bf16[32,1792]{1,0:T(8,128)(2,1)S(1)}, u32[]{:S(2)}, u32[]{:S(2)}) collective-permute-start(bf16[32,1792]{1,0:T(8,128)(2,1)S(1)} %fusion.3.refs_0_), channel_id=1, source_target_pairs={{0,4},{1,5},{2,6},{3,7},{4,0},{5,1},{6,2},{7,3},{8,12},{9,13},{10,... | collective-permute-start | bytes 344072 | tf_op jit(solution)/shard_map/ppermute | solution.py:32
  40.4 1.4 %collective-permute-start.7 = (bf16[32,1792]{1,0:T(8,128)(2,1)S(1)}, bf16[32,1792]{1,0:T(8,128)(2,1)S(1)}, u32[]{:S(2)}, u32[]{:S(2)}) collective-permute-start(bf16[32,1792]{1,0:T(8,128)(2,1)S(1)} %fusion.3.refs_0_), channel_id=1, source_target_pairs={{0,2},{1,3},{2,0},{3,1},{4,6},{5,7},{6,4},{7,5},{8,10},{9,11},{10,... | collective-permute-start | bytes 344072 | tf_op jit(solution)/shard_map/ppermute | solution.py:32
  41.8 4.6 %shard_map.59.refs_1_ = bf16[768,8192]{1,0:T(8,128)(2,1)S(1)} custom-call(bf16[1792,8192]{1,0:T(8,128)(2,1)} %weight_ref.7, bf16[32,1792]{1,0:T(8,128)(2,1)S(1)} %fusion.3.refs_0_), custom_call_target="tpu_custom_call" | custom-call | bytes 25165824 | tf_op jit(solution)/shard_map/pallas_call | solution.py:56
  46.4 0.0 collective-permute-done.9
  46.4 0.4 collective-permute-done.7
  46.8 0.1 fusion.8.rotated_ref
  46.9 5.1 %shard_map.60 = (f32[16,8192]{1,0:T(8,128)S(1)}, bf16[16,8192]{1,0:T(8,128)(2,1)S(1)}) custom-call(bf16[32,1792]{1,0:T(8,128)(2,1)S(1)} %fusion.8.rotated_ref, bf16[1792,8192]{1,0:T(8,128)(2,1)} %weight_ref.7, bf16[768,8192]{1,0:T(8,128)(2,1)S(1)} %shard_map.58.refs_0_, bf16[768,8192]{1,0:T(8,128)(2,1)S(1)} %shard_map.59.refs_1_), custom_call_target="tpu_custom_call" | custom-call | flops 939524096 | bytes 4194304 | tf_op jit(solution)/shard_map/pallas_call | solution.py:235
  52.1 0.1 collective-permute-start.10
  52.1 1.5 %collective-permute-done.10 = bf16[16,8192]{1,0:T(8,128)(2,1)S(1)} collective-permute-done((bf16[16,8192]{1,0:T(8,128)(2,1)S(1)}, bf16[16,8192]{1,0:T(8,128)(2,1)S(1)}, u32[]{:S(2)}, u32[]{:S(2)}) %collective-permute-start.10) | collective-permute-done | bytes 262176 | tf_op jit(solution)/shard_map/ppermute | solution.py:32
  53.7 0.1 convert_add_fusion
  53.7 0.1 reshape.27
  53.9 0.1 fusion.11
  54.0 0.6 collective-permute-start.11
  54.6 0.3 collective-permute-start.12
  54.9 2.6 %collective-permute-start.13 = (bf16[4,8192]{1,0:T(4,128)(2,1)S(1)}, bf16[4,8192]{1,0:T(4,128)(2,1)S(1)}, u32[]{:S(2)}, u32[]{:S(2)}) collective-permute-start(bf16[4,8192]{1,0:T(4,128)(2,1)S(1)} %get-tuple-element.43), channel_id=1, source_target_pairs={{0,6},{1,7},{2,4},{3,5},{4,2},{5,3},{6,0},{7,1},{8,14},{9,15},{10,... | collective-permute-start | bytes 196616 | tf_op jit(solution)/shard_map/ppermute | solution.py:32
  57.6 0.8 %collective-permute-done.11 = bf16[4,8192]{1,0:T(4,128)(2,1)S(1)} collective-permute-done((bf16[4,8192]{1,0:T(4,128)(2,1)S(1)}, bf16[4,8192]{1,0:T(4,128)(2,1)S(1)}, u32[]{:S(2)}, u32[]{:S(2)}) %collective-permute-start.11) | collective-permute-done | bytes 65568 | tf_op jit(solution)/shard_map/ppermute | solution.py:32
  58.3 1.1 %collective-permute-done.12 = bf16[4,8192]{1,0:T(4,128)(2,1)S(1)} collective-permute-done((bf16[4,8192]{1,0:T(4,128)(2,1)S(1)}, bf16[4,8192]{1,0:T(4,128)(2,1)S(1)}, u32[]{:S(2)}, u32[]{:S(2)}) %collective-permute-start.12) | collective-permute-done | bytes 65568 | tf_op jit(solution)/shard_map/ppermute | solution.py:32
  59.4 1.4 %collective-permute-done.13 = bf16[4,8192]{1,0:T(4,128)(2,1)S(1)} collective-permute-done((bf16[4,8192]{1,0:T(4,128)(2,1)S(1)}, bf16[4,8192]{1,0:T(4,128)(2,1)S(1)}, u32[]{:S(2)}, u32[]{:S(2)}) %collective-permute-start.13) | collective-permute-done | bytes 65568 | tf_op jit(solution)/shard_map/ppermute | solution.py:32
  60.8 0.1 fusion.10
  60.9 0.1 select_convert_fusion.3
  61.0 2.1 %collective-permute-start.14 = (bf16[2,8192]{1,0:T(2,128)(2,1)S(1)}, bf16[2,8192]{1,0:T(2,128)(2,1)S(1)}, u32[]{:S(2)}, u32[]{:S(2)}) collective-permute-start(bf16[2,8192]{1,0:T(2,128)(2,1)S(1)} %select_convert_fusion.3), channel_id=1, source_target_pairs={{0,8},{1,9},{2,10},{3,11},{4,12},{5,13},{6,14},{7,15},{8,0},{9,1},... | collective-permute-start | bytes 98312 | tf_op jit(solution)/shard_map/ppermute | solution.py:32
  63.1 2.7 %collective-permute-done.14 = bf16[2,8192]{1,0:T(2,128)(2,1)S(1)} collective-permute-done((bf16[2,8192]{1,0:T(2,128)(2,1)S(1)}, bf16[2,8192]{1,0:T(2,128)(2,1)S(1)}, u32[]{:S(2)}, u32[]{:S(2)}) %collective-permute-start.14) | collective-permute-done | bytes 32800 | tf_op jit(solution)/shard_map/ppermute | solution.py:32
  65.8 0.7 %add_convert_fusion = bf16[2,8192]{1,0:T(2,128)(2,1)} fusion(bf16[2,8192]{1,0:T(2,128)(2,1)S(1)} %collective-permute-done.14, pred[]{:T(512)S(6)} %eq.15, f32[4,8192]{1,0:T(4,128)S(1)} %fusion.10), kind=kLoop, calls=%fused_computation.33 | loop fusion | flops 65536 | bytes 196609 | tf_op jit(solution)/shard_map/convert_element_type | solution.py:362
  (9 shorter events, 0.1 us)
Async XLA Ops:
  0.0 17.1 %copy-start.1 = (bf16[256,256]{1,0:T(8,128)(2,1)S(1)}, bf16[256,256]{1,0:T(8,128)(2,1)}, u32[]{:S(2)}) copy-start(bf16[256,256]{1,0:T(8,128)(2,1)} %constant.6.clone.spread_ref) | copy-start | bytes 393220
  0.0 17.1 %copy-start = (bf16[8192,1792]{1,0:T(8,128)(2,1)S(1)}, bf16[8192,1792]{1,0:T(8,128)(2,1)}, u32[]{:S(2)}) copy-start(bf16[8192,1792]{1,0:T(8,128)(2,1)} %up_ref.1) | copy-start | bytes 88080384
  0.0 6.5 %collective-permute-start = (bf16[2,8192]{1,0:T(2,128)(2,1)}, bf16[2,8192]{1,0:T(2,128)(2,1)S(1)}, u32[]{:S(2)}, u32[]{:S(2)}) collective-permute-start(bf16[2,8192]{1,0:T(2,128)(2,1)} %value_ref), channel_id=1, source_target_pairs={{0,8},{1,9},{2,10},{3,11},{4,12},{5,13},{6,14},{7,15},{8,0},{9,1},... | collective-permute-start | bytes 98312 | tf_op jit(solution)/shard_map/ppermute | solution.py:32
  4.0 1.5 %copy-start.2 = (bf16[2,8192]{1,0:T(2,128)(2,1)S(1)}, bf16[2,8192]{1,0:T(2,128)(2,1)}, u32[]{:S(2)}) copy-start(bf16[2,8192]{1,0:T(2,128)(2,1)} %value_ref) | copy-start | bytes 98308
  6.6 6.1 %collective-permute-start.3 = (bf16[4,8192]{1,0:T(4,128)(2,1)S(1)}, bf16[4,8192]{1,0:T(4,128)(2,1)S(1)}, u32[]{:S(2)}, u32[]{:S(2)}) collective-permute-start(bf16[4,8192]{1,0:T(4,128)(2,1)S(1)} %pad_maximum_fusion.2.refs_0_), channel_id=1, source_target_pairs={{0,2},{1,3},{2,0},{3,1},{4,6},{5,7},{6,4},{7,5},{8,10},{9,11},{10,... | collective-permute-start | bytes 196616 | tf_op jit(solution)/shard_map/ppermute | solution.py:32
  8.4 4.3 %collective-permute-start.2 = (bf16[4,8192]{1,0:T(4,128)(2,1)S(1)}, bf16[4,8192]{1,0:T(4,128)(2,1)S(1)}, u32[]{:S(2)}, u32[]{:S(2)}) collective-permute-start(bf16[4,8192]{1,0:T(4,128)(2,1)S(1)} %pad_maximum_fusion.2.refs_0_), channel_id=1, source_target_pairs={{0,4},{1,5},{2,6},{3,7},{4,0},{5,1},{6,2},{7,3},{8,12},{9,13},{10,... | collective-permute-start | bytes 196616 | tf_op jit(solution)/shard_map/ppermute | solution.py:32
  9.8 5.2 %collective-permute-start.1 = (bf16[4,8192]{1,0:T(4,128)(2,1)S(1)}, bf16[4,8192]{1,0:T(4,128)(2,1)S(1)}, u32[]{:S(2)}, u32[]{:S(2)}) collective-permute-start(bf16[4,8192]{1,0:T(4,128)(2,1)S(1)} %pad_maximum_fusion.2.refs_0_), channel_id=1, source_target_pairs={{0,6},{1,7},{2,4},{3,5},{4,2},{5,3},{6,0},{7,1},{8,14},{9,15},{10,... | collective-permute-start | bytes 196616 | tf_op jit(solution)/shard_map/ppermute | solution.py:32
  15.3 1.6 %collective-permute-start.4 = (bf16[16,8192]{1,0:T(8,128)(2,1)S(1)}, bf16[16,8192]{1,0:T(8,128)(2,1)S(1)}, u32[]{:S(2)}, u32[]{:S(2)}) collective-permute-start(bf16[16,8192]{1,0:T(8,128)(2,1)S(1)} %pad_maximum_fusion.1), channel_id=1, source_target_pairs={{0,1},{1,0},{2,3},{3,2},{4,5},{5,4},{6,7},{7,6},{8,9},{9,8},{10,11... | collective-permute-start | bytes 786440 | tf_op jit(solution)/shard_map/ppermute | solution.py:32
  28.0 1.4 %collective-permute-start.5 = (bf16[32,1792]{1,0:T(8,128)(2,1)S(1)}, bf16[32,1792]{1,0:T(8,128)(2,1)S(1)}, u32[]{:S(2)}, u32[]{:S(2)}) collective-permute-start(bf16[32,1792]{1,0:T(8,128)(2,1)S(1)} %shard_map.57), channel_id=1, source_target_pairs={{0,1},{1,0},{2,3},{3,2},{4,5},{5,4},{6,7},{7,6},{8,9},{9,8},{10,11... | collective-permute-start | bytes 344072 | tf_op jit(solution)/shard_map/ppermute | solution.py:32
  29.5 8.7 %collective-permute-start.6 = (bf16[32,1792]{1,0:T(8,128)(2,1)S(1)}, bf16[32,1792]{1,0:T(8,128)(2,1)S(1)}, u32[]{:S(2)}, u32[]{:S(2)}) collective-permute-start(bf16[32,1792]{1,0:T(8,128)(2,1)S(1)} %fusion.1.refs_0_), channel_id=1, source_target_pairs={{0,8},{1,9},{2,10},{3,11},{4,12},{5,13},{6,14},{7,15},{8,0},{9,1},... | collective-permute-start | bytes 344072 | tf_op jit(solution)/shard_map/ppermute | solution.py:32
  38.3 8.1 %collective-permute-start.9 = (bf16[32,1792]{1,0:T(8,128)(2,1)S(1)}, bf16[32,1792]{1,0:T(8,128)(2,1)S(1)}, u32[]{:S(2)}, u32[]{:S(2)}) collective-permute-start(bf16[32,1792]{1,0:T(8,128)(2,1)S(1)} %fusion.3.refs_0_), channel_id=1, source_target_pairs={{0,6},{1,7},{2,4},{3,5},{4,2},{5,3},{6,0},{7,1},{8,14},{9,15},{10,... | collective-permute-start | bytes 344072 | tf_op jit(solution)/shard_map/ppermute | solution.py:32
  38.4 8.1 %collective-permute-start.8 = (bf16[32,1792]{1,0:T(8,128)(2,1)S(1)}, bf16[32,1792]{1,0:T(8,128)(2,1)S(1)}, u32[]{:S(2)}, u32[]{:S(2)}) collective-permute-start(bf16[32,1792]{1,0:T(8,128)(2,1)S(1)} %fusion.3.refs_0_), channel_id=1, source_target_pairs={{0,4},{1,5},{2,6},{3,7},{4,0},{5,1},{6,2},{7,3},{8,12},{9,13},{10,... | collective-permute-start | bytes 344072 | tf_op jit(solution)/shard_map/ppermute | solution.py:32
  40.4 6.4 %collective-permute-start.7 = (bf16[32,1792]{1,0:T(8,128)(2,1)S(1)}, bf16[32,1792]{1,0:T(8,128)(2,1)S(1)}, u32[]{:S(2)}, u32[]{:S(2)}) collective-permute-start(bf16[32,1792]{1,0:T(8,128)(2,1)S(1)} %fusion.3.refs_0_), channel_id=1, source_target_pairs={{0,2},{1,3},{2,0},{3,1},{4,6},{5,7},{6,4},{7,5},{8,10},{9,11},{10,... | collective-permute-start | bytes 344072 | tf_op jit(solution)/shard_map/ppermute | solution.py:32
  52.1 1.6 %collective-permute-start.10 = (bf16[16,8192]{1,0:T(8,128)(2,1)S(1)}, bf16[16,8192]{1,0:T(8,128)(2,1)S(1)}, u32[]{:S(2)}, u32[]{:S(2)}) collective-permute-start(bf16[16,8192]{1,0:T(8,128)(2,1)S(1)} %get-tuple-element.40), channel_id=1, source_target_pairs={{0,1},{1,0},{2,3},{3,2},{4,5},{5,4},{6,7},{7,6},{8,9},{9,8},{10,11... | collective-permute-start | bytes 786440 | tf_op jit(solution)/shard_map/ppermute | solution.py:32
  54.0 4.3 %collective-permute-start.11 = (bf16[4,8192]{1,0:T(4,128)(2,1)S(1)}, bf16[4,8192]{1,0:T(4,128)(2,1)S(1)}, u32[]{:S(2)}, u32[]{:S(2)}) collective-permute-start(bf16[4,8192]{1,0:T(4,128)(2,1)S(1)} %get-tuple-element.41), channel_id=1, source_target_pairs={{0,2},{1,3},{2,0},{3,1},{4,6},{5,7},{6,4},{7,5},{8,10},{9,11},{10,... | collective-permute-start | bytes 196616 | tf_op jit(solution)/shard_map/ppermute | solution.py:32
  54.6 4.8 %collective-permute-start.12 = (bf16[4,8192]{1,0:T(4,128)(2,1)S(1)}, bf16[4,8192]{1,0:T(4,128)(2,1)S(1)}, u32[]{:S(2)}, u32[]{:S(2)}) collective-permute-start(bf16[4,8192]{1,0:T(4,128)(2,1)S(1)} %get-tuple-element.42), channel_id=1, source_target_pairs={{0,4},{1,5},{2,6},{3,7},{4,0},{5,1},{6,2},{7,3},{8,12},{9,13},{10,... | collective-permute-start | bytes 196616 | tf_op jit(solution)/shard_map/ppermute | solution.py:32
  54.9 5.9 %collective-permute-start.13 = (bf16[4,8192]{1,0:T(4,128)(2,1)S(1)}, bf16[4,8192]{1,0:T(4,128)(2,1)S(1)}, u32[]{:S(2)}, u32[]{:S(2)}) collective-permute-start(bf16[4,8192]{1,0:T(4,128)(2,1)S(1)} %get-tuple-element.43), channel_id=1, source_target_pairs={{0,6},{1,7},{2,4},{3,5},{4,2},{5,3},{6,0},{7,1},{8,14},{9,15},{10,... | collective-permute-start | bytes 196616 | tf_op jit(solution)/shard_map/ppermute | solution.py:32
  61.0 4.9 %collective-permute-start.14 = (bf16[2,8192]{1,0:T(2,128)(2,1)S(1)}, bf16[2,8192]{1,0:T(2,128)(2,1)S(1)}, u32[]{:S(2)}, u32[]{:S(2)}) collective-permute-start(bf16[2,8192]{1,0:T(2,128)(2,1)S(1)} %select_convert_fusion.3), channel_id=1, source_target_pairs={{0,8},{1,9},{2,10},{3,11},{4,12},{5,13},{6,14},{7,15},{8,0},{9,1},... | collective-permute-start | bytes 98312 | tf_op jit(solution)/shard_map/ppermute | solution.py:32

commit v7 on v6

--- a/solution.py
+++ b/solution.py
@@ -277,11 +277,11 @@
 
 
 def gather_rounds(levels):
-    return [(level,) for level in range(levels)[:2:-1]] + [(1, 2), (0,)]
+    return [(level,) for level in range(levels)[:2:-1]] + [(2, 1), (0,)]
 
 
 def hadamard_rounds(levels):
-    return [(0,)] + [(level,) for level in range(levels)[3:]] + [(2, 1)]
+    return [(0,)] + [(level,) for level in range(levels)[3:]] + [(1, 2)]
 
 
 def per_device(tokens, gate_weight, up_weight, down_weight):

time: 66.7 us -> 66 us (0.990)
  waiting for transfers between devices: 14.9 us -> 13.8 us
    ppermute x15, waiting for transfers between devices: 14.9 us -> 13.8 us  [swapped(): return lax.ppermute(value, 'tensor', pairs)]
  transfers between devices with their start and end apart: 15 -> 15, of which waited for: 11 -> 10; matrix products, arithmetic and copies ran while one was open for 0% -> 0% of each run, Pallas kernels for 18% -> 18%
where the time goes in v7:
time: 66 us; the launch traced here: 65.8 us
  Pallas kernels  27.8 us (42%)
  starting transfers between devices  20.4 us (31%)
  waiting for transfers between devices  13.8 us (21%)
  other arithmetic  1.9 us (3%)
  local copies, waits for them, and re-layouts  1.67 us (3%)
    ppermute x15, starting transfers between devices, swapped(): return lax.ppermute(value, 'tensor', pairs)  20.4 us
    ppermute x15, waiting for transfers between devices, swapped(): return lax.ppermute(value, 'tensor', pairs)  13.8 us
    pallas_call x3, Pallas kernels, fetch(): pl.pallas_call(kernel, out_shape=jax.ShapeDtypeStruct((rows, width), weig...  11.7 us
    pallas_call x1, Pallas kernels, gate_up(): pl.pallas_call(kernel, out_shape=jax.ShapeDtypeStruct((tokens, width), jn...  10.9 us
    pallas_call x1, Pallas kernels, down(): pl.pallas_call(kernel, out_shape=(jax.ShapeDtypeStruct((half, width), jnp...  5.14 us
    unnamed x6, local copies, waits for them, and re-layouts  1.52 us
  transfers between devices with their start and end apart: 15, of which 10 were waited for; matrix products, arithmetic and copies ran while one was open for 0% of the time, Pallas kernels for 18%

profile of v7, /device:TPU:0, one launch (start us, length us, event | category | flops | bytes accessed | tf_op | source)
XLA Modules:
  0.0 65.8 jit_solution(10319503784364224743)
XLA Ops:
  0.0 4.0 %collective-permute-start = (bf16[2,8192]{1,0:T(2,128)(2,1)}, bf16[2,8192]{1,0:T(2,128)(2,1)S(1)}, u32[]{:S(2)}, u32[]{:S(2)}) collective-permute-start(bf16[2,8192]{1,0:T(2,128)(2,1)} %value_ref), channel_id=1, source_target_pairs={{0,8},{1,9},{2,10},{3,11},{4,12},{5,13},{6,14},{7,15},{8,0},{9,1},... | collective-permute-start | bytes 98312 | tf_op jit(solution)/shard_map/ppermute | solution.py:32
  4.0 1.5 %copy-done.2 = bf16[2,8192]{1,0:T(2,128)(2,1)S(1)} copy-done((bf16[2,8192]{1,0:T(2,128)(2,1)S(1)}, bf16[2,8192]{1,0:T(2,128)(2,1)}, u32[]{:S(2)}) %copy-start.2) | copy-done | bytes 32792
  5.6 0.9 %collective-permute-done = bf16[2,8192]{1,0:T(2,128)(2,1)S(1)} collective-permute-done((bf16[2,8192]{1,0:T(2,128)(2,1)}, bf16[2,8192]{1,0:T(2,128)(2,1)S(1)}, u32[]{:S(2)}, u32[]{:S(2)}) %collective-permute-start) | collective-permute-done | bytes 32800 | tf_op jit(solution)/shard_map/ppermute | solution.py:32
  6.5 0.1 broadcast_select_fusion.11
  6.6 0.1 pad_maximum_fusion.2.refs_0_
  6.6 1.6 %collective-permute-start.3 = (bf16[4,8192]{1,0:T(4,128)(2,1)S(1)}, bf16[4,8192]{1,0:T(4,128)(2,1)S(1)}, u32[]{:S(2)}, u32[]{:S(2)}) collective-permute-start(bf16[4,8192]{1,0:T(4,128)(2,1)S(1)} %pad_maximum_fusion.2.refs_0_), channel_id=1, source_target_pairs={{0,4},{1,5},{2,6},{3,7},{4,0},{5,1},{6,2},{7,3},{8,12},{9,13},{10,... | collective-permute-start | bytes 196616 | tf_op jit(solution)/shard_map/ppermute | solution.py:32
  8.3 1.5 %collective-permute-start.2 = (bf16[4,8192]{1,0:T(4,128)(2,1)S(1)}, bf16[4,8192]{1,0:T(4,128)(2,1)S(1)}, u32[]{:S(2)}, u32[]{:S(2)}) collective-permute-start(bf16[4,8192]{1,0:T(4,128)(2,1)S(1)} %pad_maximum_fusion.2.refs_0_), channel_id=1, source_target_pairs={{0,2},{1,3},{2,0},{3,1},{4,6},{5,7},{6,4},{7,5},{8,10},{9,11},{10,... | collective-permute-start | bytes 196616 | tf_op jit(solution)/shard_map/ppermute | solution.py:32
  9.8 0.4 collective-permute-start.1
  10.2 2.6 %shard_map.56.refs_0_ = bf16[1536,1792]{1,0:T(8,128)(2,1)S(1)} custom-call(bf16[8192,1792]{1,0:T(8,128)(2,1)} %gate_ref.1, bf16[4,8192]{1,0:T(4,128)(2,1)S(1)} %pad_maximum_fusion.2.refs_0_), custom_call_target="tpu_custom_call" | custom-call | bytes 11010048 | tf_op jit(solution)/shard_map/pallas_call | solution.py:56
  12.8 0.0 collective-permute-done.3
  12.8 0.2 collective-permute-done.2
  13.0 1.9 %collective-permute-done.1 = bf16[4,8192]{1,0:T(4,128)(2,1)S(1)} collective-permute-done((bf16[4,8192]{1,0:T(4,128)(2,1)S(1)}, bf16[4,8192]{1,0:T(4,128)(2,1)S(1)}, u32[]{:S(2)}, u32[]{:S(2)}) %collective-permute-start.1) | collective-permute-done | bytes 65568 | tf_op jit(solution)/shard_map/ppermute | solution.py:32
  14.9 0.1 broadcast_select_fusion.9
  15.1 0.2 pad_maximum_fusion.1
  15.3 0.1 collective-permute-start.4
  15.3 1.5 %collective-permute-done.4 = bf16[16,8192]{1,0:T(8,128)(2,1)S(1)} collective-permute-done((bf16[16,8192]{1,0:T(8,128)(2,1)S(1)}, bf16[16,8192]{1,0:T(8,128)(2,1)S(1)}, u32[]{:S(2)}, u32[]{:S(2)}) %collective-permute-start.4) | collective-permute-done | bytes 262176 | tf_op jit(solution)/shard_map/ppermute | solution.py:32
  16.9 0.2 broadcast_select_fusion.1
  17.1 0.0 copy-done
  17.1 10.9 %shard_map.57 = bf16[32,1792]{1,0:T(8,128)(2,1)S(1)} custom-call(bf16[32,8192]{1,0:T(8,128)(2,1)S(1)} %pad_maximum_fusion.x_ref, bf16[256,256]{1,0:T(8,128)(2,1)S(1)} %copy-done.1, bf16[8192,1792]{1,0:T(8,128)(2,1)} %gate_ref.1, bf16[8192,1792]{1,0:T(8,128)(2,1)S(1)} %copy-done, bf16[1536,1792]{1,0:T(8,128)(2,1)S(1)} %shard_map.56.refs_0_), custom_call_target="tpu_custom_call" | custom-call | flops 1879048192 | bytes 23855104 | tf_op jit(solution)/shard_map/pallas_call | solution.py:159
  28.0 0.2 collective-permute-start.5
  28.2 1.2 %collective-permute-done.5 = bf16[32,1792]{1,0:T(8,128)(2,1)S(1)} collective-permute-done((bf16[32,1792]{1,0:T(8,128)(2,1)S(1)}, bf16[32,1792]{1,0:T(8,128)(2,1)S(1)}, u32[]{:S(2)}, u32[]{:S(2)}) %collective-permute-start.5) | collective-permute-done | bytes 114720 | tf_op jit(solution)/shard_map/ppermute | solution.py:32
  29.5 2.9 %collective-permute-start.6 = (bf16[32,1792]{1,0:T(8,128)(2,1)S(1)}, bf16[32,1792]{1,0:T(8,128)(2,1)S(1)}, u32[]{:S(2)}, u32[]{:S(2)}) collective-permute-start(bf16[32,1792]{1,0:T(8,128)(2,1)S(1)} %fusion.1.refs_0_), channel_id=1, source_target_pairs={{0,8},{1,9},{2,10},{3,11},{4,12},{5,13},{6,14},{7,15},{8,0},{9,1},... | collective-permute-start | bytes 344072 | tf_op jit(solution)/shard_map/ppermute | solution.py:32
  32.4 4.6 %shard_map.58.refs_0_ = bf16[768,8192]{1,0:T(8,128)(2,1)S(1)} custom-call(bf16[1792,8192]{1,0:T(8,128)(2,1)} %weight_ref.7, bf16[32,1792]{1,0:T(8,128)(2,1)S(1)} %fusion.1.refs_0_), custom_call_target="tpu_custom_call" | custom-call | bytes 25165824 | tf_op jit(solution)/shard_map/pallas_call | solution.py:56
  37.0 1.3 %collective-permute-done.6 = bf16[32,1792]{1,0:T(8,128)(2,1)S(1)} collective-permute-done((bf16[32,1792]{1,0:T(8,128)(2,1)S(1)}, bf16[32,1792]{1,0:T(8,128)(2,1)S(1)}, u32[]{:S(2)}, u32[]{:S(2)}) %collective-permute-start.6) | collective-permute-done | bytes 114720 | tf_op jit(solution)/shard_map/ppermute | solution.py:32
  38.3 0.1 collective-permute-start.9
  38.4 1.0 %collective-permute-start.8 = (bf16[32,1792]{1,0:T(8,128)(2,1)S(1)}, bf16[32,1792]{1,0:T(8,128)(2,1)S(1)}, u32[]{:S(2)}, u32[]{:S(2)}) collective-permute-start(bf16[32,1792]{1,0:T(8,128)(2,1)S(1)} %fusion.3.refs_0_), channel_id=1, source_target_pairs={{0,2},{1,3},{2,0},{3,1},{4,6},{5,7},{6,4},{7,5},{8,10},{9,11},{10,... | collective-permute-start | bytes 344072 | tf_op jit(solution)/shard_map/ppermute | solution.py:32
  39.4 2.5 %collective-permute-start.7 = (bf16[32,1792]{1,0:T(8,128)(2,1)S(1)}, bf16[32,1792]{1,0:T(8,128)(2,1)S(1)}, u32[]{:S(2)}, u32[]{:S(2)}) collective-permute-start(bf16[32,1792]{1,0:T(8,128)(2,1)S(1)} %fusion.3.refs_0_), channel_id=1, source_target_pairs={{0,4},{1,5},{2,6},{3,7},{4,0},{5,1},{6,2},{7,3},{8,12},{9,13},{10,... | collective-permute-start | bytes 344072 | tf_op jit(solution)/shard_map/ppermute | solution.py:32
  41.8 4.6 %shard_map.59.refs_1_ = bf16[768,8192]{1,0:T(8,128)(2,1)S(1)} custom-call(bf16[1792,8192]{1,0:T(8,128)(2,1)} %weight_ref.7, bf16[32,1792]{1,0:T(8,128)(2,1)S(1)} %fusion.3.refs_0_), custom_call_target="tpu_custom_call" | custom-call | bytes 25165824 | tf_op jit(solution)/shard_map/pallas_call | solution.py:56
  46.4 0.0 collective-permute-done.9
  46.4 0.0 collective-permute-done.8
  46.4 0.0 collective-permute-done.7
  46.4 0.1 fusion.8.rotated_ref
  46.6 5.1 %shard_map.60 = (f32[16,8192]{1,0:T(8,128)S(1)}, bf16[16,8192]{1,0:T(8,128)(2,1)S(1)}) custom-call(bf16[32,1792]{1,0:T(8,128)(2,1)S(1)} %fusion.8.rotated_ref, bf16[1792,8192]{1,0:T(8,128)(2,1)} %weight_ref.7, bf16[768,8192]{1,0:T(8,128)(2,1)S(1)} %shard_map.58.refs_0_, bf16[768,8192]{1,0:T(8,128)(2,1)S(1)} %shard_map.59.refs_1_), custom_call_target="tpu_custom_call" | custom-call | flops 939524096 | bytes 4194304 | tf_op jit(solution)/shard_map/pallas_call | solution.py:235
  51.7 0.1 collective-permute-start.10
  51.8 1.5 %collective-permute-done.10 = bf16[16,8192]{1,0:T(8,128)(2,1)S(1)} collective-permute-done((bf16[16,8192]{1,0:T(8,128)(2,1)S(1)}, bf16[16,8192]{1,0:T(8,128)(2,1)S(1)}, u32[]{:S(2)}, u32[]{:S(2)}) %collective-permute-start.10) | collective-permute-done | bytes 262176 | tf_op jit(solution)/shard_map/ppermute | solution.py:32
  53.3 0.1 convert_add_fusion
  53.4 0.1 reshape.27
  53.5 0.1 fusion.11
  53.7 0.2 collective-permute-start.11
  53.9 1.0 %collective-permute-start.12 = (bf16[4,8192]{1,0:T(4,128)(2,1)S(1)}, bf16[4,8192]{1,0:T(4,128)(2,1)S(1)}, u32[]{:S(2)}, u32[]{:S(2)}) collective-permute-start(bf16[4,8192]{1,0:T(4,128)(2,1)S(1)} %get-tuple-element.42), channel_id=1, source_target_pairs={{0,2},{1,3},{2,0},{3,1},{4,6},{5,7},{6,4},{7,5},{8,10},{9,11},{10,... | collective-permute-start | bytes 196616 | tf_op jit(solution)/shard_map/ppermute | solution.py:32
  54.9 2.3 %collective-permute-start.13 = (bf16[4,8192]{1,0:T(4,128)(2,1)S(1)}, bf16[4,8192]{1,0:T(4,128)(2,1)S(1)}, u32[]{:S(2)}, u32[]{:S(2)}) collective-permute-start(bf16[4,8192]{1,0:T(4,128)(2,1)S(1)} %get-tuple-element.43), channel_id=1, source_target_pairs={{0,6},{1,7},{2,4},{3,5},{4,2},{5,3},{6,0},{7,1},{8,14},{9,15},{10,... | collective-permute-start | bytes 196616 | tf_op jit(solution)/shard_map/ppermute | solution.py:32
  57.2 1.1 %collective-permute-done.11 = bf16[4,8192]{1,0:T(4,128)(2,1)S(1)} collective-permute-done((bf16[4,8192]{1,0:T(4,128)(2,1)S(1)}, bf16[4,8192]{1,0:T(4,128)(2,1)S(1)}, u32[]{:S(2)}, u32[]{:S(2)}) %collective-permute-start.11) | collective-permute-done | bytes 65568 | tf_op jit(solution)/shard_map/ppermute | solution.py:32
  58.4 1.7 %collective-permute-done.13 = bf16[4,8192]{1,0:T(4,128)(2,1)S(1)} collective-permute-done((bf16[4,8192]{1,0:T(4,128)(2,1)S(1)}, bf16[4,8192]{1,0:T(4,128)(2,1)S(1)}, u32[]{:S(2)}, u32[]{:S(2)}) %collective-permute-start.13) | collective-permute-done | bytes 65568 | tf_op jit(solution)/shard_map/ppermute | solution.py:32
  60.1 0.1 fusion.10
  60.2 0.1 select_convert_fusion.3
  60.3 2.5 %collective-permute-start.14 = (bf16[2,8192]{1,0:T(2,128)(2,1)S(1)}, bf16[2,8192]{1,0:T(2,128)(2,1)S(1)}, u32[]{:S(2)}, u32[]{:S(2)}) collective-permute-start(bf16[2,8192]{1,0:T(2,128)(2,1)S(1)} %select_convert_fusion.3), channel_id=1, source_target_pairs={{0,8},{1,9},{2,10},{3,11},{4,12},{5,13},{6,14},{7,15},{8,0},{9,1},... | collective-permute-start | bytes 98312 | tf_op jit(solution)/shard_map/ppermute | solution.py:32
  62.8 2.4 %collective-permute-done.14 = bf16[2,8192]{1,0:T(2,128)(2,1)S(1)} collective-permute-done((bf16[2,8192]{1,0:T(2,128)(2,1)S(1)}, bf16[2,8192]{1,0:T(2,128)(2,1)S(1)}, u32[]{:S(2)}, u32[]{:S(2)}) %collective-permute-start.14) | collective-permute-done | bytes 32800 | tf_op jit(solution)/shard_map/ppermute | solution.py:32
  65.1 0.7 %add_convert_fusion = bf16[2,8192]{1,0:T(2,128)(2,1)} fusion(bf16[2,8192]{1,0:T(2,128)(2,1)S(1)} %collective-permute-done.14, pred[]{:T(512)S(6)} %eq.15, f32[4,8192]{1,0:T(4,128)S(1)} %fusion.10), kind=kLoop, calls=%fused_computation.33 | loop fusion | flops 65536 | bytes 196609 | tf_op jit(solution)/shard_map/convert_element_type | solution.py:362
  (9 shorter events, 0.1 us)
Async XLA Ops:
  0.0 17.1 %copy-start.1 = (bf16[256,256]{1,0:T(8,128)(2,1)S(1)}, bf16[256,256]{1,0:T(8,128)(2,1)}, u32[]{:S(2)}) copy-start(bf16[256,256]{1,0:T(8,128)(2,1)} %constant.6.clone.spread_ref) | copy-start | bytes 393220
  0.0 17.1 %copy-start = (bf16[8192,1792]{1,0:T(8,128)(2,1)S(1)}, bf16[8192,1792]{1,0:T(8,128)(2,1)}, u32[]{:S(2)}) copy-start(bf16[8192,1792]{1,0:T(8,128)(2,1)} %up_ref.1) | copy-start | bytes 88080384
  0.0 6.5 %collective-permute-start = (bf16[2,8192]{1,0:T(2,128)(2,1)}, bf16[2,8192]{1,0:T(2,128)(2,1)S(1)}, u32[]{:S(2)}, u32[]{:S(2)}) collective-permute-start(bf16[2,8192]{1,0:T(2,128)(2,1)} %value_ref), channel_id=1, source_target_pairs={{0,8},{1,9},{2,10},{3,11},{4,12},{5,13},{6,14},{7,15},{8,0},{9,1},... | collective-permute-start | bytes 98312 | tf_op jit(solution)/shard_map/ppermute | solution.py:32
  4.0 1.5 %copy-start.2 = (bf16[2,8192]{1,0:T(2,128)(2,1)S(1)}, bf16[2,8192]{1,0:T(2,128)(2,1)}, u32[]{:S(2)}) copy-start(bf16[2,8192]{1,0:T(2,128)(2,1)} %value_ref) | copy-start | bytes 98308
  6.6 6.1 %collective-permute-start.3 = (bf16[4,8192]{1,0:T(4,128)(2,1)S(1)}, bf16[4,8192]{1,0:T(4,128)(2,1)S(1)}, u32[]{:S(2)}, u32[]{:S(2)}) collective-permute-start(bf16[4,8192]{1,0:T(4,128)(2,1)S(1)} %pad_maximum_fusion.2.refs_0_), channel_id=1, source_target_pairs={{0,4},{1,5},{2,6},{3,7},{4,0},{5,1},{6,2},{7,3},{8,12},{9,13},{10,... | collective-permute-start | bytes 196616 | tf_op jit(solution)/shard_map/ppermute | solution.py:32
  8.3 4.8 %collective-permute-start.2 = (bf16[4,8192]{1,0:T(4,128)(2,1)S(1)}, bf16[4,8192]{1,0:T(4,128)(2,1)S(1)}, u32[]{:S(2)}, u32[]{:S(2)}) collective-permute-start(bf16[4,8192]{1,0:T(4,128)(2,1)S(1)} %pad_maximum_fusion.2.refs_0_), channel_id=1, source_target_pairs={{0,2},{1,3},{2,0},{3,1},{4,6},{5,7},{6,4},{7,5},{8,10},{9,11},{10,... | collective-permute-start | bytes 196616 | tf_op jit(solution)/shard_map/ppermute | solution.py:32
  9.8 5.2 %collective-permute-start.1 = (bf16[4,8192]{1,0:T(4,128)(2,1)S(1)}, bf16[4,8192]{1,0:T(4,128)(2,1)S(1)}, u32[]{:S(2)}, u32[]{:S(2)}) collective-permute-start(bf16[4,8192]{1,0:T(4,128)(2,1)S(1)} %pad_maximum_fusion.2.refs_0_), channel_id=1, source_target_pairs={{0,6},{1,7},{2,4},{3,5},{4,2},{5,3},{6,0},{7,1},{8,14},{9,15},{10,... | collective-permute-start | bytes 196616 | tf_op jit(solution)/shard_map/ppermute | solution.py:32
  15.3 1.6 %collective-permute-start.4 = (bf16[16,8192]{1,0:T(8,128)(2,1)S(1)}, bf16[16,8192]{1,0:T(8,128)(2,1)S(1)}, u32[]{:S(2)}, u32[]{:S(2)}) collective-permute-start(bf16[16,8192]{1,0:T(8,128)(2,1)S(1)} %pad_maximum_fusion.1), channel_id=1, source_target_pairs={{0,1},{1,0},{2,3},{3,2},{4,5},{5,4},{6,7},{7,6},{8,9},{9,8},{10,11... | collective-permute-start | bytes 786440 | tf_op jit(solution)/shard_map/ppermute | solution.py:32
  28.0 1.4 %collective-permute-start.5 = (bf16[32,1792]{1,0:T(8,128)(2,1)S(1)}, bf16[32,1792]{1,0:T(8,128)(2,1)S(1)}, u32[]{:S(2)}, u32[]{:S(2)}) collective-permute-start(bf16[32,1792]{1,0:T(8,128)(2,1)S(1)} %shard_map.57), channel_id=1, source_target_pairs={{0,1},{1,0},{2,3},{3,2},{4,5},{5,4},{6,7},{7,6},{8,9},{9,8},{10,11... | collective-permute-start | bytes 344072 | tf_op jit(solution)/shard_map/ppermute | solution.py:32
  29.5 8.7 %collective-permute-start.6 = (bf16[32,1792]{1,0:T(8,128)(2,1)S(1)}, bf16[32,1792]{1,0:T(8,128)(2,1)S(1)}, u32[]{:S(2)}, u32[]{:S(2)}) collective-permute-start(bf16[32,1792]{1,0:T(8,128)(2,1)S(1)} %fusion.1.refs_0_), channel_id=1, source_target_pairs={{0,8},{1,9},{2,10},{3,11},{4,12},{5,13},{6,14},{7,15},{8,0},{9,1},... | collective-permute-start | bytes 344072 | tf_op jit(solution)/shard_map/ppermute | solution.py:32
  38.3 8.1 %collective-permute-start.9 = (bf16[32,1792]{1,0:T(8,128)(2,1)S(1)}, bf16[32,1792]{1,0:T(8,128)(2,1)S(1)}, u32[]{:S(2)}, u32[]{:S(2)}) collective-permute-start(bf16[32,1792]{1,0:T(8,128)(2,1)S(1)} %fusion.3.refs_0_), channel_id=1, source_target_pairs={{0,6},{1,7},{2,4},{3,5},{4,2},{5,3},{6,0},{7,1},{8,14},{9,15},{10,... | collective-permute-start | bytes 344072 | tf_op jit(solution)/shard_map/ppermute | solution.py:32
  38.4 8.1 %collective-permute-start.8 = (bf16[32,1792]{1,0:T(8,128)(2,1)S(1)}, bf16[32,1792]{1,0:T(8,128)(2,1)S(1)}, u32[]{:S(2)}, u32[]{:S(2)}) collective-permute-start(bf16[32,1792]{1,0:T(8,128)(2,1)S(1)} %fusion.3.refs_0_), channel_id=1, source_target_pairs={{0,2},{1,3},{2,0},{3,1},{4,6},{5,7},{6,4},{7,5},{8,10},{9,11},{10,... | collective-permute-start | bytes 344072 | tf_op jit(solution)/shard_map/ppermute | solution.py:32
  39.4 7.1 %collective-permute-start.7 = (bf16[32,1792]{1,0:T(8,128)(2,1)S(1)}, bf16[32,1792]{1,0:T(8,128)(2,1)S(1)}, u32[]{:S(2)}, u32[]{:S(2)}) collective-permute-start(bf16[32,1792]{1,0:T(8,128)(2,1)S(1)} %fusion.3.refs_0_), channel_id=1, source_target_pairs={{0,4},{1,5},{2,6},{3,7},{4,0},{5,1},{6,2},{7,3},{8,12},{9,13},{10,... | collective-permute-start | bytes 344072 | tf_op jit(solution)/shard_map/ppermute | solution.py:32
  51.7 1.6 %collective-permute-start.10 = (bf16[16,8192]{1,0:T(8,128)(2,1)S(1)}, bf16[16,8192]{1,0:T(8,128)(2,1)S(1)}, u32[]{:S(2)}, u32[]{:S(2)}) collective-permute-start(bf16[16,8192]{1,0:T(8,128)(2,1)S(1)} %get-tuple-element.40), channel_id=1, source_target_pairs={{0,1},{1,0},{2,3},{3,2},{4,5},{5,4},{6,7},{7,6},{8,9},{9,8},{10,11... | collective-permute-start | bytes 786440 | tf_op jit(solution)/shard_map/ppermute | solution.py:32
  53.7 4.7 %collective-permute-start.11 = (bf16[4,8192]{1,0:T(4,128)(2,1)S(1)}, bf16[4,8192]{1,0:T(4,128)(2,1)S(1)}, u32[]{:S(2)}, u32[]{:S(2)}) collective-permute-start(bf16[4,8192]{1,0:T(4,128)(2,1)S(1)} %get-tuple-element.41), channel_id=1, source_target_pairs={{0,4},{1,5},{2,6},{3,7},{4,0},{5,1},{6,2},{7,3},{8,12},{9,13},{10,... | collective-permute-start | bytes 196616 | tf_op jit(solution)/shard_map/ppermute | solution.py:32
  53.9 4.5 %collective-permute-start.12 = (bf16[4,8192]{1,0:T(4,128)(2,1)S(1)}, bf16[4,8192]{1,0:T(4,128)(2,1)S(1)}, u32[]{:S(2)}, u32[]{:S(2)}) collective-permute-start(bf16[4,8192]{1,0:T(4,128)(2,1)S(1)} %get-tuple-element.42), channel_id=1, source_target_pairs={{0,2},{1,3},{2,0},{3,1},{4,6},{5,7},{6,4},{7,5},{8,10},{9,11},{10,... | collective-permute-start | bytes 196616 | tf_op jit(solution)/shard_map/ppermute | solution.py:32
  54.9 5.2 %collective-permute-start.13 = (bf16[4,8192]{1,0:T(4,128)(2,1)S(1)}, bf16[4,8192]{1,0:T(4,128)(2,1)S(1)}, u32[]{:S(2)}, u32[]{:S(2)}) collective-permute-start(bf16[4,8192]{1,0:T(4,128)(2,1)S(1)} %get-tuple-element.43), channel_id=1, source_target_pairs={{0,6},{1,7},{2,4},{3,5},{4,2},{5,3},{6,0},{7,1},{8,14},{9,15},{10,... | collective-permute-start | bytes 196616 | tf_op jit(solution)/shard_map/ppermute | solution.py:32
  60.3 4.9 %collective-permute-start.14 = (bf16[2,8192]{1,0:T(2,128)(2,1)S(1)}, bf16[2,8192]{1,0:T(2,128)(2,1)S(1)}, u32[]{:S(2)}, u32[]{:S(2)}) collective-permute-start(bf16[2,8192]{1,0:T(2,128)(2,1)S(1)} %select_convert_fusion.3), channel_id=1, source_target_pairs={{0,8},{1,9},{2,10},{3,11},{4,12},{5,13},{6,14},{7,15},{8,0},{9,1},... | collective-permute-start | bytes 98312 | tf_op jit(solution)/shard_map/ppermute | solution.py:32

commit v8 on v7

--- a/solution.py
+++ b/solution.py
@@ -281,7 +281,7 @@
 
 
 def hadamard_rounds(levels):
-    return [(0,)] + [(level,) for level in range(levels)[3:]] + [(1, 2)]
+    return [(0,), (1, 2)] + [(level,) for level in range(levels)[3:]]
 
 
 def per_device(tokens, gate_weight, up_weight, down_weight):

time: 66 us -> 65.9 us (level)
  waiting for transfers between devices: 13.8 us -> 13 us
  starting transfers between devices: 20.4 us -> 21.1 us
    ppermute x15, waiting for transfers between devices: 13.8 us -> 13 us  [swapped(): return lax.ppermute(value, 'tensor', pairs)]
    ppermute x15, starting transfers between devices: 20.4 us -> 21.1 us  [swapped(): return lax.ppermute(value, 'tensor', pairs)]
  transfers between devices with their start and end apart: 15 -> 15, of which waited for: 10 -> 11; matrix products, arithmetic and copies ran while one was open for 0% -> 0% of each run, Pallas kernels for 18% -> 18%
where the time goes in v8:
time: 65.9 us; the launch traced here: 65.7 us
  Pallas kernels  27.8 us (42%)
  starting transfers between devices  21.1 us (32%)
  waiting for transfers between devices  13 us (20%)
  other arithmetic  1.9 us (3%)
  local copies, waits for them, and re-layouts  1.67 us (3%)
    ppermute x15, starting transfers between devices, swapped(): return lax.ppermute(value, 'tensor', pairs)  21.1 us
    ppermute x15, waiting for transfers between devices, swapped(): return lax.ppermute(value, 'tensor', pairs)  13 us
    pallas_call x3, Pallas kernels, fetch(): pl.pallas_call(kernel, out_shape=jax.ShapeDtypeStruct((rows, width), weig...  11.7 us
    pallas_call x1, Pallas kernels, gate_up(): pl.pallas_call(kernel, out_shape=jax.ShapeDtypeStruct((tokens, width), jn...  10.9 us
    pallas_call x1, Pallas kernels, down(): pl.pallas_call(kernel, out_shape=(jax.ShapeDtypeStruct((half, width), jnp...  5.14 us
    unnamed x6, local copies, waits for them, and re-layouts  1.52 us
  transfers between devices with their start and end apart: 15, of which 11 were waited for; matrix products, arithmetic and copies ran while one was open for 0% of the time, Pallas kernels for 18%

profile of v8, /device:TPU:0, one launch (start us, length us, event | category | flops | bytes accessed | tf_op | source)
XLA Modules:
  0.0 65.7 jit_solution(2797997816465355741)
XLA Ops:
  0.0 4.0 %collective-permute-start = (bf16[2,8192]{1,0:T(2,128)(2,1)}, bf16[2,8192]{1,0:T(2,128)(2,1)S(1)}, u32[]{:S(2)}, u32[]{:S(2)}) collective-permute-start(bf16[2,8192]{1,0:T(2,128)(2,1)} %value_ref), channel_id=1, source_target_pairs={{0,8},{1,9},{2,10},{3,11},{4,12},{5,13},{6,14},{7,15},{8,0},{9,1},... | collective-permute-start | bytes 98312 | tf_op jit(solution)/shard_map/ppermute | solution.py:32
  4.0 1.5 %copy-done.2 = bf16[2,8192]{1,0:T(2,128)(2,1)S(1)} copy-done((bf16[2,8192]{1,0:T(2,128)(2,1)S(1)}, bf16[2,8192]{1,0:T(2,128)(2,1)}, u32[]{:S(2)}) %copy-start.2) | copy-done | bytes 32792
  5.6 0.9 %collective-permute-done = bf16[2,8192]{1,0:T(2,128)(2,1)S(1)} collective-permute-done((bf16[2,8192]{1,0:T(2,128)(2,1)}, bf16[2,8192]{1,0:T(2,128)(2,1)S(1)}, u32[]{:S(2)}, u32[]{:S(2)}) %collective-permute-start) | collective-permute-done | bytes 32800 | tf_op jit(solution)/shard_map/ppermute | solution.py:32
  6.5 0.1 broadcast_select_fusion.11
  6.6 0.1 pad_maximum_fusion.2.refs_0_
  6.6 1.6 %collective-permute-start.3 = (bf16[4,8192]{1,0:T(4,128)(2,1)S(1)}, bf16[4,8192]{1,0:T(4,128)(2,1)S(1)}, u32[]{:S(2)}, u32[]{:S(2)}) collective-permute-start(bf16[4,8192]{1,0:T(4,128)(2,1)S(1)} %pad_maximum_fusion.2.refs_0_), channel_id=1, source_target_pairs={{0,4},{1,5},{2,6},{3,7},{4,0},{5,1},{6,2},{7,3},{8,12},{9,13},{10,... | collective-permute-start | bytes 196616 | tf_op jit(solution)/shard_map/ppermute | solution.py:32
  8.3 1.5 %collective-permute-start.2 = (bf16[4,8192]{1,0:T(4,128)(2,1)S(1)}, bf16[4,8192]{1,0:T(4,128)(2,1)S(1)}, u32[]{:S(2)}, u32[]{:S(2)}) collective-permute-start(bf16[4,8192]{1,0:T(4,128)(2,1)S(1)} %pad_maximum_fusion.2.refs_0_), channel_id=1, source_target_pairs={{0,2},{1,3},{2,0},{3,1},{4,6},{5,7},{6,4},{7,5},{8,10},{9,11},{10,... | collective-permute-start | bytes 196616 | tf_op jit(solution)/shard_map/ppermute | solution.py:32
  9.8 0.4 collective-permute-start.1
  10.2 2.6 %shard_map.56.refs_0_ = bf16[1536,1792]{1,0:T(8,128)(2,1)S(1)} custom-call(bf16[8192,1792]{1,0:T(8,128)(2,1)} %gate_ref.1, bf16[4,8192]{1,0:T(4,128)(2,1)S(1)} %pad_maximum_fusion.2.refs_0_), custom_call_target="tpu_custom_call" | custom-call | bytes 11010048 | tf_op jit(solution)/shard_map/pallas_call | solution.py:56
  12.8 0.0 collective-permute-done.3
  12.8 0.2 collective-permute-done.2
  13.0 1.9 %collective-permute-done.1 = bf16[4,8192]{1,0:T(4,128)(2,1)S(1)} collective-permute-done((bf16[4,8192]{1,0:T(4,128)(2,1)S(1)}, bf16[4,8192]{1,0:T(4,128)(2,1)S(1)}, u32[]{:S(2)}, u32[]{:S(2)}) %collective-permute-start.1) | collective-permute-done | bytes 65568 | tf_op jit(solution)/shard_map/ppermute | solution.py:32
  14.9 0.1 broadcast_select_fusion.9
  15.1 0.2 pad_maximum_fusion.1
  15.3 0.1 collective-permute-start.4
  15.3 1.5 %collective-permute-done.4 = bf16[16,8192]{1,0:T(8,128)(2,1)S(1)} collective-permute-done((bf16[16,8192]{1,0:T(8,128)(2,1)S(1)}, bf16[16,8192]{1,0:T(8,128)(2,1)S(1)}, u32[]{:S(2)}, u32[]{:S(2)}) %collective-permute-start.4) | collective-permute-done | bytes 262176 | tf_op jit(solution)/shard_map/ppermute | solution.py:32
  16.9 0.2 broadcast_select_fusion.1
  17.1 0.0 copy-done
  17.1 10.9 %shard_map.57 = bf16[32,1792]{1,0:T(8,128)(2,1)S(1)} custom-call(bf16[32,8192]{1,0:T(8,128)(2,1)S(1)} %pad_maximum_fusion.x_ref, bf16[256,256]{1,0:T(8,128)(2,1)S(1)} %copy-done.1, bf16[8192,1792]{1,0:T(8,128)(2,1)} %gate_ref.1, bf16[8192,1792]{1,0:T(8,128)(2,1)S(1)} %copy-done, bf16[1536,1792]{1,0:T(8,128)(2,1)S(1)} %shard_map.56.refs_0_), custom_call_target="tpu_custom_call" | custom-call | flops 1879048192 | bytes 23855104 | tf_op jit(solution)/shard_map/pallas_call | solution.py:159
  28.0 0.2 collective-permute-start.5
  28.2 1.2 %collective-permute-done.5 = bf16[32,1792]{1,0:T(8,128)(2,1)S(1)} collective-permute-done((bf16[32,1792]{1,0:T(8,128)(2,1)S(1)}, bf16[32,1792]{1,0:T(8,128)(2,1)S(1)}, u32[]{:S(2)}, u32[]{:S(2)}) %collective-permute-start.5) | collective-permute-done | bytes 114720 | tf_op jit(solution)/shard_map/ppermute | solution.py:32
  29.5 0.5 collective-permute-start.8
  30.0 1.7 %collective-permute-start.7 = (bf16[32,1792]{1,0:T(8,128)(2,1)S(1)}, bf16[32,1792]{1,0:T(8,128)(2,1)S(1)}, u32[]{:S(2)}, u32[]{:S(2)}) collective-permute-start(bf16[32,1792]{1,0:T(8,128)(2,1)S(1)} %fusion.1.refs_0_), channel_id=1, source_target_pairs={{0,2},{1,3},{2,0},{3,1},{4,6},{5,7},{6,4},{7,5},{8,10},{9,11},{10,... | collective-permute-start | bytes 344072 | tf_op jit(solution)/shard_map/ppermute | solution.py:32
  31.7 1.3 %collective-permute-start.6 = (bf16[32,1792]{1,0:T(8,128)(2,1)S(1)}, bf16[32,1792]{1,0:T(8,128)(2,1)S(1)}, u32[]{:S(2)}, u32[]{:S(2)}) collective-permute-start(bf16[32,1792]{1,0:T(8,128)(2,1)S(1)} %fusion.1.refs_0_), channel_id=1, source_target_pairs={{0,4},{1,5},{2,6},{3,7},{4,0},{5,1},{6,2},{7,3},{8,12},{9,13},{10,... | collective-permute-start | bytes 344072 | tf_op jit(solution)/shard_map/ppermute | solution.py:32
  33.0 4.6 %shard_map.58.refs_0_ = bf16[768,8192]{1,0:T(8,128)(2,1)S(1)} custom-call(bf16[1792,8192]{1,0:T(8,128)(2,1)} %weight_ref.7, bf16[32,1792]{1,0:T(8,128)(2,1)S(1)} %fusion.1.refs_0_), custom_call_target="tpu_custom_call" | custom-call | bytes 25165824 | tf_op jit(solution)/shard_map/pallas_call | solution.py:56
  37.6 0.0 collective-permute-done.8
  37.7 0.1 fusion.5.refs_0_
  37.8 2.9 %collective-permute-start.9 = (bf16[32,1792]{1,0:T(8,128)(2,1)S(1)}, bf16[32,1792]{1,0:T(8,128)(2,1)S(1)}, u32[]{:S(2)}, u32[]{:S(2)}) collective-permute-start(bf16[32,1792]{1,0:T(8,128)(2,1)S(1)} %fusion.5.refs_0_), channel_id=1, source_target_pairs={{0,8},{1,9},{2,10},{3,11},{4,12},{5,13},{6,14},{7,15},{8,0},{9,1},... | collective-permute-start | bytes 344072 | tf_op jit(solution)/shard_map/ppermute | solution.py:32
  40.7 4.6 %shard_map.59.refs_1_ = bf16[768,8192]{1,0:T(8,128)(2,1)S(1)} custom-call(bf16[1792,8192]{1,0:T(8,128)(2,1)} %weight_ref.7, bf16[32,1792]{1,0:T(8,128)(2,1)S(1)} %fusion.5.refs_0_), custom_call_target="tpu_custom_call" | custom-call | bytes 25165824 | tf_op jit(solution)/shard_map/pallas_call | solution.py:56
  45.3 0.5 collective-permute-done.9
  45.8 0.1 fusion.8.rotated_ref
  45.8 5.1 %shard_map.60 = (f32[16,8192]{1,0:T(8,128)S(1)}, bf16[16,8192]{1,0:T(8,128)(2,1)S(1)}) custom-call(bf16[32,1792]{1,0:T(8,128)(2,1)S(1)} %fusion.8.rotated_ref, bf16[1792,8192]{1,0:T(8,128)(2,1)} %weight_ref.7, bf16[768,8192]{1,0:T(8,128)(2,1)S(1)} %shard_map.58.refs_0_, bf16[768,8192]{1,0:T(8,128)(2,1)S(1)} %shard_map.59.refs_1_), custom_call_target="tpu_custom_call" | custom-call | flops 939524096 | bytes 4194304 | tf_op jit(solution)/shard_map/pallas_call | solution.py:235
  51.0 0.1 collective-permute-start.10
  51.0 1.5 %collective-permute-done.10 = bf16[16,8192]{1,0:T(8,128)(2,1)S(1)} collective-permute-done((bf16[16,8192]{1,0:T(8,128)(2,1)S(1)}, bf16[16,8192]{1,0:T(8,128)(2,1)S(1)}, u32[]{:S(2)}, u32[]{:S(2)}) %collective-permute-start.10) | collective-permute-done | bytes 262176 | tf_op jit(solution)/shard_map/ppermute | solution.py:32
  52.6 0.1 convert_add_fusion
  52.6 0.1 reshape.27
  52.8 0.1 fusion.11
  52.9 0.7 %collective-permute-start.11 = (bf16[4,8192]{1,0:T(4,128)(2,1)S(1)}, bf16[4,8192]{1,0:T(4,128)(2,1)S(1)}, u32[]{:S(2)}, u32[]{:S(2)}) collective-permute-start(bf16[4,8192]{1,0:T(4,128)(2,1)S(1)} %get-tuple-element.41), channel_id=1, source_target_pairs={{0,4},{1,5},{2,6},{3,7},{4,0},{5,1},{6,2},{7,3},{8,12},{9,13},{10,... | collective-permute-start | bytes 196616 | tf_op jit(solution)/shard_map/ppermute | solution.py:32
  53.6 1.0 %collective-permute-start.12 = (bf16[4,8192]{1,0:T(4,128)(2,1)S(1)}, bf16[4,8192]{1,0:T(4,128)(2,1)S(1)}, u32[]{:S(2)}, u32[]{:S(2)}) collective-permute-start(bf16[4,8192]{1,0:T(4,128)(2,1)S(1)} %get-tuple-element.42), channel_id=1, source_target_pairs={{0,2},{1,3},{2,0},{3,1},{4,6},{5,7},{6,4},{7,5},{8,10},{9,11},{10,... | collective-permute-start | bytes 196616 | tf_op jit(solution)/shard_map/ppermute | solution.py:32
  54.6 1.9 %collective-permute-start.13 = (bf16[4,8192]{1,0:T(4,128)(2,1)S(1)}, bf16[4,8192]{1,0:T(4,128)(2,1)S(1)}, u32[]{:S(2)}, u32[]{:S(2)}) collective-permute-start(bf16[4,8192]{1,0:T(4,128)(2,1)S(1)} %get-tuple-element.43), channel_id=1, source_target_pairs={{0,6},{1,7},{2,4},{3,5},{4,2},{5,3},{6,0},{7,1},{8,14},{9,15},{10,... | collective-permute-start | bytes 196616 | tf_op jit(solution)/shard_map/ppermute | solution.py:32
  56.4 0.8 %collective-permute-done.11 = bf16[4,8192]{1,0:T(4,128)(2,1)S(1)} collective-permute-done((bf16[4,8192]{1,0:T(4,128)(2,1)S(1)}, bf16[4,8192]{1,0:T(4,128)(2,1)S(1)}, u32[]{:S(2)}, u32[]{:S(2)}) %collective-permute-start.11) | collective-permute-done | bytes 65568 | tf_op jit(solution)/shard_map/ppermute | solution.py:32
  57.2 0.6 collective-permute-done.12
  57.9 1.9 %collective-permute-done.13 = bf16[4,8192]{1,0:T(4,128)(2,1)S(1)} collective-permute-done((bf16[4,8192]{1,0:T(4,128)(2,1)S(1)}, bf16[4,8192]{1,0:T(4,128)(2,1)S(1)}, u32[]{:S(2)}, u32[]{:S(2)}) %collective-permute-start.13) | collective-permute-done | bytes 65568 | tf_op jit(solution)/shard_map/ppermute | solution.py:32
  59.7 0.1 fusion.10
  59.8 0.1 select_convert_fusion.3
  59.9 3.2 %collective-permute-start.14 = (bf16[2,8192]{1,0:T(2,128)(2,1)S(1)}, bf16[2,8192]{1,0:T(2,128)(2,1)S(1)}, u32[]{:S(2)}, u32[]{:S(2)}) collective-permute-start(bf16[2,8192]{1,0:T(2,128)(2,1)S(1)} %select_convert_fusion.3), channel_id=1, source_target_pairs={{0,8},{1,9},{2,10},{3,11},{4,12},{5,13},{6,14},{7,15},{8,0},{9,1},... | collective-permute-start | bytes 98312 | tf_op jit(solution)/shard_map/ppermute | solution.py:32
  63.1 1.9 %collective-permute-done.14 = bf16[2,8192]{1,0:T(2,128)(2,1)S(1)} collective-permute-done((bf16[2,8192]{1,0:T(2,128)(2,1)S(1)}, bf16[2,8192]{1,0:T(2,128)(2,1)S(1)}, u32[]{:S(2)}, u32[]{:S(2)}) %collective-permute-start.14) | collective-permute-done | bytes 32800 | tf_op jit(solution)/shard_map/ppermute | solution.py:32
  65.0 0.7 %add_convert_fusion = bf16[2,8192]{1,0:T(2,128)(2,1)} fusion(bf16[2,8192]{1,0:T(2,128)(2,1)S(1)} %collective-permute-done.14, pred[]{:T(512)S(6)} %eq.15, f32[4,8192]{1,0:T(4,128)S(1)} %fusion.10), kind=kLoop, calls=%fused_computation.33 | loop fusion | flops 65536 | bytes 196609 | tf_op jit(solution)/shard_map/convert_element_type | solution.py:362
  (9 shorter events, 0.1 us)
Async XLA Ops:
  0.0 17.1 %copy-start.1 = (bf16[256,256]{1,0:T(8,128)(2,1)S(1)}, bf16[256,256]{1,0:T(8,128)(2,1)}, u32[]{:S(2)}) copy-start(bf16[256,256]{1,0:T(8,128)(2,1)} %constant.6.clone.spread_ref) | copy-start | bytes 393220
  0.0 17.1 %copy-start = (bf16[8192,1792]{1,0:T(8,128)(2,1)S(1)}, bf16[8192,1792]{1,0:T(8,128)(2,1)}, u32[]{:S(2)}) copy-start(bf16[8192,1792]{1,0:T(8,128)(2,1)} %up_ref.1) | copy-start | bytes 88080384
  0.0 6.5 %collective-permute-start = (bf16[2,8192]{1,0:T(2,128)(2,1)}, bf16[2,8192]{1,0:T(2,128)(2,1)S(1)}, u32[]{:S(2)}, u32[]{:S(2)}) collective-permute-start(bf16[2,8192]{1,0:T(2,128)(2,1)} %value_ref), channel_id=1, source_target_pairs={{0,8},{1,9},{2,10},{3,11},{4,12},{5,13},{6,14},{7,15},{8,0},{9,1},... | collective-permute-start | bytes 98312 | tf_op jit(solution)/shard_map/ppermute | solution.py:32
  4.0 1.5 %copy-start.2 = (bf16[2,8192]{1,0:T(2,128)(2,1)S(1)}, bf16[2,8192]{1,0:T(2,128)(2,1)}, u32[]{:S(2)}) copy-start(bf16[2,8192]{1,0:T(2,128)(2,1)} %value_ref) | copy-start | bytes 98308
  6.6 6.1 %collective-permute-start.3 = (bf16[4,8192]{1,0:T(4,128)(2,1)S(1)}, bf16[4,8192]{1,0:T(4,128)(2,1)S(1)}, u32[]{:S(2)}, u32[]{:S(2)}) collective-permute-start(bf16[4,8192]{1,0:T(4,128)(2,1)S(1)} %pad_maximum_fusion.2.refs_0_), channel_id=1, source_target_pairs={{0,4},{1,5},{2,6},{3,7},{4,0},{5,1},{6,2},{7,3},{8,12},{9,13},{10,... | collective-permute-start | bytes 196616 | tf_op jit(solution)/shard_map/ppermute | solution.py:32
  8.3 4.8 %collective-permute-start.2 = (bf16[4,8192]{1,0:T(4,128)(2,1)S(1)}, bf16[4,8192]{1,0:T(4,128)(2,1)S(1)}, u32[]{:S(2)}, u32[]{:S(2)}) collective-permute-start(bf16[4,8192]{1,0:T(4,128)(2,1)S(1)} %pad_maximum_fusion.2.refs_0_), channel_id=1, source_target_pairs={{0,2},{1,3},{2,0},{3,1},{4,6},{5,7},{6,4},{7,5},{8,10},{9,11},{10,... | collective-permute-start | bytes 196616 | tf_op jit(solution)/shard_map/ppermute | solution.py:32
  9.8 5.2 %collective-permute-start.1 = (bf16[4,8192]{1,0:T(4,128)(2,1)S(1)}, bf16[4,8192]{1,0:T(4,128)(2,1)S(1)}, u32[]{:S(2)}, u32[]{:S(2)}) collective-permute-start(bf16[4,8192]{1,0:T(4,128)(2,1)S(1)} %pad_maximum_fusion.2.refs_0_), channel_id=1, source_target_pairs={{0,6},{1,7},{2,4},{3,5},{4,2},{5,3},{6,0},{7,1},{8,14},{9,15},{10,... | collective-permute-start | bytes 196616 | tf_op jit(solution)/shard_map/ppermute | solution.py:32
  15.3 1.6 %collective-permute-start.4 = (bf16[16,8192]{1,0:T(8,128)(2,1)S(1)}, bf16[16,8192]{1,0:T(8,128)(2,1)S(1)}, u32[]{:S(2)}, u32[]{:S(2)}) collective-permute-start(bf16[16,8192]{1,0:T(8,128)(2,1)S(1)} %pad_maximum_fusion.1), channel_id=1, source_target_pairs={{0,1},{1,0},{2,3},{3,2},{4,5},{5,4},{6,7},{7,6},{8,9},{9,8},{10,11... | collective-permute-start | bytes 786440 | tf_op jit(solution)/shard_map/ppermute | solution.py:32
  28.0 1.4 %collective-permute-start.5 = (bf16[32,1792]{1,0:T(8,128)(2,1)S(1)}, bf16[32,1792]{1,0:T(8,128)(2,1)S(1)}, u32[]{:S(2)}, u32[]{:S(2)}) collective-permute-start(bf16[32,1792]{1,0:T(8,128)(2,1)S(1)} %shard_map.57), channel_id=1, source_target_pairs={{0,1},{1,0},{2,3},{3,2},{4,5},{5,4},{6,7},{7,6},{8,9},{9,8},{10,11... | collective-permute-start | bytes 344072 | tf_op jit(solution)/shard_map/ppermute | solution.py:32
  29.5 8.1 %collective-permute-start.8 = (bf16[32,1792]{1,0:T(8,128)(2,1)S(1)}, bf16[32,1792]{1,0:T(8,128)(2,1)S(1)}, u32[]{:S(2)}, u32[]{:S(2)}) collective-permute-start(bf16[32,1792]{1,0:T(8,128)(2,1)S(1)} %fusion.1.refs_0_), channel_id=1, source_target_pairs={{0,6},{1,7},{2,4},{3,5},{4,2},{5,3},{6,0},{7,1},{8,14},{9,15},{10,... | collective-permute-start | bytes 344072 | tf_op jit(solution)/shard_map/ppermute | solution.py:32
  30.0 7.7 %collective-permute-start.7 = (bf16[32,1792]{1,0:T(8,128)(2,1)S(1)}, bf16[32,1792]{1,0:T(8,128)(2,1)S(1)}, u32[]{:S(2)}, u32[]{:S(2)}) collective-permute-start(bf16[32,1792]{1,0:T(8,128)(2,1)S(1)} %fusion.1.refs_0_), channel_id=1, source_target_pairs={{0,2},{1,3},{2,0},{3,1},{4,6},{5,7},{6,4},{7,5},{8,10},{9,11},{10,... | collective-permute-start | bytes 344072 | tf_op jit(solution)/shard_map/ppermute | solution.py:32
  31.7 6.0 %collective-permute-start.6 = (bf16[32,1792]{1,0:T(8,128)(2,1)S(1)}, bf16[32,1792]{1,0:T(8,128)(2,1)S(1)}, u32[]{:S(2)}, u32[]{:S(2)}) collective-permute-start(bf16[32,1792]{1,0:T(8,128)(2,1)S(1)} %fusion.1.refs_0_), channel_id=1, source_target_pairs={{0,4},{1,5},{2,6},{3,7},{4,0},{5,1},{6,2},{7,3},{8,12},{9,13},{10,... | collective-permute-start | bytes 344072 | tf_op jit(solution)/shard_map/ppermute | solution.py:32
  37.8 8.0 %collective-permute-start.9 = (bf16[32,1792]{1,0:T(8,128)(2,1)S(1)}, bf16[32,1792]{1,0:T(8,128)(2,1)S(1)}, u32[]{:S(2)}, u32[]{:S(2)}) collective-permute-start(bf16[32,1792]{1,0:T(8,128)(2,1)S(1)} %fusion.5.refs_0_), channel_id=1, source_target_pairs={{0,8},{1,9},{2,10},{3,11},{4,12},{5,13},{6,14},{7,15},{8,0},{9,1},... | collective-permute-start | bytes 344072 | tf_op jit(solution)/shard_map/ppermute | solution.py:32
  51.0 1.6 %collective-permute-start.10 = (bf16[16,8192]{1,0:T(8,128)(2,1)S(1)}, bf16[16,8192]{1,0:T(8,128)(2,1)S(1)}, u32[]{:S(2)}, u32[]{:S(2)}) collective-permute-start(bf16[16,8192]{1,0:T(8,128)(2,1)S(1)} %get-tuple-element.40), channel_id=1, source_target_pairs={{0,1},{1,0},{2,3},{3,2},{4,5},{5,4},{6,7},{7,6},{8,9},{9,8},{10,11... | collective-permute-start | bytes 786440 | tf_op jit(solution)/shard_map/ppermute | solution.py:32
  52.9 4.3 %collective-permute-start.11 = (bf16[4,8192]{1,0:T(4,128)(2,1)S(1)}, bf16[4,8192]{1,0:T(4,128)(2,1)S(1)}, u32[]{:S(2)}, u32[]{:S(2)}) collective-permute-start(bf16[4,8192]{1,0:T(4,128)(2,1)S(1)} %get-tuple-element.41), channel_id=1, source_target_pairs={{0,4},{1,5},{2,6},{3,7},{4,0},{5,1},{6,2},{7,3},{8,12},{9,13},{10,... | collective-permute-start | bytes 196616 | tf_op jit(solution)/shard_map/ppermute | solution.py:32
  53.6 4.3 %collective-permute-start.12 = (bf16[4,8192]{1,0:T(4,128)(2,1)S(1)}, bf16[4,8192]{1,0:T(4,128)(2,1)S(1)}, u32[]{:S(2)}, u32[]{:S(2)}) collective-permute-start(bf16[4,8192]{1,0:T(4,128)(2,1)S(1)} %get-tuple-element.42), channel_id=1, source_target_pairs={{0,2},{1,3},{2,0},{3,1},{4,6},{5,7},{6,4},{7,5},{8,10},{9,11},{10,... | collective-permute-start | bytes 196616 | tf_op jit(solution)/shard_map/ppermute | solution.py:32
  54.6 5.2 %collective-permute-start.13 = (bf16[4,8192]{1,0:T(4,128)(2,1)S(1)}, bf16[4,8192]{1,0:T(4,128)(2,1)S(1)}, u32[]{:S(2)}, u32[]{:S(2)}) collective-permute-start(bf16[4,8192]{1,0:T(4,128)(2,1)S(1)} %get-tuple-element.43), channel_id=1, source_target_pairs={{0,6},{1,7},{2,4},{3,5},{4,2},{5,3},{6,0},{7,1},{8,14},{9,15},{10,... | collective-permute-start | bytes 196616 | tf_op jit(solution)/shard_map/ppermute | solution.py:32
  59.9 5.1 %collective-permute-start.14 = (bf16[2,8192]{1,0:T(2,128)(2,1)S(1)}, bf16[2,8192]{1,0:T(2,128)(2,1)S(1)}, u32[]{:S(2)}, u32[]{:S(2)}) collective-permute-start(bf16[2,8192]{1,0:T(2,128)(2,1)S(1)} %select_convert_fusion.3), channel_id=1, source_target_pairs={{0,8},{1,9},{2,10},{3,11},{4,12},{5,13},{6,14},{7,15},{8,0},{9,1},... | collective-permute-start | bytes 98312 | tf_op jit(solution)/shard_map/ppermute | solution.py:32

commit v9 on v7

--- a/solution.py
+++ b/solution.py
@@ -14,7 +14,7 @@
 VMEM = pl.BlockSpec(memory_space=pltpu.VMEM)
 ANY = pl.BlockSpec(memory_space=pl.ANY)
 GATHER_BYTES = (0 * MIB, 6 * MIB, 0 * MIB)
-HADAMARD_BYTES = (0, 12 * MIB, 12 * MIB)
+HADAMARD_BYTES = (0, 16 * MIB, 8 * MIB)
 SLOTS = 4
 
 

time: 66 us -> 66.1 us (level)
  transfers between devices with their start and end apart: 15 -> 15, of which waited for: 10 -> 13; matrix products, arithmetic and copies ran while one was open for 0% -> 0% of each run, Pallas kernels for 18% -> 18%
where the time goes in v9:
time: 66.1 us; the launch traced here: 65.8 us
  Pallas kernels  27.8 us (42%)
  starting transfers between devices  20 us (30%)
  waiting for transfers between devices  14.4 us (22%)
  other arithmetic  1.89 us (3%)
  local copies, waits for them, and re-layouts  1.67 us (3%)
    ppermute x15, starting transfers between devices, swapped(): return lax.ppermute(value, 'tensor', pairs)  20 us
    ppermute x15, waiting for transfers between devices, swapped(): return lax.ppermute(value, 'tensor', pairs)  14.4 us
    pallas_call x3, Pallas kernels, fetch(): pl.pallas_call(kernel, out_shape=jax.ShapeDtypeStruct((rows, width), weig...  11.7 us
    pallas_call x1, Pallas kernels, gate_up(): pl.pallas_call(kernel, out_shape=jax.ShapeDtypeStruct((tokens, width), jn...  10.9 us
    pallas_call x1, Pallas kernels, down(): pl.pallas_call(kernel, out_shape=(jax.ShapeDtypeStruct((half, width), jnp...  5.15 us
    unnamed x6, local copies, waits for them, and re-layouts  1.52 us
  transfers between devices with their start and end apart: 15, of which 13 were waited for; matrix products, arithmetic and copies ran while one was open for 0% of the time, Pallas kernels for 18%

profile of v9, /device:TPU:0, one launch (start us, length us, event | category | flops | bytes accessed | tf_op | source)
XLA Modules:
  0.0 65.8 jit_solution(16165741880240835958)
XLA Ops:
  0.0 4.0 %collective-permute-start = (bf16[2,8192]{1,0:T(2,128)(2,1)}, bf16[2,8192]{1,0:T(2,128)(2,1)S(1)}, u32[]{:S(2)}, u32[]{:S(2)}) collective-permute-start(bf16[2,8192]{1,0:T(2,128)(2,1)} %value_ref), channel_id=1, source_target_pairs={{0,8},{1,9},{2,10},{3,11},{4,12},{5,13},{6,14},{7,15},{8,0},{9,1},... | collective-permute-start | bytes 98312 | tf_op jit(solution)/shard_map/ppermute | solution.py:32
  4.0 1.5 %copy-done.2 = bf16[2,8192]{1,0:T(2,128)(2,1)S(1)} copy-done((bf16[2,8192]{1,0:T(2,128)(2,1)S(1)}, bf16[2,8192]{1,0:T(2,128)(2,1)}, u32[]{:S(2)}) %copy-start.2) | copy-done | bytes 32792
  5.6 0.9 %collective-permute-done = bf16[2,8192]{1,0:T(2,128)(2,1)S(1)} collective-permute-done((bf16[2,8192]{1,0:T(2,128)(2,1)}, bf16[2,8192]{1,0:T(2,128)(2,1)S(1)}, u32[]{:S(2)}, u32[]{:S(2)}) %collective-permute-start) | collective-permute-done | bytes 32800 | tf_op jit(solution)/shard_map/ppermute | solution.py:32
  6.5 0.1 broadcast_select_fusion.11
  6.6 0.1 pad_maximum_fusion.2.refs_0_
  6.6 1.6 %collective-permute-start.3 = (bf16[4,8192]{1,0:T(4,128)(2,1)S(1)}, bf16[4,8192]{1,0:T(4,128)(2,1)S(1)}, u32[]{:S(2)}, u32[]{:S(2)}) collective-permute-start(bf16[4,8192]{1,0:T(4,128)(2,1)S(1)} %pad_maximum_fusion.2.refs_0_), channel_id=1, source_target_pairs={{0,4},{1,5},{2,6},{3,7},{4,0},{5,1},{6,2},{7,3},{8,12},{9,13},{10,... | collective-permute-start | bytes 196616 | tf_op jit(solution)/shard_map/ppermute | solution.py:32
  8.3 1.5 %collective-permute-start.2 = (bf16[4,8192]{1,0:T(4,128)(2,1)S(1)}, bf16[4,8192]{1,0:T(4,128)(2,1)S(1)}, u32[]{:S(2)}, u32[]{:S(2)}) collective-permute-start(bf16[4,8192]{1,0:T(4,128)(2,1)S(1)} %pad_maximum_fusion.2.refs_0_), channel_id=1, source_target_pairs={{0,2},{1,3},{2,0},{3,1},{4,6},{5,7},{6,4},{7,5},{8,10},{9,11},{10,... | collective-permute-start | bytes 196616 | tf_op jit(solution)/shard_map/ppermute | solution.py:32
  9.8 0.4 collective-permute-start.1
  10.2 2.6 %shard_map.56.refs_0_ = bf16[1536,1792]{1,0:T(8,128)(2,1)S(1)} custom-call(bf16[8192,1792]{1,0:T(8,128)(2,1)} %gate_ref.1, bf16[4,8192]{1,0:T(4,128)(2,1)S(1)} %pad_maximum_fusion.2.refs_0_), custom_call_target="tpu_custom_call" | custom-call | bytes 11010048 | tf_op jit(solution)/shard_map/pallas_call | solution.py:56
  12.8 0.0 collective-permute-done.3
  12.8 0.2 collective-permute-done.2
  13.0 1.9 %collective-permute-done.1 = bf16[4,8192]{1,0:T(4,128)(2,1)S(1)} collective-permute-done((bf16[4,8192]{1,0:T(4,128)(2,1)S(1)}, bf16[4,8192]{1,0:T(4,128)(2,1)S(1)}, u32[]{:S(2)}, u32[]{:S(2)}) %collective-permute-start.1) | collective-permute-done | bytes 65568 | tf_op jit(solution)/shard_map/ppermute | solution.py:32
  14.9 0.1 broadcast_select_fusion.9
  15.1 0.2 pad_maximum_fusion.1
  15.3 0.1 collective-permute-start.4
  15.3 1.5 %collective-permute-done.4 = bf16[16,8192]{1,0:T(8,128)(2,1)S(1)} collective-permute-done((bf16[16,8192]{1,0:T(8,128)(2,1)S(1)}, bf16[16,8192]{1,0:T(8,128)(2,1)S(1)}, u32[]{:S(2)}, u32[]{:S(2)}) %collective-permute-start.4) | collective-permute-done | bytes 262176 | tf_op jit(solution)/shard_map/ppermute | solution.py:32
  16.9 0.2 broadcast_select_fusion.1
  17.1 10.9 %shard_map.57 = bf16[32,1792]{1,0:T(8,128)(2,1)S(1)} custom-call(bf16[32,8192]{1,0:T(8,128)(2,1)S(1)} %pad_maximum_fusion.x_ref, bf16[256,256]{1,0:T(8,128)(2,1)S(1)} %copy-done.1, bf16[8192,1792]{1,0:T(8,128)(2,1)} %gate_ref.1, bf16[8192,1792]{1,0:T(8,128)(2,1)S(1)} %copy-done, bf16[1536,1792]{1,0:T(8,128)(2,1)S(1)} %shard_map.56.refs_0_), custom_call_target="tpu_custom_call" | custom-call | flops 1879048192 | bytes 23855104 | tf_op jit(solution)/shard_map/pallas_call | solution.py:159
  28.0 0.2 collective-permute-start.5
  28.2 1.2 %collective-permute-done.5 = bf16[32,1792]{1,0:T(8,128)(2,1)S(1)} collective-permute-done((bf16[32,1792]{1,0:T(8,128)(2,1)S(1)}, bf16[32,1792]{1,0:T(8,128)(2,1)S(1)}, u32[]{:S(2)}, u32[]{:S(2)}) %collective-permute-start.5) | collective-permute-done | bytes 114720 | tf_op jit(solution)/shard_map/ppermute | solution.py:32
  29.5 2.9 %collective-permute-start.6 = (bf16[32,1792]{1,0:T(8,128)(2,1)S(1)}, bf16[32,1792]{1,0:T(8,128)(2,1)S(1)}, u32[]{:S(2)}, u32[]{:S(2)}) collective-permute-start(bf16[32,1792]{1,0:T(8,128)(2,1)S(1)} %fusion.1.refs_0_), channel_id=1, source_target_pairs={{0,8},{1,9},{2,10},{3,11},{4,12},{5,13},{6,14},{7,15},{8,0},{9,1},... | collective-permute-start | bytes 344072 | tf_op jit(solution)/shard_map/ppermute | solution.py:32
  32.4 5.8 %shard_map.58.refs_0_ = bf16[1024,8192]{1,0:T(8,128)(2,1)S(1)} custom-call(bf16[1792,8192]{1,0:T(8,128)(2,1)} %weight_ref.7, bf16[32,1792]{1,0:T(8,128)(2,1)S(1)} %fusion.1.refs_0_), custom_call_target="tpu_custom_call" | custom-call | bytes 33554432 | tf_op jit(solution)/shard_map/pallas_call | solution.py:56
  38.2 0.1 collective-permute-done.6
  38.3 0.4 collective-permute-start.9
  38.7 1.3 %collective-permute-start.8 = (bf16[32,1792]{1,0:T(8,128)(2,1)S(1)}, bf16[32,1792]{1,0:T(8,128)(2,1)S(1)}, u32[]{:S(2)}, u32[]{:S(2)}) collective-permute-start(bf16[32,1792]{1,0:T(8,128)(2,1)S(1)} %fusion.3.refs_0_), channel_id=1, source_target_pairs={{0,2},{1,3},{2,0},{3,1},{4,6},{5,7},{6,4},{7,5},{8,10},{9,11},{10,... | collective-permute-start | bytes 344072 | tf_op jit(solution)/shard_map/ppermute | solution.py:32
  40.0 1.8 %collective-permute-start.7 = (bf16[32,1792]{1,0:T(8,128)(2,1)S(1)}, bf16[32,1792]{1,0:T(8,128)(2,1)S(1)}, u32[]{:S(2)}, u32[]{:S(2)}) collective-permute-start(bf16[32,1792]{1,0:T(8,128)(2,1)S(1)} %fusion.3.refs_0_), channel_id=1, source_target_pairs={{0,4},{1,5},{2,6},{3,7},{4,0},{5,1},{6,2},{7,3},{8,12},{9,13},{10,... | collective-permute-start | bytes 344072 | tf_op jit(solution)/shard_map/ppermute | solution.py:32
  41.8 3.4 %shard_map.59.refs_1_ = bf16[512,8192]{1,0:T(8,128)(2,1)S(1)} custom-call(bf16[1792,8192]{1,0:T(8,128)(2,1)} %weight_ref.7, bf16[32,1792]{1,0:T(8,128)(2,1)S(1)} %fusion.3.refs_0_), custom_call_target="tpu_custom_call" | custom-call | bytes 16777216 | tf_op jit(solution)/shard_map/pallas_call | solution.py:56
  45.2 0.1 collective-permute-done.9
  45.3 0.7 %collective-permute-done.8 = bf16[32,1792]{1,0:T(8,128)(2,1)S(1)} collective-permute-done((bf16[32,1792]{1,0:T(8,128)(2,1)S(1)}, bf16[32,1792]{1,0:T(8,128)(2,1)S(1)}, u32[]{:S(2)}, u32[]{:S(2)}) %collective-permute-start.8) | collective-permute-done | bytes 114720 | tf_op jit(solution)/shard_map/ppermute | solution.py:32
  46.0 0.0 collective-permute-done.7
  46.0 0.1 fusion.8.rotated_ref
  46.1 5.2 %shard_map.60 = (f32[16,8192]{1,0:T(8,128)S(1)}, bf16[16,8192]{1,0:T(8,128)(2,1)S(1)}) custom-call(bf16[32,1792]{1,0:T(8,128)(2,1)S(1)} %fusion.8.rotated_ref, bf16[1792,8192]{1,0:T(8,128)(2,1)} %weight_ref.7, bf16[1024,8192]{1,0:T(8,128)(2,1)S(1)} %shard_map.58.refs_0_, bf16[512,8192]{1,0:T(8,128)(2,1)S(1)} %shard_map.59.refs_1_), custom_call_target="tpu_custom_call" | custom-call | flops 939524096 | bytes 4194304 | tf_op jit(solution)/shard_map/pallas_call | solution.py:235
  51.3 0.1 collective-permute-start.10
  51.3 1.5 %collective-permute-done.10 = bf16[16,8192]{1,0:T(8,128)(2,1)S(1)} collective-permute-done((bf16[16,8192]{1,0:T(8,128)(2,1)S(1)}, bf16[16,8192]{1,0:T(8,128)(2,1)S(1)}, u32[]{:S(2)}, u32[]{:S(2)}) %collective-permute-start.10) | collective-permute-done | bytes 262176 | tf_op jit(solution)/shard_map/ppermute | solution.py:32
  52.9 0.1 convert_add_fusion
  52.9 0.1 reshape.27
  53.1 0.1 fusion.11
  53.2 0.9 %collective-permute-start.11 = (bf16[4,8192]{1,0:T(4,128)(2,1)S(1)}, bf16[4,8192]{1,0:T(4,128)(2,1)S(1)}, u32[]{:S(2)}, u32[]{:S(2)}) collective-permute-start(bf16[4,8192]{1,0:T(4,128)(2,1)S(1)} %get-tuple-element.41), channel_id=1, source_target_pairs={{0,4},{1,5},{2,6},{3,7},{4,0},{5,1},{6,2},{7,3},{8,12},{9,13},{10,... | collective-permute-start | bytes 196616 | tf_op jit(solution)/shard_map/ppermute | solution.py:32
  54.1 0.8 %collective-permute-start.12 = (bf16[4,8192]{1,0:T(4,128)(2,1)S(1)}, bf16[4,8192]{1,0:T(4,128)(2,1)S(1)}, u32[]{:S(2)}, u32[]{:S(2)}) collective-permute-start(bf16[4,8192]{1,0:T(4,128)(2,1)S(1)} %get-tuple-element.42), channel_id=1, source_target_pairs={{0,2},{1,3},{2,0},{3,1},{4,6},{5,7},{6,4},{7,5},{8,10},{9,11},{10,... | collective-permute-start | bytes 196616 | tf_op jit(solution)/shard_map/ppermute | solution.py:32
  54.9 1.8 %collective-permute-start.13 = (bf16[4,8192]{1,0:T(4,128)(2,1)S(1)}, bf16[4,8192]{1,0:T(4,128)(2,1)S(1)}, u32[]{:S(2)}, u32[]{:S(2)}) collective-permute-start(bf16[4,8192]{1,0:T(4,128)(2,1)S(1)} %get-tuple-element.43), channel_id=1, source_target_pairs={{0,6},{1,7},{2,4},{3,5},{4,2},{5,3},{6,0},{7,1},{8,14},{9,15},{10,... | collective-permute-start | bytes 196616 | tf_op jit(solution)/shard_map/ppermute | solution.py:32
  56.8 0.8 %collective-permute-done.11 = bf16[4,8192]{1,0:T(4,128)(2,1)S(1)} collective-permute-done((bf16[4,8192]{1,0:T(4,128)(2,1)S(1)}, bf16[4,8192]{1,0:T(4,128)(2,1)S(1)}, u32[]{:S(2)}, u32[]{:S(2)}) %collective-permute-start.11) | collective-permute-done | bytes 65568 | tf_op jit(solution)/shard_map/ppermute | solution.py:32
  57.5 1.1 %collective-permute-done.12 = bf16[4,8192]{1,0:T(4,128)(2,1)S(1)} collective-permute-done((bf16[4,8192]{1,0:T(4,128)(2,1)S(1)}, bf16[4,8192]{1,0:T(4,128)(2,1)S(1)}, u32[]{:S(2)}, u32[]{:S(2)}) %collective-permute-start.12) | collective-permute-done | bytes 65568 | tf_op jit(solution)/shard_map/ppermute | solution.py:32
  58.7 1.4 %collective-permute-done.13 = bf16[4,8192]{1,0:T(4,128)(2,1)S(1)} collective-permute-done((bf16[4,8192]{1,0:T(4,128)(2,1)S(1)}, bf16[4,8192]{1,0:T(4,128)(2,1)S(1)}, u32[]{:S(2)}, u32[]{:S(2)}) %collective-permute-start.13) | collective-permute-done | bytes 65568 | tf_op jit(solution)/shard_map/ppermute | solution.py:32
  60.1 0.1 fusion.10
  60.2 0.1 select_convert_fusion.3
  60.3 2.0 %collective-permute-start.14 = (bf16[2,8192]{1,0:T(2,128)(2,1)S(1)}, bf16[2,8192]{1,0:T(2,128)(2,1)S(1)}, u32[]{:S(2)}, u32[]{:S(2)}) collective-permute-start(bf16[2,8192]{1,0:T(2,128)(2,1)S(1)} %select_convert_fusion.3), channel_id=1, source_target_pairs={{0,8},{1,9},{2,10},{3,11},{4,12},{5,13},{6,14},{7,15},{8,0},{9,1},... | collective-permute-start | bytes 98312 | tf_op jit(solution)/shard_map/ppermute | solution.py:32
  62.3 2.9 %collective-permute-done.14 = bf16[2,8192]{1,0:T(2,128)(2,1)S(1)} collective-permute-done((bf16[2,8192]{1,0:T(2,128)(2,1)S(1)}, bf16[2,8192]{1,0:T(2,128)(2,1)S(1)}, u32[]{:S(2)}, u32[]{:S(2)}) %collective-permute-start.14) | collective-permute-done | bytes 32800 | tf_op jit(solution)/shard_map/ppermute | solution.py:32
  65.2 0.7 %add_convert_fusion = bf16[2,8192]{1,0:T(2,128)(2,1)} fusion(bf16[2,8192]{1,0:T(2,128)(2,1)S(1)} %collective-permute-done.14, pred[]{:T(512)S(6)} %eq.15, f32[4,8192]{1,0:T(4,128)S(1)} %fusion.10), kind=kLoop, calls=%fused_computation.33 | loop fusion | flops 65536 | bytes 196609 | tf_op jit(solution)/shard_map/convert_element_type | solution.py:362
  (9 shorter events, 0.1 us)
Async XLA Ops:
  0.0 17.1 %copy-start.1 = (bf16[256,256]{1,0:T(8,128)(2,1)S(1)}, bf16[256,256]{1,0:T(8,128)(2,1)}, u32[]{:S(2)}) copy-start(bf16[256,256]{1,0:T(8,128)(2,1)} %constant.6.clone.spread_ref) | copy-start | bytes 393220
  0.0 17.1 %copy-start = (bf16[8192,1792]{1,0:T(8,128)(2,1)S(1)}, bf16[8192,1792]{1,0:T(8,128)(2,1)}, u32[]{:S(2)}) copy-start(bf16[8192,1792]{1,0:T(8,128)(2,1)} %up_ref.1) | copy-start | bytes 88080384
  0.0 6.5 %collective-permute-start = (bf16[2,8192]{1,0:T(2,128)(2,1)}, bf16[2,8192]{1,0:T(2,128)(2,1)S(1)}, u32[]{:S(2)}, u32[]{:S(2)}) collective-permute-start(bf16[2,8192]{1,0:T(2,128)(2,1)} %value_ref), channel_id=1, source_target_pairs={{0,8},{1,9},{2,10},{3,11},{4,12},{5,13},{6,14},{7,15},{8,0},{9,1},... | collective-permute-start | bytes 98312 | tf_op jit(solution)/shard_map/ppermute | solution.py:32
  4.0 1.5 %copy-start.2 = (bf16[2,8192]{1,0:T(2,128)(2,1)S(1)}, bf16[2,8192]{1,0:T(2,128)(2,1)}, u32[]{:S(2)}) copy-start(bf16[2,8192]{1,0:T(2,128)(2,1)} %value_ref) | copy-start | bytes 98308
  6.6 6.1 %collective-permute-start.3 = (bf16[4,8192]{1,0:T(4,128)(2,1)S(1)}, bf16[4,8192]{1,0:T(4,128)(2,1)S(1)}, u32[]{:S(2)}, u32[]{:S(2)}) collective-permute-start(bf16[4,8192]{1,0:T(4,128)(2,1)S(1)} %pad_maximum_fusion.2.refs_0_), channel_id=1, source_target_pairs={{0,4},{1,5},{2,6},{3,7},{4,0},{5,1},{6,2},{7,3},{8,12},{9,13},{10,... | collective-permute-start | bytes 196616 | tf_op jit(solution)/shard_map/ppermute | solution.py:32
  8.3 4.8 %collective-permute-start.2 = (bf16[4,8192]{1,0:T(4,128)(2,1)S(1)}, bf16[4,8192]{1,0:T(4,128)(2,1)S(1)}, u32[]{:S(2)}, u32[]{:S(2)}) collective-permute-start(bf16[4,8192]{1,0:T(4,128)(2,1)S(1)} %pad_maximum_fusion.2.refs_0_), channel_id=1, source_target_pairs={{0,2},{1,3},{2,0},{3,1},{4,6},{5,7},{6,4},{7,5},{8,10},{9,11},{10,... | collective-permute-start | bytes 196616 | tf_op jit(solution)/shard_map/ppermute | solution.py:32
  9.8 5.2 %collective-permute-start.1 = (bf16[4,8192]{1,0:T(4,128)(2,1)S(1)}, bf16[4,8192]{1,0:T(4,128)(2,1)S(1)}, u32[]{:S(2)}, u32[]{:S(2)}) collective-permute-start(bf16[4,8192]{1,0:T(4,128)(2,1)S(1)} %pad_maximum_fusion.2.refs_0_), channel_id=1, source_target_pairs={{0,6},{1,7},{2,4},{3,5},{4,2},{5,3},{6,0},{7,1},{8,14},{9,15},{10,... | collective-permute-start | bytes 196616 | tf_op jit(solution)/shard_map/ppermute | solution.py:32
  15.3 1.6 %collective-permute-start.4 = (bf16[16,8192]{1,0:T(8,128)(2,1)S(1)}, bf16[16,8192]{1,0:T(8,128)(2,1)S(1)}, u32[]{:S(2)}, u32[]{:S(2)}) collective-permute-start(bf16[16,8192]{1,0:T(8,128)(2,1)S(1)} %pad_maximum_fusion.1), channel_id=1, source_target_pairs={{0,1},{1,0},{2,3},{3,2},{4,5},{5,4},{6,7},{7,6},{8,9},{9,8},{10,11... | collective-permute-start | bytes 786440 | tf_op jit(solution)/shard_map/ppermute | solution.py:32
  28.0 1.4 %collective-permute-start.5 = (bf16[32,1792]{1,0:T(8,128)(2,1)S(1)}, bf16[32,1792]{1,0:T(8,128)(2,1)S(1)}, u32[]{:S(2)}, u32[]{:S(2)}) collective-permute-start(bf16[32,1792]{1,0:T(8,128)(2,1)S(1)} %shard_map.57), channel_id=1, source_target_pairs={{0,1},{1,0},{2,3},{3,2},{4,5},{5,4},{6,7},{7,6},{8,9},{9,8},{10,11... | collective-permute-start | bytes 344072 | tf_op jit(solution)/shard_map/ppermute | solution.py:32
  29.5 8.7 %collective-permute-start.6 = (bf16[32,1792]{1,0:T(8,128)(2,1)S(1)}, bf16[32,1792]{1,0:T(8,128)(2,1)S(1)}, u32[]{:S(2)}, u32[]{:S(2)}) collective-permute-start(bf16[32,1792]{1,0:T(8,128)(2,1)S(1)} %fusion.1.refs_0_), channel_id=1, source_target_pairs={{0,8},{1,9},{2,10},{3,11},{4,12},{5,13},{6,14},{7,15},{8,0},{9,1},... | collective-permute-start | bytes 344072 | tf_op jit(solution)/shard_map/ppermute | solution.py:32
  38.3 7.0 %collective-permute-start.9 = (bf16[32,1792]{1,0:T(8,128)(2,1)S(1)}, bf16[32,1792]{1,0:T(8,128)(2,1)S(1)}, u32[]{:S(2)}, u32[]{:S(2)}) collective-permute-start(bf16[32,1792]{1,0:T(8,128)(2,1)S(1)} %fusion.3.refs_0_), channel_id=1, source_target_pairs={{0,6},{1,7},{2,4},{3,5},{4,2},{5,3},{6,0},{7,1},{8,14},{9,15},{10,... | collective-permute-start | bytes 344072 | tf_op jit(solution)/shard_map/ppermute | solution.py:32
  38.7 7.3 %collective-permute-start.8 = (bf16[32,1792]{1,0:T(8,128)(2,1)S(1)}, bf16[32,1792]{1,0:T(8,128)(2,1)S(1)}, u32[]{:S(2)}, u32[]{:S(2)}) collective-permute-start(bf16[32,1792]{1,0:T(8,128)(2,1)S(1)} %fusion.3.refs_0_), channel_id=1, source_target_pairs={{0,2},{1,3},{2,0},{3,1},{4,6},{5,7},{6,4},{7,5},{8,10},{9,11},{10,... | collective-permute-start | bytes 344072 | tf_op jit(solution)/shard_map/ppermute | solution.py:32
  40.0 6.0 %collective-permute-start.7 = (bf16[32,1792]{1,0:T(8,128)(2,1)S(1)}, bf16[32,1792]{1,0:T(8,128)(2,1)S(1)}, u32[]{:S(2)}, u32[]{:S(2)}) collective-permute-start(bf16[32,1792]{1,0:T(8,128)(2,1)S(1)} %fusion.3.refs_0_), channel_id=1, source_target_pairs={{0,4},{1,5},{2,6},{3,7},{4,0},{5,1},{6,2},{7,3},{8,12},{9,13},{10,... | collective-permute-start | bytes 344072 | tf_op jit(solution)/shard_map/ppermute | solution.py:32
  51.3 1.6 %collective-permute-start.10 = (bf16[16,8192]{1,0:T(8,128)(2,1)S(1)}, bf16[16,8192]{1,0:T(8,128)(2,1)S(1)}, u32[]{:S(2)}, u32[]{:S(2)}) collective-permute-start(bf16[16,8192]{1,0:T(8,128)(2,1)S(1)} %get-tuple-element.40), channel_id=1, source_target_pairs={{0,1},{1,0},{2,3},{3,2},{4,5},{5,4},{6,7},{7,6},{8,9},{9,8},{10,11... | collective-permute-start | bytes 786440 | tf_op jit(solution)/shard_map/ppermute | solution.py:32
  53.2 4.3 %collective-permute-start.11 = (bf16[4,8192]{1,0:T(4,128)(2,1)S(1)}, bf16[4,8192]{1,0:T(4,128)(2,1)S(1)}, u32[]{:S(2)}, u32[]{:S(2)}) collective-permute-start(bf16[4,8192]{1,0:T(4,128)(2,1)S(1)} %get-tuple-element.41), channel_id=1, source_target_pairs={{0,4},{1,5},{2,6},{3,7},{4,0},{5,1},{6,2},{7,3},{8,12},{9,13},{10,... | collective-permute-start | bytes 196616 | tf_op jit(solution)/shard_map/ppermute | solution.py:32
  54.1 4.6 %collective-permute-start.12 = (bf16[4,8192]{1,0:T(4,128)(2,1)S(1)}, bf16[4,8192]{1,0:T(4,128)(2,1)S(1)}, u32[]{:S(2)}, u32[]{:S(2)}) collective-permute-start(bf16[4,8192]{1,0:T(4,128)(2,1)S(1)} %get-tuple-element.42), channel_id=1, source_target_pairs={{0,2},{1,3},{2,0},{3,1},{4,6},{5,7},{6,4},{7,5},{8,10},{9,11},{10,... | collective-permute-start | bytes 196616 | tf_op jit(solution)/shard_map/ppermute | solution.py:32
  54.9 5.2 %collective-permute-start.13 = (bf16[4,8192]{1,0:T(4,128)(2,1)S(1)}, bf16[4,8192]{1,0:T(4,128)(2,1)S(1)}, u32[]{:S(2)}, u32[]{:S(2)}) collective-permute-start(bf16[4,8192]{1,0:T(4,128)(2,1)S(1)} %get-tuple-element.43), channel_id=1, source_target_pairs={{0,6},{1,7},{2,4},{3,5},{4,2},{5,3},{6,0},{7,1},{8,14},{9,15},{10,... | collective-permute-start | bytes 196616 | tf_op jit(solution)/shard_map/ppermute | solution.py:32
  60.3 4.9 %collective-permute-start.14 = (bf16[2,8192]{1,0:T(2,128)(2,1)S(1)}, bf16[2,8192]{1,0:T(2,128)(2,1)S(1)}, u32[]{:S(2)}, u32[]{:S(2)}) collective-permute-start(bf16[2,8192]{1,0:T(2,128)(2,1)S(1)} %select_convert_fusion.3), channel_id=1, source_target_pairs={{0,8},{1,9},{2,10},{3,11},{4,12},{5,13},{6,14},{7,15},{8,0},{9,1},... | collective-permute-start | bytes 98312 | tf_op jit(solution)/shard_map/ppermute | solution.py:32
